TPU v7x, 32 devices: a whole 2x2x4 slice. The times are simulated.
32 devices in a mesh: gx: 4 (over y, x), gy: 8 (over z, core).
Axes of the slice: x: 2, y: 2, z: 4, core: 2. Of those that a mesh axis runs over, the one named last changes fastest.
Arguments:
- features: bfloat16 [4, 8, 32, 8, 8, 512], P('gx', 'gy'), may hold values from -6 to 6
- occupancy: int32 [4, 8, 32, 25], P('gx', 'gy'), may hold values from 0 to 2097151, as said below
- neighbors: int32 [4, 8, 32, 27], P('gx', 'gy'), may hold values from 0 to 48, as said below
- face_lists: int32 [4, 8, 8], P('gx', 'gy'), may hold values from 0 to 31, as said below
- face_relays: int32 [4, 8, 8], P('gx', 'gy'), may hold values from 0 to 39, as said below
- send_slots: int32 [4, 8, 8, 4], P('gx', 'gy'), may hold values from -1 to 31, as said below
- receive_order: int32 [4, 8, 16], P('gx', 'gy'), may hold values from 0 to 31, as said below
- weights: bfloat16 [27, 64, 64], replicated, may hold values from -0.15625 to 0.15625
- channel_bias: float32 [64], replicated, may hold values from -3 to 3
Outputs:
- conv_out: bfloat16 [4, 8, 16, 8, 8, 512], P('gx', 'gy')
Inputs may be any that keep to these rules, and one draw needn't show every extreme that they name: `occupancy`: bit k of word w of a held block is voxel 21 * w + k; bits past voxel 8 * 8 * 8 - 1 are zero; slots that hold no block have all words zero. `neighbors`: entries name pool blocks: held slots below 32, then blocks received across faces, then the zero block 48; entry 13 is the block's own slot; other held entries name occupied slots, or any slot where the device holds none. `face_lists`: entries name slots of the device that hold blocks, or any slot where the device holds none. `face_relays`: entries below 32 name occupied held slots, or any slot where the device holds none; the others name blocks received from gy neighbours. `send_slots`: device d of a gx index sends the same number c_d of items, 0 or more, to every device of that gx index, in items q < c_d, and -1 in the others; every occupied held slot is sent exactly once; in every gx index some device has c_d = 4. `receive_order`: every device receives exactly 16 used items; its rows name each of them exactly once.
All inputs are finite; a program needn't handle non-finite values.
Results may differ from a plain program's by a relative error of at most 0.001.
Values may be sent and summed in bfloat16 or wider, within the bound.
No kernel may reach another device: no remote copies, remote signals or barrier semaphores. Data moves between devices by JAX's collectives and lax.ppermute only.
A program may use at most 128 MiB of HBM per device.

v0:
```python
import functools

import jax
import jax.numpy as jnp
from jax import lax
from jax.experimental import pallas as pl
from jax.experimental.pallas import tpu as pltpu
from jax.sharding import PartitionSpec as P

C = 64
BS = 8
ROWS = BS * BS
LANES = BS * C
WORD_BITS = 21
GROUP = 4
K_BAND = (GROUP + 2) * C
N_BAND = GROUP * C
EXT = (BS + 2) * C
VMEM_LIMIT = 48 * 1024 * 1024

ANY = pl.BlockSpec(memory_space=pl.ANY)
SMEM = pl.BlockSpec(memory_space=pltpu.SMEM)
VMEM = pl.BlockSpec(memory_space=pltpu.VMEM)


def params():
    return pltpu.CompilerParams(vmem_limit_bytes=VMEM_LIMIT)


def voxel_ids(x):
    rows = lax.broadcasted_iota(jnp.int32, (BS, LANES), 0)
    lanes = lax.broadcasted_iota(jnp.int32, (BS, LANES), 1)
    return x * ROWS + rows * BS + lanes // C


def shift_amounts(x):
    v = voxel_ids(x)
    first = (x * ROWS) // WORD_BITS
    last = (x * ROWS + ROWS - 1) // WORD_BITS
    amounts = v - first * WORD_BITS
    for k in range(first + 1, last + 1):
        amounts = jnp.where(v >= k * WORD_BITS, v - k * WORD_BITS, amounts)
    return amounts


def plane_bits(occ_ref, slot, x, shifts):
    v = voxel_ids(x)
    first = (x * ROWS) // WORD_BITS
    last = (x * ROWS + ROWS - 1) // WORD_BITS
    words = jnp.full((BS, LANES), occ_ref[slot, first], jnp.int32)
    for k in range(first + 1, last + 1):
        words = jnp.where(v >= k * WORD_BITS, occ_ref[slot, k], words)
    return lax.shift_right_logical(words, shifts) & 1


def mask_block(occ_ref, slot, shift_ref, source, target):
    for i in range(BS // 2):
        bits = jnp.concatenate(
            [
                plane_bits(occ_ref, slot, x, shift_ref[x])
                for x in (2 * i, 2 * i + 1)
            ],
            axis=0,
        )
        rows = pl.ds(2 * BS * i, 2 * BS)
        values = source[rows, :].astype(jnp.float32)
        target[rows, :] = jnp.where(bits > 0, values, 0.0).astype(jnp.bfloat16)


def outgoing_kernel(lists_ref, occ_ref, feat_ref, low_ref, high_ref, held, shift_ref, sems):
    count = held.shape[0]
    width = count // 2
    copies = [
        pltpu.make_async_copy(feat_ref.at[lists_ref[t]], held.at[t], sems.at[t]) for t in range(count)
    ]
    for copy in copies:
        copy.start()
    for x in range(BS):
        shift_ref[x] = shift_amounts(x)
    for copy in copies:
        copy.wait()

    def body(t, carry):
        mask_block(occ_ref, lists_ref[t], shift_ref, held.at[t], low_ref.at[t])
        mask_block(occ_ref, lists_ref[t + width], shift_ref, held.at[t + width], high_ref.at[t])
        return carry

    lax.fori_loop(0, width, body, 0)


def masked_outgoing(face_lists, occupancy, features):
    count = face_lists.shape[0]
    half = jax.ShapeDtypeStruct((count // 2, ROWS, LANES), jnp.bfloat16)
    return pl.pallas_call(
        outgoing_kernel,
        out_shape=(half, half),
        in_specs=[SMEM, SMEM, ANY],
        out_specs=(VMEM, VMEM),
        scratch_shapes=[
            pltpu.VMEM((count, ROWS, LANES), jnp.bfloat16),
            pltpu.VMEM((BS, BS, LANES), jnp.int32),
            pltpu.SemaphoreType.DMA((count,)),
        ],
        compiler_params=params(),
        cost_estimate=pl.CostEstimate(flops=2000000, bytes_accessed=2 * count * ROWS * LANES * 2, transcendentals=0),
        name="mask_outgoing",
    )(face_lists, occupancy, features)


def mask_all_kernel(occ_ref, feat_ref, out_ref, shift_ref):
    per_step = feat_ref.shape[0]
    step = pl.program_id(0)

    @pl.when(step == 0)
    def _():
        for x in range(BS):
            shift_ref[x] = shift_amounts(x)

    def body(t, carry):
        mask_block(occ_ref, step * per_step + t, shift_ref, feat_ref.at[t], out_ref.at[t])
        return carry

    lax.fori_loop(0, per_step, body, 0)


def masked_all(occupancy, features):
    slots = features.shape[0]
    per_step = 8
    spec = pl.BlockSpec((per_step, ROWS, LANES), lambda i: (i, 0, 0))
    return pl.pallas_call(
        mask_all_kernel,
        grid=(slots // per_step,),
        out_shape=jax.ShapeDtypeStruct(features.shape, jnp.bfloat16),
        in_specs=[SMEM, spec],
        out_specs=spec,
        scratch_shapes=[pltpu.VMEM((BS, BS, LANES), jnp.int32)],
        compiler_params=params(),
        cost_estimate=pl.CostEstimate(flops=8000000, bytes_accessed=2 * slots * ROWS * LANES * 2, transcendentals=0),
        name="mask_held",
    )(occupancy, features)


def bands_kernel(weights_ref, out_ref):
    zeros = jnp.zeros((C, C), jnp.float32)
    for pair in range(9):
        taps = [weights_ref[3 * pair + c].astype(jnp.float32) for c in range(3)]
        for z_in in range(GROUP + 2):
            row = [taps[z_in - z_out] if 0 <= z_in - z_out <= 2 else zeros for z_out in range(GROUP)]
            out_ref[pair, pl.ds(z_in * C, C), :] = jnp.concatenate(row, axis=1).astype(jnp.bfloat16)


def banded(weights):
    return pl.pallas_call(
        bands_kernel,
        out_shape=jax.ShapeDtypeStruct((9, K_BAND, N_BAND), jnp.bfloat16),
        in_specs=[VMEM],
        out_specs=VMEM,
        compiler_params=params(),
        cost_estimate=pl.CostEstimate(flops=100000, bytes_accessed=4000000, transcendentals=0),
        name="band_weights",
    )(weights)


def relay_kernel(relays_ref, held_ref, low_ref, high_ref, out_low, out_high, sems):
    held = held_ref.shape[0]
    width = low_ref.shape[0]
    targets = [out_low.at[t] for t in range(width)] + [out_high.at[t] for t in range(width)]
    for t, target in enumerate(targets):
        index = relays_ref[t]

        @pl.when(index < held)
        def _():
            pltpu.make_async_copy(held_ref.at[index], target, sems.at[t]).start()

        @pl.when((index >= held) & (index < held + width))
        def _():
            pltpu.make_async_copy(low_ref.at[index - held], target, sems.at[t]).start()

        @pl.when(index >= held + width)
        def _():
            pltpu.make_async_copy(high_ref.at[index - held - width], target, sems.at[t]).start()

    for t, target in enumerate(targets):
        pltpu.make_async_copy(held_ref.at[0], target, sems.at[t]).wait()


def relayed(face_relays, held, low, high):
    half = jax.ShapeDtypeStruct(low.shape, jnp.bfloat16)
    count = face_relays.shape[0]
    return pl.pallas_call(
        relay_kernel,
        out_shape=(half, half),
        in_specs=[SMEM, ANY, ANY, ANY],
        out_specs=(ANY, ANY),
        scratch_shapes=[pltpu.SemaphoreType.DMA((count,))],
        compiler_params=params(),
        cost_estimate=pl.CostEstimate(flops=0, bytes_accessed=2 * count * ROWS * LANES * 2, transcendentals=0),
        name="gather_relays",
    )(face_relays, held, low, high)


def extended_plane(blocks, lane_low):
    below, own, above = blocks
    columns = [below] + [own[:, 128 * i : 128 * i + 128] for i in range(4)] + [above]
    turned = [pltpu.roll(column, C, 1) for column in columns]
    return [jnp.where(lane_low, turned[i], turned[i + 1]) for i in range(5)]


def conv_kernel(
    me_ref,
    slots_ref,
    occ_ref,
    neighbors_ref,
    bias_ref,
    bands_ref,
    held_ref,
    y_low_ref,
    y_high_ref,
    x_low_ref,
    x_high_ref,
    out_ref,
    pool,
    tiles,
    shift_ref,
    sems,
    *,
    distance,
):
    items = out_ref.shape[0]
    pairs = (items + 1) // 2
    held = held_ref.shape[0]
    width = y_low_ref.shape[0]
    parts = [held_ref, y_low_ref, y_high_ref, x_low_ref, x_high_ref]
    starts = [0, held, held + width, held + 2 * width, held + 3 * width]
    copies = [
        pltpu.make_async_copy(part, pool.at[pl.ds(start, part.shape[0])], sems.at[i])
        for i, (part, start) in enumerate(zip(parts, starts))
    ]
    for copy in copies:
        copy.start()
    pool[held + 4 * width] = jnp.zeros((ROWS, LANES), jnp.bfloat16)
    for x in range(BS):
        shift_ref[x] = shift_amounts(x)
    partner = me_ref[0] ^ distance
    for copy in copies:
        copy.wait()

    row_ids = lax.broadcasted_iota(jnp.int32, (BS, 128), 0)
    lane_low = lax.broadcasted_iota(jnp.int32, (2 * BS, 128), 1) < C
    is_last = row_ids == BS - 1
    is_first = row_ids == 0

    def slot_of(item):
        return jnp.maximum(slots_ref[partner, jnp.minimum(item, items - 1)], 0)

    def row_pair(slot, depth_x, depth_y, i):
        first = 9 * depth_x + 3 * depth_y
        rows = pl.ds(2 * BS * i, 2 * BS)
        below = pool[neighbors_ref[slot, first], rows, pl.ds(LANES - 128, 128)]
        own = pool[neighbors_ref[slot, first + 1], rows, :]
        above = pool[neighbors_ref[slot, first + 2], rows, pl.ds(0, 128)]
        return extended_plane([v.astype(jnp.float32) for v in (below, own, above)], lane_low)

    def build(pair, carry):
        slots = [slot_of(2 * pair), slot_of(2 * pair + 1)]
        for depth_x, i in ((0, 3), (1, 0), (1, 1), (1, 2), (1, 3), (2, 0)):
            rows = [[row_pair(slot, depth_x, depth_y, i) for depth_y in range(3)] for slot in slots]
            if depth_x == 0:
                planes = ((1, 0),)
            elif depth_x == 2:
                planes = ((0, BS + 1),)
            else:
                planes = ((0, 2 * i + 1), (1, 2 * i + 2))
            for half, plane in planes:
                cut = slice(half * BS, half * BS + BS)
                for column in range(5):
                    lanes = pl.ds(128 * column, 128)
                    shifted = ([], [], [])
                    for k in range(2):
                        before, own, after = (rows[k][depth_y][column][cut] for depth_y in range(3))
                        shifted[0].append(pltpu.roll(jnp.where(is_last, before, own), 1, 0))
                        shifted[1].append(own)
                        shifted[2].append(pltpu.roll(jnp.where(is_first, after, own), BS - 1, 0))
                    for depth_y in range(3):
                        tiles[depth_y, plane, pair, :, lanes] = jnp.concatenate(shifted[depth_y], axis=0).astype(
                            jnp.bfloat16
                        )
        return carry

    lax.fori_loop(0, pairs, build, 0)

    bias = bias_ref[...]
    for group in range(BS // GROUP):
        window = pl.ds(group * N_BAND, K_BAND)
        total = None
        for depth_x in range(3):
            for depth_y in range(3):
                left = tiles[depth_y, pl.ds(depth_x, BS), :, :, window].reshape(BS * pairs * 2 * BS, K_BAND)
                term = jnp.dot(left, bands_ref[3 * depth_x + depth_y], preferred_element_type=jnp.float32)
                total = term if total is None else total + term
        total = (total + bias).reshape(BS, pairs * 2, BS, N_BAND)
        for item in range(items):
            slot = slot_of(item)
            for i in range(BS // 2):
                parts = []
                for x in (2 * i, 2 * i + 1):
                    bits = plane_bits(occ_ref, slot, x, shift_ref[x])[:, group * N_BAND : group * N_BAND + N_BAND]
                    parts.append(jnp.where(bits > 0, total[x, item], 0.0))
                out_ref[item, pl.ds(2 * BS * i, 2 * BS), pl.ds(group * N_BAND, N_BAND)] = jnp.concatenate(
                    parts, axis=0
                ).astype(jnp.bfloat16)


def convolved(distance, me, send_slots, occupancy, neighbors, bias, bands, parts):
    items = send_slots.shape[1]
    pairs = (items + 1) // 2
    held = parts[0].shape[0]
    pool_blocks = sum(part.shape[0] for part in parts) + 1
    return pl.pallas_call(
        functools.partial(conv_kernel, distance=distance),
        out_shape=jax.ShapeDtypeStruct((items, ROWS, LANES), jnp.bfloat16),
        in_specs=[SMEM, SMEM, SMEM, SMEM, VMEM, VMEM] + [ANY] * 5,
        out_specs=VMEM,
        scratch_shapes=[
            pltpu.VMEM((pool_blocks, ROWS, LANES), jnp.bfloat16),
            pltpu.VMEM((3, BS + 2, pairs, 2 * BS, EXT), jnp.bfloat16),
            pltpu.VMEM((BS, BS, LANES), jnp.int32),
            pltpu.SemaphoreType.DMA((5,)),
        ],
        compiler_params=params(),
        cost_estimate=pl.CostEstimate(
            flops=2 * 9 * 2 * items * ROWS * K_BAND * N_BAND,
            bytes_accessed=(pool_blocks + items) * ROWS * LANES * 2 + 9 * K_BAND * N_BAND * 2,
            transcendentals=0,
        ),
        name="convolve_%d" % distance,
    )(me, send_slots, occupancy, neighbors, bias, bands, *parts)


def place_kernel(me_ref, order_ref, *refs):
    sems = refs[-1]
    out_ref = refs[-2]
    sources = refs[:-2]
    items = sources[0].shape[0]

    def body(r, carry):
        name = order_ref[r]
        distance = me_ref[0] ^ (name // items)
        for m, source in enumerate(sources):

            @pl.when(distance == m)
            def _():
                pltpu.make_async_copy(source.at[name % items], out_ref.at[r], sems.at[r]).start()

        return carry

    lax.fori_loop(0, out_ref.shape[0], body, 0)
    for r in range(out_ref.shape[0]):
        pltpu.make_async_copy(sources[0].at[0], out_ref.at[r], sems.at[r]).wait()


def placed(me, receive_order, arrived):
    count = receive_order.shape[0]
    return pl.pallas_call(
        place_kernel,
        out_shape=jax.ShapeDtypeStruct((count, ROWS, LANES), jnp.bfloat16),
        in_specs=[SMEM, SMEM] + [ANY] * len(arrived),
        out_specs=ANY,
        scratch_shapes=[pltpu.SemaphoreType.DMA((count,))],
        compiler_params=params(),
        cost_estimate=pl.CostEstimate(flops=0, bytes_accessed=2 * count * ROWS * LANES * 2, transcendentals=0),
        name="place_rows",
    )(me, receive_order, *arrived)


def both_ways(low, high, axis):
    ends = lax.axis_size(axis) - 1
    from_low = lax.ppermute(high, axis, [(i, i + 1) for i in range(ends)])
    from_high = lax.ppermute(low, axis, [(i + 1, i) for i in range(ends)])
    return from_low, from_high


def on_device(
    features,
    occupancy,
    neighbors,
    face_lists,
    face_relays,
    send_slots,
    receive_order,
    weights,
    channel_bias,
):
    slots = features.shape[2]
    blocks = features.reshape(slots, ROWS, LANES)
    words = occupancy[0, 0]
    me = lax.axis_index("gy").astype(jnp.int32).reshape(1)
    peers = lax.axis_size("gy")

    out_low, out_high = masked_outgoing(face_lists[0, 0], words, blocks)
    y_low, y_high = both_ways(out_low, out_high, "gy")
    held = masked_all(words, blocks)
    bands = banded(weights)
    bias = jnp.tile(channel_bias, GROUP).reshape(1, N_BAND)
    relay_low, relay_high = relayed(face_relays[0, 0], held, y_low, y_high)
    x_low, x_high = both_ways(relay_low, relay_high, "gx")

    parts = (held, y_low, y_high, x_low, x_high)
    arrived = [None] * peers
    far_first = [m for m in range(peers) if m >= peers // 2] + [m for m in reversed(range(peers // 2))]
    for m in far_first:
        result = convolved(m, me, send_slots[0, 0], words, neighbors[0, 0], bias, bands, parts)
        arrived[m] = lax.ppermute(result, "gy", [(d, d ^ m) for d in range(peers)]) if m else result
    output = placed(me, receive_order[0, 0], arrived)
    return output.reshape(1, 1, output.shape[0], BS, BS, LANES)


def solution(mesh):
    in_specs = (
        P("gx", "gy", None, None, None, None),
        P("gx", "gy", None, None),
        P("gx", "gy", None, None),
        P("gx", "gy", None),
        P("gx", "gy", None),
        P("gx", "gy", None, None),
        P("gx", "gy", None),
        P(),
        P(),
    )
    out_specs = P("gx", "gy", None, None, None, None)
    return jax.shard_map(
        on_device, mesh=mesh, in_specs=in_specs, out_specs=out_specs, check_vma=False
    )
```

profile of v0, /device:TPU:9, one launch (start us, length us, event | category | flops | bytes accessed | tf_op | source)
XLA Modules:
  0.0 101.0 jit_solution(15256068265002347655)
XLA Ops:
  0.0 0.8 copy.10
  0.8 1.6 %copy-done.2 = bf16[1,1,32,8,8,512]{5,4,3,2,1,0:T(8,128)(2,1)S(1)} copy-done((bf16[1,1,32,8,8,512]{5,4,3,2,1,0:T(8,128)(2,1)S(1)}, bf16[1,1,32,8,8,512]{5,4,3,2,1,0:T(8,128)(2,1)}, u32[]{:S(2)}) %copy-start.2) | copy-done | bytes 2097176
  2.4 0.7 copy-done.4
  3.0 2.0 %mask_outgoing.1 = (bf16[4,64,512]{2,1,0:T(8,128)(2,1)S(1)}, bf16[4,64,512]{2,1,0:T(8,128)(2,1)S(1)}) custom-call(s32[8]{0:T(128)S(1)} %bitcast.29, s32[32,25]{1,0:T(8,128)S(1)} %bitcast.11, bf16[32,64,512]{2,1,0:T(8,128)(2,1)S(1)} %bitcast.9), custom_call_target="tpu_custom_call" | custom-call | flops 2000000 | bytes 1048576 | tf_op jit(solution)/shard_map/mask_outgoing/pallas_call | solution.py:94
  5.1 3.8 %collective-permute-start = (bf16[4,64,512]{2,1,0:T(8,128)(2,1)S(1)}, bf16[4,64,512]{2,1,0:T(8,128)(2,1)S(1)}, u32[]{:S(2)}, u32[]{:S(2)}) collective-permute-start(bf16[4,64,512]{2,1,0:T(8,128)(2,1)S(1)} %get-tuple-element.9), channel_id=1, source_target_pairs={{0,1},{1,2},{2,3},{3,4},{4,5},{5,6},{6,7},{8,9},{9,10},{10,11},{11... | collective-permute-start | bytes 786440 | tf_op jit(solution)/shard_map/ppermute | solution.py:378
  8.9 0.0 copy-start.6
  8.9 1.9 %collective-permute-start.1 = (bf16[4,64,512]{2,1,0:T(8,128)(2,1)S(1)}, bf16[4,64,512]{2,1,0:T(8,128)(2,1)S(1)}, u32[]{:S(2)}, u32[]{:S(2)}) collective-permute-start(bf16[4,64,512]{2,1,0:T(8,128)(2,1)S(1)} %get-tuple-element.10), channel_id=1, source_target_pairs={{1,0},{2,1},{3,2},{4,3},{5,4},{6,5},{7,6},{9,8},{10,9},{11,10},{12... | collective-permute-start | bytes 786440 | tf_op jit(solution)/shard_map/ppermute | solution.py:379
  10.8 3.0 %mask_held.1.held_ref = bf16[32,64,512]{2,1,0:T(8,128)(2,1)S(1)} custom-call(s32[32,25]{1,0:T(8,128)S(1)} %bitcast.12, bf16[32,64,512]{2,1,0:T(8,128)(2,1)S(1)} %bitcast.10), custom_call_target="tpu_custom_call" | custom-call | flops 8000000 | bytes 4194304 | tf_op jit(solution)/shard_map/mask_held/pallas_call | solution.py:130
  13.8 0.0 copy-start.3
  13.8 0.0 collective-permute-done.low_ref.y_low_ref
  13.8 2.7 %collective-permute-done.1.high_ref.y_high_ref = bf16[4,64,512]{2,1,0:T(8,128)(2,1)S(1)} collective-permute-done((bf16[4,64,512]{2,1,0:T(8,128)(2,1)S(1)}, bf16[4,64,512]{2,1,0:T(8,128)(2,1)S(1)}, u32[]{:S(2)}, u32[]{:S(2)}) %collective-permute-start.1) | collective-permute-done | bytes 262176 | tf_op jit(solution)/shard_map/ppermute | solution.py:379
  16.6 1.7 %gather_relays.1 = (bf16[4,64,512]{2,1,0:T(8,128)(2,1)S(1)}, bf16[4,64,512]{2,1,0:T(8,128)(2,1)}) custom-call(s32[8]{0:T(128)S(1)} %bitcast.31, bf16[32,64,512]{2,1,0:T(8,128)(2,1)S(1)} %mask_held.1.held_ref, bf16[4,64,512]{2,1,0:T(8,128)(2,1)S(1)} %collective-permute-done.low_ref.y_low_ref, bf16[4,64,512]{2,1,0:T(8,128)(2,1)S(1)} %collective-permute-done.1.high_ref.y_high_ref), custom_call_target="tpu_custom_call" | custom-call | bytes 1048576 | tf_op jit(solution)/shard_map/gather_relays/pallas_call | solution.py:190
  18.3 3.1 %collective-permute-start.2 = (bf16[4,64,512]{2,1,0:T(8,128)(2,1)}, bf16[4,64,512]{2,1,0:T(8,128)(2,1)S(1)}, u32[]{:S(2)}, u32[]{:S(2)}) collective-permute-start(bf16[4,64,512]{2,1,0:T(8,128)(2,1)} %get-tuple-element.11), channel_id=1, source_target_pairs={{0,8},{8,16},{16,24},{1,9},{9,17},{17,25},{2,10},{10,18},{18,26},{... | collective-permute-start | bytes 786440 | tf_op jit(solution)/shard_map/ppermute | solution.py:378
  21.4 1.3 %collective-permute-start.3 = (bf16[4,64,512]{2,1,0:T(8,128)(2,1)S(1)}, bf16[4,64,512]{2,1,0:T(8,128)(2,1)S(1)}, u32[]{:S(2)}, u32[]{:S(2)}) collective-permute-start(bf16[4,64,512]{2,1,0:T(8,128)(2,1)S(1)} %get-tuple-element.12), channel_id=1, source_target_pairs={{8,0},{16,8},{24,16},{9,1},{17,9},{25,17},{10,2},{18,10},{26,18},{... | collective-permute-start | bytes 786440 | tf_op jit(solution)/shard_map/ppermute | solution.py:379
  22.8 0.2 band_weights.1.bands_ref
  23.0 1.2 %copy-done = bf16[9,384,256]{2,1,0:T(8,128)(2,1)} copy-done((bf16[9,384,256]{2,1,0:T(8,128)(2,1)}, bf16[9,384,256]{2,1,0:T(8,128)(2,1)S(1)}, u32[]{:S(2)}) %copy-start) | copy-done | bytes 1769496
  24.2 0.0 copy-done.9
  24.2 0.1 reshape_tile.3.bias_ref
  24.3 0.1 copy.12.slots_ref
  24.4 0.0 copy-done.7
  24.4 0.1 copy.11
  24.5 2.5 %collective-permute-done.2.x_low_ref = bf16[4,64,512]{2,1,0:T(8,128)(2,1)S(1)} collective-permute-done((bf16[4,64,512]{2,1,0:T(8,128)(2,1)}, bf16[4,64,512]{2,1,0:T(8,128)(2,1)S(1)}, u32[]{:S(2)}, u32[]{:S(2)}) %collective-permute-start.2) | collective-permute-done | bytes 262176 | tf_op jit(solution)/shard_map/ppermute | solution.py:378
  27.0 7.2 %collective-permute-done.3.x_high_ref = bf16[4,64,512]{2,1,0:T(8,128)(2,1)S(1)} collective-permute-done((bf16[4,64,512]{2,1,0:T(8,128)(2,1)S(1)}, bf16[4,64,512]{2,1,0:T(8,128)(2,1)S(1)}, u32[]{:S(2)}, u32[]{:S(2)}) %collective-permute-start.3) | collective-permute-done | bytes 262176 | tf_op jit(solution)/shard_map/ppermute | solution.py:379
  34.1 1.5 %copy-done.1 = bf16[9,384,256]{2,1,0:T(8,128)(2,1)S(1)} copy-done((bf16[9,384,256]{2,1,0:T(8,128)(2,1)S(1)}, bf16[9,384,256]{2,1,0:T(8,128)(2,1)}, u32[]{:S(2)}) %copy-start.1) | copy-done | bytes 1769496
  35.6 3.5 %convolve_1.1 = bf16[4,64,512]{2,1,0:T(8,128)(2,1)S(1)} custom-call(s32[1]{0:T(128)} %bitcast.me_ref, s32[8,4]{1,0:T(8,128)S(1)} %copy.12.slots_ref, s32[32,25]{1,0:T(8,128)S(1)} %bitcast.13, s32[32,27]{1,0:T(8,128)S(1)} %bitcast.21, f32[1,256]{1,0:T(1,128)S(1)} %reshape_tile.3.bias_ref, bf16[9,384,256]{2,1,0:T(8,128)(2,1)S(1)} %copy-done.1, ...), custom_call_target="tpu_custom_call" | custom-call | flops 905969664 | bytes 5242880 | tf_op jit(solution)/shard_map/convolve_1/pallas_call | solution.py:319
  39.1 0.1 collective-permute-start.4
  39.2 3.5 %convolve_2.1 = bf16[4,64,512]{2,1,0:T(8,128)(2,1)S(1)} custom-call(s32[1]{0:T(128)} %bitcast.me_ref, s32[8,4]{1,0:T(8,128)S(1)} %copy.12.slots_ref, s32[32,25]{1,0:T(8,128)S(1)} %bitcast.14, s32[32,27]{1,0:T(8,128)S(1)} %bitcast.22, f32[1,256]{1,0:T(1,128)S(1)} %reshape_tile.3.bias_ref, bf16[9,384,256]{2,1,0:T(8,128)(2,1)S(1)} %copy-done.1, ...), custom_call_target="tpu_custom_call" | custom-call | flops 905969664 | bytes 5242880 | tf_op jit(solution)/shard_map/convolve_2/pallas_call | solution.py:319
  42.7 0.1 collective-permute-start.5
  42.8 3.5 %convolve_3.1 = bf16[4,64,512]{2,1,0:T(8,128)(2,1)S(1)} custom-call(s32[1]{0:T(128)} %bitcast.me_ref, s32[8,4]{1,0:T(8,128)S(1)} %copy.12.slots_ref, s32[32,25]{1,0:T(8,128)S(1)} %bitcast.15, s32[32,27]{1,0:T(8,128)S(1)} %bitcast.23, f32[1,256]{1,0:T(1,128)S(1)} %reshape_tile.3.bias_ref, bf16[9,384,256]{2,1,0:T(8,128)(2,1)S(1)} %copy-done.1, ...), custom_call_target="tpu_custom_call" | custom-call | flops 905969664 | bytes 5242880 | tf_op jit(solution)/shard_map/convolve_3/pallas_call | solution.py:319
  46.3 2.2 %collective-permute-start.6 = (bf16[4,64,512]{2,1,0:T(8,128)(2,1)S(1)}, bf16[4,64,512]{2,1,0:T(8,128)(2,1)S(1)}, u32[]{:S(2)}, u32[]{:S(2)}) collective-permute-start(bf16[4,64,512]{2,1,0:T(8,128)(2,1)S(1)} %convolve_3.1), channel_id=1, source_target_pairs={{0,3},{1,2},{2,1},{3,0},{4,7},{5,6},{6,5},{7,4},{8,11},{9,10},{10,... | collective-permute-start | bytes 786440 | tf_op jit(solution)/shard_map/ppermute | solution.py:413
  48.5 3.5 %convolve_4.1 = bf16[4,64,512]{2,1,0:T(8,128)(2,1)S(1)} custom-call(s32[1]{0:T(128)} %bitcast.me_ref, s32[8,4]{1,0:T(8,128)S(1)} %copy.12.slots_ref, s32[32,25]{1,0:T(8,128)S(1)} %bitcast.16, s32[32,27]{1,0:T(8,128)S(1)} %bitcast.24, f32[1,256]{1,0:T(1,128)S(1)} %reshape_tile.3.bias_ref, bf16[9,384,256]{2,1,0:T(8,128)(2,1)S(1)} %copy-done.1, ...), custom_call_target="tpu_custom_call" | custom-call | flops 905969664 | bytes 5242880 | tf_op jit(solution)/shard_map/convolve_4/pallas_call | solution.py:319
  52.0 0.8 collective-permute-start.7
  52.8 3.5 %convolve_5.1 = bf16[4,64,512]{2,1,0:T(8,128)(2,1)S(1)} custom-call(s32[1]{0:T(128)} %bitcast.me_ref, s32[8,4]{1,0:T(8,128)S(1)} %copy.12.slots_ref, s32[32,25]{1,0:T(8,128)S(1)} %bitcast.17, s32[32,27]{1,0:T(8,128)S(1)} %bitcast.25, f32[1,256]{1,0:T(1,128)S(1)} %reshape_tile.3.bias_ref, bf16[9,384,256]{2,1,0:T(8,128)(2,1)S(1)} %copy-done.1, ...), custom_call_target="tpu_custom_call" | custom-call | flops 905969664 | bytes 5242880 | tf_op jit(solution)/shard_map/convolve_5/pallas_call | solution.py:319
  56.3 1.6 %collective-permute-start.8 = (bf16[4,64,512]{2,1,0:T(8,128)(2,1)S(1)}, bf16[4,64,512]{2,1,0:T(8,128)(2,1)S(1)}, u32[]{:S(2)}, u32[]{:S(2)}) collective-permute-start(bf16[4,64,512]{2,1,0:T(8,128)(2,1)S(1)} %convolve_5.1), channel_id=1, source_target_pairs={{0,5},{1,4},{2,7},{3,6},{4,1},{5,0},{6,3},{7,2},{8,13},{9,12},{10,... | collective-permute-start | bytes 786440 | tf_op jit(solution)/shard_map/ppermute | solution.py:413
  57.9 3.5 %convolve_7.1 = bf16[4,64,512]{2,1,0:T(8,128)(2,1)S(1)} custom-call(s32[1]{0:T(128)} %bitcast.me_ref, s32[8,4]{1,0:T(8,128)S(1)} %copy.12.slots_ref, s32[32,25]{1,0:T(8,128)S(1)} %bitcast.18, s32[32,27]{1,0:T(8,128)S(1)} %bitcast.26, f32[1,256]{1,0:T(1,128)S(1)} %reshape_tile.3.bias_ref, bf16[9,384,256]{2,1,0:T(8,128)(2,1)S(1)} %copy-done.1, ...), custom_call_target="tpu_custom_call" | custom-call | flops 905969664 | bytes 5242880 | tf_op jit(solution)/shard_map/convolve_7/pallas_call | solution.py:319
  61.4 3.5 %convolve_6.1 = bf16[4,64,512]{2,1,0:T(8,128)(2,1)S(1)} custom-call(s32[1]{0:T(128)} %bitcast.me_ref, s32[8,4]{1,0:T(8,128)S(1)} %copy.12.slots_ref, s32[32,25]{1,0:T(8,128)S(1)} %bitcast.19, s32[32,27]{1,0:T(8,128)S(1)} %bitcast.27, f32[1,256]{1,0:T(1,128)S(1)} %reshape_tile.3.bias_ref, bf16[9,384,256]{2,1,0:T(8,128)(2,1)S(1)} %copy-done.1, ...), custom_call_target="tpu_custom_call" | custom-call | flops 905969664 | bytes 5242880 | tf_op jit(solution)/shard_map/convolve_6/pallas_call | solution.py:319
  64.9 0.0 copy-start.5
  64.9 0.0 collective-permute-done.4.refs_1_
  64.9 1.4 %collective-permute-start.9 = (bf16[4,64,512]{2,1,0:T(8,128)(2,1)S(1)}, bf16[4,64,512]{2,1,0:T(8,128)(2,1)S(1)}, u32[]{:S(2)}, u32[]{:S(2)}) collective-permute-start(bf16[4,64,512]{2,1,0:T(8,128)(2,1)S(1)} %convolve_6.1), channel_id=1, source_target_pairs={{0,6},{1,7},{2,4},{3,5},{4,2},{5,3},{6,0},{7,1},{8,14},{9,15},{10,... | collective-permute-start | bytes 786440 | tf_op jit(solution)/shard_map/ppermute | solution.py:413
  66.3 0.0 collective-permute-done.5.refs_2_
  66.3 0.8 collective-permute-start.10
  67.1 3.5 %convolve_0.1.refs_0_ = bf16[4,64,512]{2,1,0:T(8,128)(2,1)S(1)} custom-call(s32[1]{0:T(128)} %bitcast.me_ref, s32[8,4]{1,0:T(8,128)S(1)} %copy.12.slots_ref, s32[32,25]{1,0:T(8,128)S(1)} %bitcast.20, s32[32,27]{1,0:T(8,128)S(1)} %bitcast.28, f32[1,256]{1,0:T(1,128)S(1)} %reshape_tile.3.bias_ref, bf16[9,384,256]{2,1,0:T(8,128)(2,1)S(1)} %copy-done.1, ...), custom_call_target="tpu_custom_call" | custom-call | flops 905969664 | bytes 5242880 | tf_op jit(solution)/shard_map/convolve_0/pallas_call | solution.py:319
  70.6 0.0 collective-permute-done.6.refs_3_
  70.6 10.0 %collective-permute-done.7.refs_4_ = bf16[4,64,512]{2,1,0:T(8,128)(2,1)S(1)} collective-permute-done((bf16[4,64,512]{2,1,0:T(8,128)(2,1)S(1)}, bf16[4,64,512]{2,1,0:T(8,128)(2,1)S(1)}, u32[]{:S(2)}, u32[]{:S(2)}) %collective-permute-start.7) | collective-permute-done | bytes 262176 | tf_op jit(solution)/shard_map/ppermute | solution.py:413
  80.6 5.6 %collective-permute-done.8.refs_5_ = bf16[4,64,512]{2,1,0:T(8,128)(2,1)S(1)} collective-permute-done((bf16[4,64,512]{2,1,0:T(8,128)(2,1)S(1)}, bf16[4,64,512]{2,1,0:T(8,128)(2,1)S(1)}, u32[]{:S(2)}, u32[]{:S(2)}) %collective-permute-start.8) | collective-permute-done | bytes 262176 | tf_op jit(solution)/shard_map/ppermute | solution.py:413
  86.2 7.4 %collective-permute-done.9.refs_6_ = bf16[4,64,512]{2,1,0:T(8,128)(2,1)S(1)} collective-permute-done((bf16[4,64,512]{2,1,0:T(8,128)(2,1)S(1)}, bf16[4,64,512]{2,1,0:T(8,128)(2,1)S(1)}, u32[]{:S(2)}, u32[]{:S(2)}) %collective-permute-start.9) | collective-permute-done | bytes 262176 | tf_op jit(solution)/shard_map/ppermute | solution.py:413
  93.6 5.7 %collective-permute-done.10.refs_7_ = bf16[4,64,512]{2,1,0:T(8,128)(2,1)S(1)} collective-permute-done((bf16[4,64,512]{2,1,0:T(8,128)(2,1)S(1)}, bf16[4,64,512]{2,1,0:T(8,128)(2,1)S(1)}, u32[]{:S(2)}, u32[]{:S(2)}) %collective-permute-start.10) | collective-permute-done | bytes 262176 | tf_op jit(solution)/shard_map/ppermute | solution.py:413
  99.3 1.7 %place_rows.1 = bf16[16,64,512]{2,1,0:T(8,128)(2,1)} custom-call(s32[1]{0:T(128)} %bitcast.me_ref, s32[16]{0:T(128)S(1)} %bitcast.30, bf16[4,64,512]{2,1,0:T(8,128)(2,1)S(1)} %convolve_0.1.refs_0_, bf16[4,64,512]{2,1,0:T(8,128)(2,1)S(1)} %collective-permute-done.4.refs_1_, bf16[4,64,512]{2,1,0:T(8,128)(2,1)S(1)} %collective-permute-done.5.refs_2_, ...), custom_call_target="tpu_custom_call" | custom-call | bytes 2097152 | tf_op jit(solution)/shard_map/place_rows/pallas_call | solution.py:364
  (12 shorter events, 0.0 us)
Async XLA Ops:
  0.8 1.6 %copy-start.2 = (bf16[1,1,32,8,8,512]{5,4,3,2,1,0:T(8,128)(2,1)S(1)}, bf16[1,1,32,8,8,512]{5,4,3,2,1,0:T(8,128)(2,1)}, u32[]{:S(2)}) copy-start(bf16[1,1,32,8,8,512]{5,4,3,2,1,0:T(8,128)(2,1)} %param.9) | copy-start | bytes 6291460
  2.4 0.7 copy-start.4
  5.1 8.7 %collective-permute-start = (bf16[4,64,512]{2,1,0:T(8,128)(2,1)S(1)}, bf16[4,64,512]{2,1,0:T(8,128)(2,1)S(1)}, u32[]{:S(2)}, u32[]{:S(2)}) collective-permute-start(bf16[4,64,512]{2,1,0:T(8,128)(2,1)S(1)} %get-tuple-element.9), channel_id=1, source_target_pairs={{0,1},{1,2},{2,3},{3,4},{4,5},{5,6},{6,7},{8,9},{9,10},{10,11},{11... | collective-permute-start | bytes 786440 | tf_op jit(solution)/shard_map/ppermute | solution.py:378
  8.9 7.7 %copy-start.6 = (s32[1,1,8]{2,1,0:T(1,128)S(1)}, s32[1,1,8]{2,1,0:T(1,128)}, u32[]{:S(2)}) copy-start(s32[1,1,8]{2,1,0:T(1,128)} %param.13) | copy-start | bytes 100
  8.9 7.7 %collective-permute-start.1 = (bf16[4,64,512]{2,1,0:T(8,128)(2,1)S(1)}, bf16[4,64,512]{2,1,0:T(8,128)(2,1)S(1)}, u32[]{:S(2)}, u32[]{:S(2)}) collective-permute-start(bf16[4,64,512]{2,1,0:T(8,128)(2,1)S(1)} %get-tuple-element.10), channel_id=1, source_target_pairs={{1,0},{2,1},{3,2},{4,3},{5,4},{6,5},{7,6},{9,8},{10,9},{11,10},{12... | collective-permute-start | bytes 786440 | tf_op jit(solution)/shard_map/ppermute | solution.py:379
  13.8 8.9 %copy-start.3 = (bf16[27,64,64]{2,1,0:T(8,128)(2,1)S(1)}, bf16[27,64,64]{2,1,0:T(8,128)(2,1)}, u32[]{:S(2)}) copy-start(bf16[27,64,64]{2,1,0:T(8,128)(2,1)} %weights_ref.1) | copy-start | bytes 663556
  16.6 7.7 %copy-start.9 = (f32[64]{0:T(128)S(1)}, f32[64]{0:T(128)}, u32[]{:S(2)}) copy-start(f32[64]{0:T(128)} %param.17) | copy-start | bytes 772
  16.6 7.7 %copy-start.8 = (s32[1,1,8,4]{2,3,1,0:T(4,128)S(1)}, s32[1,1,8,4]{2,3,1,0:T(4,128)}, u32[]{:S(2)}) copy-start(s32[1,1,8,4]{2,3,1,0:T(4,128)} %param.14) | copy-start | bytes 388
  16.6 7.8 %copy-start.7 = (s32[1,1,32,27]{2,1,3,0:T(1,128)S(1)}, s32[1,1,32,27]{2,1,3,0:T(1,128)}, u32[]{:S(2)}) copy-start(s32[1,1,32,27]{2,1,3,0:T(1,128)} %param.11) | copy-start | bytes 10372
  18.3 8.7 %collective-permute-start.2 = (bf16[4,64,512]{2,1,0:T(8,128)(2,1)}, bf16[4,64,512]{2,1,0:T(8,128)(2,1)S(1)}, u32[]{:S(2)}, u32[]{:S(2)}) collective-permute-start(bf16[4,64,512]{2,1,0:T(8,128)(2,1)} %get-tuple-element.11), channel_id=1, source_target_pairs={{0,8},{8,16},{16,24},{1,9},{9,17},{17,25},{2,10},{10,18},{18,26},{... | collective-permute-start | bytes 786440 | tf_op jit(solution)/shard_map/ppermute | solution.py:378
  21.4 12.7 %collective-permute-start.3 = (bf16[4,64,512]{2,1,0:T(8,128)(2,1)S(1)}, bf16[4,64,512]{2,1,0:T(8,128)(2,1)S(1)}, u32[]{:S(2)}, u32[]{:S(2)}) collective-permute-start(bf16[4,64,512]{2,1,0:T(8,128)(2,1)S(1)} %get-tuple-element.12), channel_id=1, source_target_pairs={{8,0},{16,8},{24,16},{9,1},{17,9},{25,17},{10,2},{18,10},{26,18},{... | collective-permute-start | bytes 786440 | tf_op jit(solution)/shard_map/ppermute | solution.py:379
  23.0 1.2 %copy-start = (bf16[9,384,256]{2,1,0:T(8,128)(2,1)}, bf16[9,384,256]{2,1,0:T(8,128)(2,1)S(1)}, u32[]{:S(2)}) copy-start(bf16[9,384,256]{2,1,0:T(8,128)(2,1)S(1)} %band_weights.1.bands_ref) | copy-start | bytes 5308420
  34.1 1.5 %copy-start.1 = (bf16[9,384,256]{2,1,0:T(8,128)(2,1)S(1)}, bf16[9,384,256]{2,1,0:T(8,128)(2,1)}, u32[]{:S(2)}) copy-start(bf16[9,384,256]{2,1,0:T(8,128)(2,1)} %copy-done) | copy-start | bytes 5308420
  39.1 25.8 %collective-permute-start.4 = (bf16[4,64,512]{2,1,0:T(8,128)(2,1)S(1)}, bf16[4,64,512]{2,1,0:T(8,128)(2,1)S(1)}, u32[]{:S(2)}, u32[]{:S(2)}) collective-permute-start(bf16[4,64,512]{2,1,0:T(8,128)(2,1)S(1)} %convolve_1.1), channel_id=1, source_target_pairs={{0,1},{1,0},{2,3},{3,2},{4,5},{5,4},{6,7},{7,6},{8,9},{9,8},{10,11... | collective-permute-start | bytes 786440 | tf_op jit(solution)/shard_map/ppermute | solution.py:413
  42.7 23.6 %collective-permute-start.5 = (bf16[4,64,512]{2,1,0:T(8,128)(2,1)S(1)}, bf16[4,64,512]{2,1,0:T(8,128)(2,1)S(1)}, u32[]{:S(2)}, u32[]{:S(2)}) collective-permute-start(bf16[4,64,512]{2,1,0:T(8,128)(2,1)S(1)} %convolve_2.1), channel_id=1, source_target_pairs={{0,2},{1,3},{2,0},{3,1},{4,6},{5,7},{6,4},{7,5},{8,10},{9,11},{10,... | collective-permute-start | bytes 786440 | tf_op jit(solution)/shard_map/ppermute | solution.py:413
  46.3 24.3 %collective-permute-start.6 = (bf16[4,64,512]{2,1,0:T(8,128)(2,1)S(1)}, bf16[4,64,512]{2,1,0:T(8,128)(2,1)S(1)}, u32[]{:S(2)}, u32[]{:S(2)}) collective-permute-start(bf16[4,64,512]{2,1,0:T(8,128)(2,1)S(1)} %convolve_3.1), channel_id=1, source_target_pairs={{0,3},{1,2},{2,1},{3,0},{4,7},{5,6},{6,5},{7,4},{8,11},{9,10},{10,... | collective-permute-start | bytes 786440 | tf_op jit(solution)/shard_map/ppermute | solution.py:413
  52.0 28.6 %collective-permute-start.7 = (bf16[4,64,512]{2,1,0:T(8,128)(2,1)S(1)}, bf16[4,64,512]{2,1,0:T(8,128)(2,1)S(1)}, u32[]{:S(2)}, u32[]{:S(2)}) collective-permute-start(bf16[4,64,512]{2,1,0:T(8,128)(2,1)S(1)} %convolve_4.1), channel_id=1, source_target_pairs={{0,4},{1,5},{2,6},{3,7},{4,0},{5,1},{6,2},{7,3},{8,12},{9,13},{10,... | collective-permute-start | bytes 786440 | tf_op jit(solution)/shard_map/ppermute | solution.py:413
  56.3 29.9 %collective-permute-start.8 = (bf16[4,64,512]{2,1,0:T(8,128)(2,1)S(1)}, bf16[4,64,512]{2,1,0:T(8,128)(2,1)S(1)}, u32[]{:S(2)}, u32[]{:S(2)}) collective-permute-start(bf16[4,64,512]{2,1,0:T(8,128)(2,1)S(1)} %convolve_5.1), channel_id=1, source_target_pairs={{0,5},{1,4},{2,7},{3,6},{4,1},{5,0},{6,3},{7,2},{8,13},{9,12},{10,... | collective-permute-start | bytes 786440 | tf_op jit(solution)/shard_map/ppermute | solution.py:413
  64.9 34.4 %copy-start.5 = (s32[1,1,16]{2,1,0:T(1,128)S(1)}, s32[1,1,16]{2,1,0:T(1,128)}, u32[]{:S(2)}) copy-start(s32[1,1,16]{2,1,0:T(1,128)} %param.15) | copy-start | bytes 196
  64.9 28.6 %collective-permute-start.9 = (bf16[4,64,512]{2,1,0:T(8,128)(2,1)S(1)}, bf16[4,64,512]{2,1,0:T(8,128)(2,1)S(1)}, u32[]{:S(2)}, u32[]{:S(2)}) collective-permute-start(bf16[4,64,512]{2,1,0:T(8,128)(2,1)S(1)} %convolve_6.1), channel_id=1, source_target_pairs={{0,6},{1,7},{2,4},{3,5},{4,2},{5,3},{6,0},{7,1},{8,14},{9,15},{10,... | collective-permute-start | bytes 786440 | tf_op jit(solution)/shard_map/ppermute | solution.py:413
  66.3 33.0 %collective-permute-start.10 = (bf16[4,64,512]{2,1,0:T(8,128)(2,1)S(1)}, bf16[4,64,512]{2,1,0:T(8,128)(2,1)S(1)}, u32[]{:S(2)}, u32[]{:S(2)}) collective-permute-start(bf16[4,64,512]{2,1,0:T(8,128)(2,1)S(1)} %convolve_7.1), channel_id=1, source_target_pairs={{0,7},{1,6},{2,5},{3,4},{4,3},{5,2},{6,1},{7,0},{8,15},{9,14},{10,... | collective-permute-start | bytes 786440 | tf_op jit(solution)/shard_map/ppermute | solution.py:413
where the time goes:
time: 101 us
  waiting for transfers between devices  41 us (41%)
  Pallas kernels  36.7 us (36%)
  starting transfers between devices  17 us (17%)
  local copies, waits for them, and re-layouts  6.02 us (6%)
    ppermute x7, waiting for transfers between devices, on_device(): lax.ppermute(result, 'gy', [(d, d ^ m) for d in range(peers)])  28.7 us
    pallas_call x8, Pallas kernels, convolved(): pl.pallas_call(functools.partial(conv_kernel, distance=distance), out_sha...  28 us
    ppermute x2, waiting for transfers between devices, both_ways(): from_high = lax.ppermute(low, axis, [(i + 1, i) for i in range(ends)])  9.88 us
    ppermute x2, starting transfers between devices, both_ways(): from_low = lax.ppermute(high, axis, [(i, i + 1) for i in range(ends)])  6.9 us
    ppermute x7, starting transfers between devices, on_device(): lax.ppermute(result, 'gy', [(d, d ^ m) for d in range(peers)])  6.89 us
    unnamed x22, local copies, waits for them, and re-layouts  5.85 us
    ppermute x2, starting transfers between devices, both_ways(): from_high = lax.ppermute(low, axis, [(i + 1, i) for i in range(ends)])  3.21 us
    pallas_call x1, Pallas kernels, masked_all(): pl.pallas_call(mask_all_kernel, grid=(slots // per_step,), out_shape=jax....  3.01 us
  transfers between devices with their start and end apart: 11, of which 7 were waited for; matrix products, arithmetic and copies ran while one was open for 0% of the time, Pallas kernels for 27%

commit v1 on v0

--- a/solution.py
+++ b/solution.py
@@ -16,7 +16,9 @@
 K_BAND = (GROUP + 2) * C
 N_BAND = GROUP * C
 EXT = (BS + 2) * C
-VMEM_LIMIT = 48 * 1024 * 1024
+SHELL = (2 * BS, LANES + 6 * 128)
+VMEM_LIMIT = 16 * 1024 * 1024
+FIRST_LIMIT = 56 * 1024 * 1024
 
 ANY = pl.BlockSpec(memory_space=pl.ANY)
 SMEM = pl.BlockSpec(memory_space=pltpu.SMEM)
@@ -47,24 +49,79 @@
     v = voxel_ids(x)
     first = (x * ROWS) // WORD_BITS
     last = (x * ROWS + ROWS - 1) // WORD_BITS
-    words = jnp.full((BS, LANES), occ_ref[slot, first], jnp.int32)
+    words = jnp.full((BS, LANES), occ_ref[first, 0, slot], jnp.int32)
     for k in range(first + 1, last + 1):
-        words = jnp.where(v >= k * WORD_BITS, occ_ref[slot, k], words)
+        words = jnp.where(v >= k * WORD_BITS, occ_ref[k, 0, slot], words)
     return lax.shift_right_logical(words, shifts) & 1
 
 
-def mask_block(occ_ref, slot, shift_ref, source, target):
+def masked_planes(occ_ref, slot, shift_ref, source):
+    planes = []
     for i in range(BS // 2):
-        bits = jnp.concatenate(
-            [
-                plane_bits(occ_ref, slot, x, shift_ref[x])
-                for x in (2 * i, 2 * i + 1)
-            ],
-            axis=0,
-        )
+        values = source[pl.ds(2 * BS * i, 2 * BS), :].astype(jnp.float32)
+        for half in range(2):
+            x = 2 * i + half
+            bits = plane_bits(occ_ref, slot, x, shift_ref[x])
+            planes.append(jnp.where(bits > 0, values[half * BS : half * BS + BS], 0.0))
+    return planes
+
+
+def store_pair(ref, lanes, first, second):
+    ref[:, lanes] = jnp.concatenate([first, second], axis=0).astype(jnp.bfloat16)
+
+
+def store_block(ref, planes):
+    for i in range(BS // 2):
         rows = pl.ds(2 * BS * i, 2 * BS)
-        values = source[rows, :].astype(jnp.float32)
-        target[rows, :] = jnp.where(bits > 0, values, 0.0).astype(jnp.bfloat16)
+        ref[rows, :] = jnp.concatenate(planes[2 * i : 2 * i + 2], axis=0).astype(jnp.bfloat16)
+
+
+def columns_of(plane):
+    return [plane[:, 128 * i : 128 * i + 128] for i in range(LANES // 128)]
+
+
+def tile_ids():
+    rows = lax.broadcasted_iota(jnp.int32, (BS, 128), 0)
+    lanes = lax.broadcasted_iota(jnp.int32, (BS, 128), 1)
+    return rows, lanes
+
+
+def pack_shell(ref, planes):
+    rows, lanes = tile_ids()
+    store_pair(ref, pl.ds(0, LANES), planes[0], planes[BS - 1])
+    edges, ends = [], []
+    for x in range(1, BS - 1):
+        columns = columns_of(planes[x])
+        edges.append(jnp.where(lanes < C, columns[0], columns[-1]))
+        end = columns[0]
+        for i, column in enumerate(columns):
+            if i:
+                end = jnp.where(rows == i, pltpu.roll(column, i, 0), end)
+            end = jnp.where(rows == 4 + i, pltpu.roll(column, (i + 5) % BS, 0), end)
+        ends.append(end)
+    for k in range(3):
+        store_pair(ref, pl.ds(LANES + 128 * k, 128), edges[2 * k], edges[2 * k + 1])
+        store_pair(ref, pl.ds(LANES + 128 * (3 + k), 128), ends[2 * k], ends[2 * k + 1])
+
+
+def unpack_shell(ref, packed):
+    rows, _ = tile_ids()
+    outer = packed[:, pl.ds(0, LANES)].astype(jnp.float32)
+    planes = [None] * BS
+    planes[0], planes[BS - 1] = outer[:BS], outer[BS:]
+    for k in range(3):
+        edges = packed[:, pl.ds(LANES + 128 * k, 128)].astype(jnp.float32)
+        ends = packed[:, pl.ds(LANES + 128 * (3 + k), 128)].astype(jnp.float32)
+        for half in range(2):
+            cut = slice(half * BS, half * BS + BS)
+            edge, end = edges[cut], ends[cut]
+            columns = []
+            for i in range(4):
+                first = pltpu.roll(end, (BS - i) % BS, 0) if i else end
+                last = pltpu.roll(end, (3 - i) % BS, 0) if i != 3 else end
+                columns.append(jnp.where(rows == 0, first, jnp.where(rows == BS - 1, last, edge)))
+            planes[2 * k + 1 + half] = jnp.concatenate(columns, axis=1)
+    store_block(ref, planes)
 
 
 def outgoing_kernel(lists_ref, occ_ref, feat_ref, low_ref, high_ref, held, shift_ref, sems):
@@ -81,8 +138,10 @@
         copy.wait()
 
     def body(t, carry):
-        mask_block(occ_ref, lists_ref[t], shift_ref, held.at[t], low_ref.at[t])
-        mask_block(occ_ref, lists_ref[t + width], shift_ref, held.at[t + width], high_ref.at[t])
+        pack_shell(low_ref.at[t], masked_planes(occ_ref, lists_ref[t], shift_ref, held.at[t]))
+        pack_shell(
+            high_ref.at[t], masked_planes(occ_ref, lists_ref[t + width], shift_ref, held.at[t + width])
+        )
         return carry
 
     lax.fori_loop(0, width, body, 0)
@@ -90,7 +149,7 @@
 
 def masked_outgoing(face_lists, occupancy, features):
     count = face_lists.shape[0]
-    half = jax.ShapeDtypeStruct((count // 2, ROWS, LANES), jnp.bfloat16)
+    half = jax.ShapeDtypeStruct((count // 2,) + SHELL, jnp.bfloat16)
     return pl.pallas_call(
         outgoing_kernel,
         out_shape=(half, half),
@@ -101,43 +160,65 @@
             pltpu.VMEM((BS, BS, LANES), jnp.int32),
             pltpu.SemaphoreType.DMA((count,)),
         ],
-        compiler_params=params(),
+        compiler_params=pltpu.CompilerParams(vmem_limit_bytes=FIRST_LIMIT),
         cost_estimate=pl.CostEstimate(flops=2000000, bytes_accessed=2 * count * ROWS * LANES * 2, transcendentals=0),
         name="mask_outgoing",
     )(face_lists, occupancy, features)
 
 
-def mask_all_kernel(occ_ref, feat_ref, out_ref, shift_ref):
-    per_step = feat_ref.shape[0]
-    step = pl.program_id(0)
-
-    @pl.when(step == 0)
-    def _():
-        for x in range(BS):
-            shift_ref[x] = shift_amounts(x)
+def mask_all_kernel(occ_ref, feat_ref, pool_ref, shells_ref, shift_ref):
+    for x in range(BS):
+        shift_ref[x] = shift_amounts(x)
+    pool_ref[pool_ref.shape[0] - 1] = jnp.zeros((ROWS, LANES), jnp.bfloat16)
 
     def body(t, carry):
-        mask_block(occ_ref, step * per_step + t, shift_ref, feat_ref.at[t], out_ref.at[t])
+        planes = masked_planes(occ_ref, t, shift_ref, feat_ref.at[t])
+        store_block(pool_ref.at[t], planes)
+        pack_shell(shells_ref.at[t], planes)
         return carry
 
-    lax.fori_loop(0, per_step, body, 0)
-
-
-def masked_all(occupancy, features):
+    lax.fori_loop(0, feat_ref.shape[0], body, 0)
+
+
+def masked_all(occupancy, features, pool_blocks):
     slots = features.shape[0]
-    per_step = 8
-    spec = pl.BlockSpec((per_step, ROWS, LANES), lambda i: (i, 0, 0))
     return pl.pallas_call(
         mask_all_kernel,
-        grid=(slots // per_step,),
-        out_shape=jax.ShapeDtypeStruct(features.shape, jnp.bfloat16),
-        in_specs=[SMEM, spec],
-        out_specs=spec,
+        out_shape=(
+            jax.ShapeDtypeStruct((pool_blocks, ROWS, LANES), jnp.bfloat16),
+            jax.ShapeDtypeStruct((slots,) + SHELL, jnp.bfloat16),
+        ),
+        in_specs=[SMEM, VMEM],
+        out_specs=(VMEM, VMEM),
         scratch_shapes=[pltpu.VMEM((BS, BS, LANES), jnp.int32)],
         compiler_params=params(),
-        cost_estimate=pl.CostEstimate(flops=8000000, bytes_accessed=2 * slots * ROWS * LANES * 2, transcendentals=0),
+        cost_estimate=pl.CostEstimate(flops=8000000, bytes_accessed=3 * slots * ROWS * LANES * 2, transcendentals=0),
         name="mask_held",
     )(occupancy, features)
+
+
+def unpack_kernel(pool_in, low_ref, high_ref, pool_ref, *, start):
+    width = low_ref.shape[0]
+
+    def body(t, carry):
+        unpack_shell(pool_ref.at[start + t], low_ref.at[t])
+        unpack_shell(pool_ref.at[start + width + t], high_ref.at[t])
+        return carry
+
+    lax.fori_loop(0, width, body, 0)
+
+
+def unpacked(pool, low, high, start):
+    return pl.pallas_call(
+        functools.partial(unpack_kernel, start=start),
+        out_shape=jax.ShapeDtypeStruct(pool.shape, pool.dtype),
+        in_specs=[VMEM, VMEM, VMEM],
+        out_specs=VMEM,
+        input_output_aliases={0: 0},
+        compiler_params=params(),
+        cost_estimate=pl.CostEstimate(flops=100000, bytes_accessed=1000000, transcendentals=0),
+        name="unpack_%d" % start,
+    )(pool, low, high)
 
 
 def bands_kernel(weights_ref, out_ref):
@@ -194,7 +275,7 @@
         out_specs=(ANY, ANY),
         scratch_shapes=[pltpu.SemaphoreType.DMA((count,))],
         compiler_params=params(),
-        cost_estimate=pl.CostEstimate(flops=0, bytes_accessed=2 * count * ROWS * LANES * 2, transcendentals=0),
+        cost_estimate=pl.CostEstimate(flops=0, bytes_accessed=2 * count * SHELL[0] * SHELL[1] * 2, transcendentals=0),
         name="gather_relays",
     )(face_relays, held, low, high)
 
@@ -213,37 +294,19 @@
     neighbors_ref,
     bias_ref,
     bands_ref,
-    held_ref,
-    y_low_ref,
-    y_high_ref,
-    x_low_ref,
-    x_high_ref,
+    pool,
+    earlier_ref,
     out_ref,
-    pool,
     tiles,
     shift_ref,
-    sems,
     *,
     distance,
 ):
     items = out_ref.shape[0]
     pairs = (items + 1) // 2
-    held = held_ref.shape[0]
-    width = y_low_ref.shape[0]
-    parts = [held_ref, y_low_ref, y_high_ref, x_low_ref, x_high_ref]
-    starts = [0, held, held + width, held + 2 * width, held + 3 * width]
-    copies = [
-        pltpu.make_async_copy(part, pool.at[pl.ds(start, part.shape[0])], sems.at[i])
-        for i, (part, start) in enumerate(zip(parts, starts))
-    ]
-    for copy in copies:
-        copy.start()
-    pool[held + 4 * width] = jnp.zeros((ROWS, LANES), jnp.bfloat16)
     for x in range(BS):
         shift_ref[x] = shift_amounts(x)
     partner = me_ref[0] ^ distance
-    for copy in copies:
-        copy.wait()
 
     row_ids = lax.broadcasted_iota(jnp.int32, (BS, 128), 0)
     lane_low = lax.broadcasted_iota(jnp.int32, (2 * BS, 128), 1) < C
@@ -251,14 +314,14 @@
     is_first = row_ids == 0
 
     def slot_of(item):
-        return jnp.maximum(slots_ref[partner, jnp.minimum(item, items - 1)], 0)
+        return jnp.maximum(slots_ref[jnp.minimum(item, items - 1), partner], 0)
 
     def row_pair(slot, depth_x, depth_y, i):
         first = 9 * depth_x + 3 * depth_y
         rows = pl.ds(2 * BS * i, 2 * BS)
-        below = pool[neighbors_ref[slot, first], rows, pl.ds(LANES - 128, 128)]
-        own = pool[neighbors_ref[slot, first + 1], rows, :]
-        above = pool[neighbors_ref[slot, first + 2], rows, pl.ds(0, 128)]
+        below = pool[neighbors_ref[first, 0, slot], rows, pl.ds(LANES - 128, 128)]
+        own = pool[neighbors_ref[first + 1, 0, slot], rows, :]
+        above = pool[neighbors_ref[first + 2, 0, slot], rows, pl.ds(0, 128)]
         return extended_plane([v.astype(jnp.float32) for v in (below, own, above)], lane_low)
 
     def build(pair, carry):
@@ -311,66 +374,61 @@
                 ).astype(jnp.bfloat16)
 
 
-def convolved(distance, me, send_slots, occupancy, neighbors, bias, bands, parts):
-    items = send_slots.shape[1]
+def convolved(distance, me, send_slots, occupancy, neighbors, bias, bands, pool, earlier):
+    items = send_slots.shape[0]
     pairs = (items + 1) // 2
-    held = parts[0].shape[0]
-    pool_blocks = sum(part.shape[0] for part in parts) + 1
     return pl.pallas_call(
         functools.partial(conv_kernel, distance=distance),
         out_shape=jax.ShapeDtypeStruct((items, ROWS, LANES), jnp.bfloat16),
-        in_specs=[SMEM, SMEM, SMEM, SMEM, VMEM, VMEM] + [ANY] * 5,
+        in_specs=[SMEM, SMEM, SMEM, SMEM, VMEM, VMEM, VMEM, ANY],
         out_specs=VMEM,
         scratch_shapes=[
-            pltpu.VMEM((pool_blocks, ROWS, LANES), jnp.bfloat16),
             pltpu.VMEM((3, BS + 2, pairs, 2 * BS, EXT), jnp.bfloat16),
             pltpu.VMEM((BS, BS, LANES), jnp.int32),
-            pltpu.SemaphoreType.DMA((5,)),
         ],
         compiler_params=params(),
         cost_estimate=pl.CostEstimate(
             flops=2 * 9 * 2 * items * ROWS * K_BAND * N_BAND,
-            bytes_accessed=(pool_blocks + items) * ROWS * LANES * 2 + 9 * K_BAND * N_BAND * 2,
+            bytes_accessed=(27 + items) * ROWS * LANES * 2 + 9 * K_BAND * N_BAND * 2,
             transcendentals=0,
         ),
         name="convolve_%d" % distance,
-    )(me, send_slots, occupancy, neighbors, bias, bands, *parts)
-
-
-def place_kernel(me_ref, order_ref, *refs):
-    sems = refs[-1]
-    out_ref = refs[-2]
-    sources = refs[:-2]
+    )(me, send_slots, occupancy, neighbors, bias, bands, pool, earlier)
+
+
+def place_kernel(me_ref, order_ref, *refs, distances):
+    out_ref, sems = refs[-2:]
+    sources = refs[: len(distances)]
     items = sources[0].shape[0]
-
-    def body(r, carry):
-        name = order_ref[r]
-        distance = me_ref[0] ^ (name // items)
-        for m, source in enumerate(sources):
-
-            @pl.when(distance == m)
-            def _():
-                pltpu.make_async_copy(source.at[name % items], out_ref.at[r], sems.at[r]).start()
-
-        return carry
-
-    lax.fori_loop(0, out_ref.shape[0], body, 0)
-    for r in range(out_ref.shape[0]):
-        pltpu.make_async_copy(sources[0].at[0], out_ref.at[r], sems.at[r]).wait()
-
-
-def placed(me, receive_order, arrived):
+    names = [order_ref[r] for r in range(out_ref.shape[0])]
+
+    def each(act):
+        for distance, source in zip(distances, sources):
+            peer = me_ref[0] ^ distance
+            for r, name in enumerate(names):
+
+                @pl.when(name // items == peer)
+                def _():
+                    act(pltpu.make_async_copy(source.at[name % items], out_ref.at[r], sems.at[r]))
+
+    each(lambda copy: copy.start())
+    each(lambda copy: copy.wait())
+
+
+def placed(distances, me, receive_order, arrived, output):
     count = receive_order.shape[0]
-    return pl.pallas_call(
-        place_kernel,
+    filled = () if output is None else (output,)
+    return pl.pallas_call(
+        functools.partial(place_kernel, distances=distances),
         out_shape=jax.ShapeDtypeStruct((count, ROWS, LANES), jnp.bfloat16),
-        in_specs=[SMEM, SMEM] + [ANY] * len(arrived),
+        in_specs=[SMEM, SMEM] + [ANY] * (len(distances) + len(filled)),
         out_specs=ANY,
         scratch_shapes=[pltpu.SemaphoreType.DMA((count,))],
+        input_output_aliases={2 + len(distances): 0} if filled else {},
         compiler_params=params(),
-        cost_estimate=pl.CostEstimate(flops=0, bytes_accessed=2 * count * ROWS * LANES * 2, transcendentals=0),
-        name="place_rows",
-    )(me, receive_order, *arrived)
+        cost_estimate=pl.CostEstimate(flops=0, bytes_accessed=8 * ROWS * LANES * 2, transcendentals=0),
+        name="place_%d" % distances[0],
+    )(me, receive_order, *[arrived[m] for m in distances], *filled)
 
 
 def both_ways(low, high, axis):
@@ -378,6 +436,12 @@
     from_low = lax.ppermute(high, axis, [(i, i + 1) for i in range(ends)])
     from_high = lax.ppermute(low, axis, [(i + 1, i) for i in range(ends)])
     return from_low, from_high
+
+
+def sending_order(peers):
+    far = list(range(peers // 2, peers))
+    near = list(reversed(range(1, peers // 2)))
+    return far[:1] + near[:1] + far[1:2] + near[1:] + far[2:]
 
 
 def on_device(
@@ -393,25 +457,31 @@
 ):
     slots = features.shape[2]
     blocks = features.reshape(slots, ROWS, LANES)
-    words = occupancy[0, 0]
+    words = jnp.transpose(occupancy[0], (2, 0, 1))
+    table = jnp.transpose(neighbors[0], (2, 0, 1))
+    listed = jnp.transpose(send_slots[0, 0])
     me = lax.axis_index("gy").astype(jnp.int32).reshape(1)
     peers = lax.axis_size("gy")
+    faces = face_lists.shape[-1]
 
     out_low, out_high = masked_outgoing(face_lists[0, 0], words, blocks)
     y_low, y_high = both_ways(out_low, out_high, "gy")
-    held = masked_all(words, blocks)
+    pool, shells = masked_all(words, blocks, slots + 2 * faces + 1)
     bands = banded(weights)
     bias = jnp.tile(channel_bias, GROUP).reshape(1, N_BAND)
-    relay_low, relay_high = relayed(face_relays[0, 0], held, y_low, y_high)
+    relay_low, relay_high = relayed(face_relays[0, 0], shells, y_low, y_high)
     x_low, x_high = both_ways(relay_low, relay_high, "gx")
-
-    parts = (held, y_low, y_high, x_low, x_high)
-    arrived = [None] * peers
-    far_first = [m for m in range(peers) if m >= peers // 2] + [m for m in reversed(range(peers // 2))]
-    for m in far_first:
-        result = convolved(m, me, send_slots[0, 0], words, neighbors[0, 0], bias, bands, parts)
-        arrived[m] = lax.ppermute(result, "gy", [(d, d ^ m) for d in range(peers)]) if m else result
-    output = placed(me, receive_order[0, 0], arrived)
+    pool = unpacked(pool, y_low, y_high, slots)
+    pool = unpacked(pool, x_low, x_high, slots + faces)
+
+    result, output = bias, None
+    arrived = {}
+    for m in sending_order(peers):
+        result = convolved(m, me, listed, words, table, bias, bands, pool, result)
+        arrived[m] = lax.ppermute(result, "gy", [(d, d ^ m) for d in range(peers)])
+    arrived[0] = convolved(0, me, listed, words, table, bias, bands, pool, result)
+    for m in [0] + sending_order(peers):
+        output = placed((m,), me, receive_order[0, 0], arrived, output)
     return output.reshape(1, 1, output.shape[0], BS, BS, LANES)
 
 

time: 101 us -> 84.7 us (0.84)
  the two profiles are of different devices: /device:TPU:9 before, /device:TPU:1 now
where the time goes in v1:
time: 84.7 us; the launch traced here: 83.7 us
  Pallas kernels  45.5 us (54%)
  starting transfers between devices  22.3 us (26%)
  waiting for transfers between devices  13.5 us (16%)
  local copies, waits for them, and re-layouts  2.06 us (2%)
    pallas_call x8, Pallas kernels, convolved(): pl.pallas_call(functools.partial(conv_kernel, distance=distance), out_sha...  25 us
    pallas_call x8, Pallas kernels, placed(): pl.pallas_call(functools.partial(place_kernel, distances=distances), out_...  11.2 us
    ppermute x7, starting transfers between devices, on_device(): arrived[m] = lax.ppermute(result, 'gy', [(d, d ^ m) for d in range(peers)])  10.7 us
    ppermute x7, waiting for transfers between devices, on_device(): arrived[m] = lax.ppermute(result, 'gy', [(d, d ^ m) for d in range(peers)])  8.42 us
    ppermute x2, starting transfers between devices, both_ways(): from_low = lax.ppermute(high, axis, [(i, i + 1) for i in range(ends)])  8.39 us
    ppermute x2, waiting for transfers between devices, both_ways(): from_high = lax.ppermute(low, axis, [(i + 1, i) for i in range(ends)])  5.1 us
    pallas_call x1, Pallas kernels, masked_outgoing(): pl.pallas_call(outgoing_kernel, out_shape=(half, half), in_specs=[SMEM, S...  3.37 us
    ppermute x2, starting transfers between devices, both_ways(): from_high = lax.ppermute(low, axis, [(i + 1, i) for i in range(ends)])  3.2 us
  transfers between devices with their start and end apart: 11, of which 3 were waited for; matrix products, arithmetic and copies ran while one was open for 0% of the time, Pallas kernels for 38%

profile of v1, /device:TPU:1, one launch (start us, length us, event | category | flops | bytes accessed | tf_op | source)
XLA Modules:
  0.0 83.7 jit_solution(2782609208244755222)
XLA Ops:
  0.0 3.4 %mask_outgoing.1 = (bf16[4,16,1280]{2,1,0:T(8,128)(2,1)}, bf16[4,16,1280]{2,1,0:T(8,128)(2,1)}) custom-call(s32[8]{0:T(128)} %bitcast.52, s32[25,1,32]{2,1,0:T(1,128)} %bitcast.17, bf16[32,64,512]{2,1,0:T(8,128)(2,1)} %bitcast.15), custom_call_target="tpu_custom_call" | custom-call | flops 2000000 | bytes 1048576 | tf_op jit(solution)/shard_map/mask_outgoing/pallas_call | solution.py:153
  3.4 0.0 copy-start.10
  3.4 4.6 %collective-permute-start = (bf16[4,16,1280]{2,1,0:T(8,128)(2,1)}, bf16[4,16,1280]{2,1,0:T(8,128)(2,1)S(1)}, u32[]{:S(2)}, u32[]{:S(2)}) collective-permute-start(bf16[4,16,1280]{2,1,0:T(8,128)(2,1)} %get-tuple-element.12), channel_id=1, source_target_pairs={{0,1},{1,2},{2,3},{3,4},{4,5},{5,6},{6,7},{8,9},{9,10},{10,11},{11... | collective-permute-start | bytes 491528 | tf_op jit(solution)/shard_map/ppermute | solution.py:436
  8.0 1.9 %collective-permute-start.1 = (bf16[4,16,1280]{2,1,0:T(8,128)(2,1)}, bf16[4,16,1280]{2,1,0:T(8,128)(2,1)S(1)}, u32[]{:S(2)}, u32[]{:S(2)}) collective-permute-start(bf16[4,16,1280]{2,1,0:T(8,128)(2,1)} %get-tuple-element.13), channel_id=1, source_target_pairs={{1,0},{2,1},{3,2},{4,3},{5,4},{6,5},{7,6},{9,8},{10,9},{11,10},{12... | collective-permute-start | bytes 491528 | tf_op jit(solution)/shard_map/ppermute | solution.py:437
  9.9 0.0 copy-start.3
  9.9 0.7 copy-done.3
  10.7 3.1 %mask_held.1 = (bf16[49,64,512]{2,1,0:T(8,128)(2,1)S(1)}, bf16[32,16,1280]{2,1,0:T(8,128)(2,1)S(1)}) custom-call(s32[25,1,32]{2,1,0:T(1,128)S(1)} %bitcast.18, bf16[32,64,512]{2,1,0:T(8,128)(2,1)S(1)} %bitcast.16), custom_call_target="tpu_custom_call" | custom-call | flops 8000000 | bytes 6291456 | tf_op jit(solution)/shard_map/mask_held/pallas_call | solution.py:185
  13.8 1.1 %collective-permute-done.1.high_ref = bf16[4,16,1280]{2,1,0:T(8,128)(2,1)S(1)} collective-permute-done((bf16[4,16,1280]{2,1,0:T(8,128)(2,1)}, bf16[4,16,1280]{2,1,0:T(8,128)(2,1)S(1)}, u32[]{:S(2)}, u32[]{:S(2)}) %collective-permute-start.1) | collective-permute-done | bytes 163872 | tf_op jit(solution)/shard_map/ppermute | solution.py:437
  14.8 1.3 %gather_relays.1 = (bf16[4,16,1280]{2,1,0:T(8,128)(2,1)}, bf16[4,16,1280]{2,1,0:T(8,128)(2,1)}) custom-call(s32[8]{0:T(128)S(1)} %bitcast.51, bf16[32,16,1280]{2,1,0:T(8,128)(2,1)S(1)} %get-tuple-element.14.held_ref, bf16[4,16,1280]{2,1,0:T(8,128)(2,1)S(1)} %collective-permute-done.low_ref, bf16[4,16,1280]{2,1,0:T(8,128)(2,1)S(1)} %collective-permute-done.1.high_ref), custom_call_target="tpu_custom_call" | custom-call | bytes 655360 | tf_op jit(solution)/shard_map/gather_relays/pallas_call | solution.py:271
  16.2 3.8 %collective-permute-start.2 = (bf16[4,16,1280]{2,1,0:T(8,128)(2,1)}, bf16[4,16,1280]{2,1,0:T(8,128)(2,1)}, u32[]{:S(2)}, u32[]{:S(2)}) collective-permute-start(bf16[4,16,1280]{2,1,0:T(8,128)(2,1)} %get-tuple-element.15), channel_id=1, source_target_pairs={{0,8},{8,16},{16,24},{1,9},{9,17},{17,25},{2,10},{10,18},{18,26},{... | collective-permute-start | bytes 491528 | tf_op jit(solution)/shard_map/ppermute | solution.py:436
  20.0 1.3 %collective-permute-start.3 = (bf16[4,16,1280]{2,1,0:T(8,128)(2,1)}, bf16[4,16,1280]{2,1,0:T(8,128)(2,1)}, u32[]{:S(2)}, u32[]{:S(2)}) collective-permute-start(bf16[4,16,1280]{2,1,0:T(8,128)(2,1)} %get-tuple-element.16), channel_id=1, source_target_pairs={{8,0},{16,8},{24,16},{9,1},{17,9},{25,17},{10,2},{18,10},{26,18},{... | collective-permute-start | bytes 491528 | tf_op jit(solution)/shard_map/ppermute | solution.py:437
  21.3 0.2 band_weights.1.bands_ref
  21.5 1.2 %copy-done = bf16[9,384,256]{2,1,0:T(8,128)(2,1)} copy-done((bf16[9,384,256]{2,1,0:T(8,128)(2,1)}, bf16[9,384,256]{2,1,0:T(8,128)(2,1)S(1)}, u32[]{:S(2)}) %copy-start) | copy-done | bytes 1769496
  22.7 0.1 reshape_tile.3.bias_ref.earlier_ref
  22.8 0.1 unpack_32.1.pool_in
  23.0 0.0 copy-start.4
  23.0 0.0 copy-start.5
  23.0 0.0 copy-start.7
  23.0 0.0 collective-permute-done.2.low_ref
  23.0 4.0 %collective-permute-done.3.high_ref = bf16[4,16,1280]{2,1,0:T(8,128)(2,1)} collective-permute-done((bf16[4,16,1280]{2,1,0:T(8,128)(2,1)}, bf16[4,16,1280]{2,1,0:T(8,128)(2,1)}, u32[]{:S(2)}, u32[]{:S(2)}) %collective-permute-start.3) | collective-permute-done | bytes 163872 | tf_op jit(solution)/shard_map/ppermute | solution.py:437
  27.0 1.1 %unpack_40.1.pool = bf16[49,64,512]{2,1,0:T(8,128)(2,1)S(1)} custom-call(bf16[49,64,512]{2,1,0:T(8,128)(2,1)S(1)} %unpack_32.1.pool_in, bf16[4,16,1280]{2,1,0:T(8,128)(2,1)} %collective-permute-done.2.low_ref, bf16[4,16,1280]{2,1,0:T(8,128)(2,1)} %collective-permute-done.3.high_ref), custom_call_target="tpu_custom_call", output_to_operand_aliasing={{}: (0, {})} | custom-call | flops 100000 | bytes 1000000 | tf_op jit(solution)/shard_map/unpack_40/pallas_call | solution.py:212
  28.2 3.1 %convolve_4.1.earlier_ref = bf16[4,64,512]{2,1,0:T(8,128)(2,1)S(1)} custom-call(s32[1]{0:T(128)} %bitcast.me_ref, s32[4,8]{1,0:T(4,128)S(1)} %bitcast.35, s32[25,1,32]{2,1,0:T(1,128)S(1)} %bitcast.19, s32[27,1,32]{2,1,0:T(1,128)S(1)} %bitcast.27, f32[1,256]{1,0:T(1,128)S(1)} %reshape_tile.3.bias_ref.earlier_ref, bf16[9,384,256]{2,1,0:T(8,128)(2,1)S(1)} %copy-done.1, ...), custom_call_target="tpu_custom_call" | custom-call | flops 905969664 | bytes 3801088 | tf_op jit(solution)/shard_map/convolve_4/pallas_call | solution.py:380
  31.3 3.1 %convolve_3.1.earlier_ref = bf16[4,64,512]{2,1,0:T(8,128)(2,1)S(1)} custom-call(s32[1]{0:T(128)} %bitcast.me_ref, s32[4,8]{1,0:T(4,128)S(1)} %bitcast.36, s32[25,1,32]{2,1,0:T(1,128)S(1)} %bitcast.20, s32[27,1,32]{2,1,0:T(1,128)S(1)} %bitcast.28, f32[1,256]{1,0:T(1,128)S(1)} %reshape_tile.3.bias_ref.earlier_ref, bf16[9,384,256]{2,1,0:T(8,128)(2,1)S(1)} %copy-done.1, ...), custom_call_target="tpu_custom_call" | custom-call | flops 905969664 | bytes 3801088 | tf_op jit(solution)/shard_map/convolve_3/pallas_call | solution.py:380
  34.5 4.4 %collective-permute-start.10 = (bf16[4,64,512]{2,1,0:T(8,128)(2,1)S(1)}, bf16[4,64,512]{2,1,0:T(8,128)(2,1)S(1)}, u32[]{:S(2)}, u32[]{:S(2)}) collective-permute-start(bf16[4,64,512]{2,1,0:T(8,128)(2,1)S(1)} %convolve_4.1.earlier_ref), channel_id=1, source_target_pairs={{0,4},{1,5},{2,6},{3,7},{4,0},{5,1},{6,2},{7,3},{8,12},{9,13},{10,... | collective-permute-start | bytes 786440 | tf_op jit(solution)/shard_map/ppermute | solution.py:481
  38.9 3.1 %convolve_5.1.earlier_ref = bf16[4,64,512]{2,1,0:T(8,128)(2,1)S(1)} custom-call(s32[1]{0:T(128)} %bitcast.me_ref, s32[4,8]{1,0:T(4,128)S(1)} %bitcast.37, s32[25,1,32]{2,1,0:T(1,128)S(1)} %bitcast.21, s32[27,1,32]{2,1,0:T(1,128)S(1)} %bitcast.29, f32[1,256]{1,0:T(1,128)S(1)} %reshape_tile.3.bias_ref.earlier_ref, bf16[9,384,256]{2,1,0:T(8,128)(2,1)S(1)} %copy-done.1, ...), custom_call_target="tpu_custom_call" | custom-call | flops 905969664 | bytes 3801088 | tf_op jit(solution)/shard_map/convolve_5/pallas_call | solution.py:380
  42.0 0.1 collective-permute-start.9
  42.1 3.1 %convolve_2.1.earlier_ref = bf16[4,64,512]{2,1,0:T(8,128)(2,1)S(1)} custom-call(s32[1]{0:T(128)} %bitcast.me_ref, s32[4,8]{1,0:T(4,128)S(1)} %bitcast.38, s32[25,1,32]{2,1,0:T(1,128)S(1)} %bitcast.22, s32[27,1,32]{2,1,0:T(1,128)S(1)} %bitcast.30, f32[1,256]{1,0:T(1,128)S(1)} %reshape_tile.3.bias_ref.earlier_ref, bf16[9,384,256]{2,1,0:T(8,128)(2,1)S(1)} %copy-done.1, ...), custom_call_target="tpu_custom_call" | custom-call | flops 905969664 | bytes 3801088 | tf_op jit(solution)/shard_map/convolve_2/pallas_call | solution.py:380
  45.3 1.5 %collective-permute-start.8 = (bf16[4,64,512]{2,1,0:T(8,128)(2,1)S(1)}, bf16[4,64,512]{2,1,0:T(8,128)(2,1)S(1)}, u32[]{:S(2)}, u32[]{:S(2)}) collective-permute-start(bf16[4,64,512]{2,1,0:T(8,128)(2,1)S(1)} %convolve_5.1.earlier_ref), channel_id=1, source_target_pairs={{0,5},{1,4},{2,7},{3,6},{4,1},{5,0},{6,3},{7,2},{8,13},{9,12},{10,... | collective-permute-start | bytes 786440 | tf_op jit(solution)/shard_map/ppermute | solution.py:481
  46.7 0.6 collective-permute-start.7
  47.4 3.1 %convolve_1.1.earlier_ref = bf16[4,64,512]{2,1,0:T(8,128)(2,1)S(1)} custom-call(s32[1]{0:T(128)} %bitcast.me_ref, s32[4,8]{1,0:T(4,128)S(1)} %bitcast.39, s32[25,1,32]{2,1,0:T(1,128)S(1)} %bitcast.23, s32[27,1,32]{2,1,0:T(1,128)S(1)} %bitcast.31, f32[1,256]{1,0:T(1,128)S(1)} %reshape_tile.3.bias_ref.earlier_ref, bf16[9,384,256]{2,1,0:T(8,128)(2,1)S(1)} %copy-done.1, ...), custom_call_target="tpu_custom_call" | custom-call | flops 905969664 | bytes 3801088 | tf_op jit(solution)/shard_map/convolve_1/pallas_call | solution.py:380
  50.5 0.4 collective-permute-start.6
  50.9 3.1 %convolve_6.1.earlier_ref = bf16[4,64,512]{2,1,0:T(8,128)(2,1)S(1)} custom-call(s32[1]{0:T(128)} %bitcast.me_ref, s32[4,8]{1,0:T(4,128)S(1)} %bitcast.40, s32[25,1,32]{2,1,0:T(1,128)S(1)} %bitcast.24, s32[27,1,32]{2,1,0:T(1,128)S(1)} %bitcast.32, f32[1,256]{1,0:T(1,128)S(1)} %reshape_tile.3.bias_ref.earlier_ref, bf16[9,384,256]{2,1,0:T(8,128)(2,1)S(1)} %copy-done.1, ...), custom_call_target="tpu_custom_call" | custom-call | flops 905969664 | bytes 3801088 | tf_op jit(solution)/shard_map/convolve_6/pallas_call | solution.py:380
  54.0 3.1 %convolve_7.1.earlier_ref = bf16[4,64,512]{2,1,0:T(8,128)(2,1)S(1)} custom-call(s32[1]{0:T(128)} %bitcast.me_ref, s32[4,8]{1,0:T(4,128)S(1)} %bitcast.41, s32[25,1,32]{2,1,0:T(1,128)S(1)} %bitcast.25, s32[27,1,32]{2,1,0:T(1,128)S(1)} %bitcast.33, f32[1,256]{1,0:T(1,128)S(1)} %reshape_tile.3.bias_ref.earlier_ref, bf16[9,384,256]{2,1,0:T(8,128)(2,1)S(1)} %copy-done.1, ...), custom_call_target="tpu_custom_call" | custom-call | flops 905969664 | bytes 3801088 | tf_op jit(solution)/shard_map/convolve_7/pallas_call | solution.py:380
  57.2 0.0 copy-start.8
  57.2 0.0 collective-permute-done.10.refs_0_
  57.2 2.1 %collective-permute-start.5 = (bf16[4,64,512]{2,1,0:T(8,128)(2,1)S(1)}, bf16[4,64,512]{2,1,0:T(8,128)(2,1)S(1)}, u32[]{:S(2)}, u32[]{:S(2)}) collective-permute-start(bf16[4,64,512]{2,1,0:T(8,128)(2,1)S(1)} %convolve_6.1.earlier_ref), channel_id=1, source_target_pairs={{0,6},{1,7},{2,4},{3,5},{4,2},{5,3},{6,0},{7,1},{8,14},{9,15},{10,... | collective-permute-start | bytes 786440 | tf_op jit(solution)/shard_map/ppermute | solution.py:481
  59.3 1.5 %collective-permute-start.4 = (bf16[4,64,512]{2,1,0:T(8,128)(2,1)S(1)}, bf16[4,64,512]{2,1,0:T(8,128)(2,1)S(1)}, u32[]{:S(2)}, u32[]{:S(2)}) collective-permute-start(bf16[4,64,512]{2,1,0:T(8,128)(2,1)S(1)} %convolve_7.1.earlier_ref), channel_id=1, source_target_pairs={{0,7},{1,6},{2,5},{3,4},{4,3},{5,2},{6,1},{7,0},{8,15},{9,14},{10,... | collective-permute-start | bytes 786440 | tf_op jit(solution)/shard_map/ppermute | solution.py:481
  60.9 3.1 %convolve_0.1.refs_0_ = bf16[4,64,512]{2,1,0:T(8,128)(2,1)S(1)} custom-call(s32[1]{0:T(128)} %bitcast.me_ref, s32[4,8]{1,0:T(4,128)S(1)} %bitcast.42, s32[25,1,32]{2,1,0:T(1,128)S(1)} %bitcast.26, s32[27,1,32]{2,1,0:T(1,128)S(1)} %bitcast.34, f32[1,256]{1,0:T(1,128)S(1)} %reshape_tile.3.bias_ref.earlier_ref, bf16[9,384,256]{2,1,0:T(8,128)(2,1)S(1)} %copy-done.1, ...), custom_call_target="tpu_custom_call" | custom-call | flops 905969664 | bytes 3801088 | tf_op jit(solution)/shard_map/convolve_0/pallas_call | solution.py:380
  64.0 1.4 %place_0.1.refs_1_ = bf16[16,64,512]{2,1,0:T(8,128)(2,1)} custom-call(s32[1]{0:T(128)} %bitcast.me_ref, s32[16]{0:T(128)S(1)} %bitcast.43, bf16[4,64,512]{2,1,0:T(8,128)(2,1)S(1)} %convolve_0.1.refs_0_), custom_call_target="tpu_custom_call" | custom-call | bytes 524288 | tf_op jit(solution)/shard_map/place_0/pallas_call | solution.py:421
  65.4 1.4 %place_4.1.refs_1_ = bf16[16,64,512]{2,1,0:T(8,128)(2,1)} custom-call(s32[1]{0:T(128)} %bitcast.me_ref, s32[16]{0:T(128)S(1)} %bitcast.44, bf16[4,64,512]{2,1,0:T(8,128)(2,1)S(1)} %collective-permute-done.10.refs_0_, bf16[16,64,512]{2,1,0:T(8,128)(2,1)} %place_0.1.refs_1_), custom_call_target="tpu_custom_call", output_to_operand_aliasing={{}: (3, {})} | custom-call | bytes 524288 | tf_op jit(solution)/shard_map/place_4/pallas_call | solution.py:421
  66.8 1.4 %place_3.1.refs_1_ = bf16[16,64,512]{2,1,0:T(8,128)(2,1)} custom-call(s32[1]{0:T(128)} %bitcast.me_ref, s32[16]{0:T(128)S(1)} %bitcast.45, bf16[4,64,512]{2,1,0:T(8,128)(2,1)S(1)} %collective-permute-done.9.refs_0_, bf16[16,64,512]{2,1,0:T(8,128)(2,1)} %place_4.1.refs_1_), custom_call_target="tpu_custom_call", output_to_operand_aliasing={{}: (3, {})} | custom-call | bytes 524288 | tf_op jit(solution)/shard_map/place_3/pallas_call | solution.py:421
  68.2 0.0 collective-permute-done.8.refs_0_
  68.2 1.4 %place_5.1.refs_1_ = bf16[16,64,512]{2,1,0:T(8,128)(2,1)} custom-call(s32[1]{0:T(128)} %bitcast.me_ref, s32[16]{0:T(128)S(1)} %bitcast.46, bf16[4,64,512]{2,1,0:T(8,128)(2,1)S(1)} %collective-permute-done.8.refs_0_, bf16[16,64,512]{2,1,0:T(8,128)(2,1)} %place_3.1.refs_1_), custom_call_target="tpu_custom_call", output_to_operand_aliasing={{}: (3, {})} | custom-call | bytes 524288 | tf_op jit(solution)/shard_map/place_5/pallas_call | solution.py:421
  69.6 8.4 %collective-permute-done.7.refs_0_ = bf16[4,64,512]{2,1,0:T(8,128)(2,1)S(1)} collective-permute-done((bf16[4,64,512]{2,1,0:T(8,128)(2,1)S(1)}, bf16[4,64,512]{2,1,0:T(8,128)(2,1)S(1)}, u32[]{:S(2)}, u32[]{:S(2)}) %collective-permute-start.7) | collective-permute-done | bytes 262176 | tf_op jit(solution)/shard_map/ppermute | solution.py:481
  78.0 1.4 %place_2.1.refs_1_ = bf16[16,64,512]{2,1,0:T(8,128)(2,1)} custom-call(s32[1]{0:T(128)} %bitcast.me_ref, s32[16]{0:T(128)S(1)} %bitcast.47, bf16[4,64,512]{2,1,0:T(8,128)(2,1)S(1)} %collective-permute-done.7.refs_0_, bf16[16,64,512]{2,1,0:T(8,128)(2,1)} %place_5.1.refs_1_), custom_call_target="tpu_custom_call", output_to_operand_aliasing={{}: (3, {})} | custom-call | bytes 524288 | tf_op jit(solution)/shard_map/place_2/pallas_call | solution.py:421
  79.5 1.4 %place_1.1.refs_1_ = bf16[16,64,512]{2,1,0:T(8,128)(2,1)} custom-call(s32[1]{0:T(128)} %bitcast.me_ref, s32[16]{0:T(128)S(1)} %bitcast.48, bf16[4,64,512]{2,1,0:T(8,128)(2,1)S(1)} %collective-permute-done.6.refs_0_, bf16[16,64,512]{2,1,0:T(8,128)(2,1)} %place_2.1.refs_1_), custom_call_target="tpu_custom_call", output_to_operand_aliasing={{}: (3, {})} | custom-call | bytes 524288 | tf_op jit(solution)/shard_map/place_1/pallas_call | solution.py:421
  80.8 1.4 %place_6.1.refs_1_ = bf16[16,64,512]{2,1,0:T(8,128)(2,1)} custom-call(s32[1]{0:T(128)} %bitcast.me_ref, s32[16]{0:T(128)S(1)} %bitcast.49, bf16[4,64,512]{2,1,0:T(8,128)(2,1)S(1)} %collective-permute-done.5.refs_0_, bf16[16,64,512]{2,1,0:T(8,128)(2,1)} %place_1.1.refs_1_), custom_call_target="tpu_custom_call", output_to_operand_aliasing={{}: (3, {})} | custom-call | bytes 524288 | tf_op jit(solution)/shard_map/place_6/pallas_call | solution.py:421
  82.2 1.4 %place_7.1 = bf16[16,64,512]{2,1,0:T(8,128)(2,1)} custom-call(s32[1]{0:T(128)} %bitcast.me_ref, s32[16]{0:T(128)S(1)} %bitcast.50, bf16[4,64,512]{2,1,0:T(8,128)(2,1)S(1)} %collective-permute-done.4.refs_0_, bf16[16,64,512]{2,1,0:T(8,128)(2,1)} %place_6.1.refs_1_), custom_call_target="tpu_custom_call", output_to_operand_aliasing={{}: (3, {})} | custom-call | bytes 524288 | tf_op jit(solution)/shard_map/place_7/pallas_call | solution.py:421
  (20 shorter events, 0.0 us)
Async XLA Ops:
  0.0 9.9 %copy-start.2 = (bf16[1,1,32,8,8,512]{5,4,3,2,1,0:T(8,128)(2,1)S(1)}, bf16[1,1,32,8,8,512]{5,4,3,2,1,0:T(8,128)(2,1)}, u32[]{:S(2)}) copy-start(bf16[1,1,32,8,8,512]{5,4,3,2,1,0:T(8,128)(2,1)} %param.9) | copy-start | bytes 6291460
  0.0 14.8 %copy-start.9 = (s32[1,1,8]{2,1,0:T(1,128)S(1)}, s32[1,1,8]{2,1,0:T(1,128)}, u32[]{:S(2)}) copy-start(s32[1,1,8]{2,1,0:T(1,128)} %param.13) | copy-start | bytes 100
  3.4 19.4 %copy-start.10 = (f32[64]{0:T(128)S(1)}, f32[64]{0:T(128)}, u32[]{:S(2)}) copy-start(f32[64]{0:T(128)} %param.17) | copy-start | bytes 772
  3.4 10.3 %collective-permute-start = (bf16[4,16,1280]{2,1,0:T(8,128)(2,1)}, bf16[4,16,1280]{2,1,0:T(8,128)(2,1)S(1)}, u32[]{:S(2)}, u32[]{:S(2)}) collective-permute-start(bf16[4,16,1280]{2,1,0:T(8,128)(2,1)} %get-tuple-element.12), channel_id=1, source_target_pairs={{0,1},{1,2},{2,3},{3,4},{4,5},{5,6},{6,7},{8,9},{9,10},{10,11},{11... | collective-permute-start | bytes 491528 | tf_op jit(solution)/shard_map/ppermute | solution.py:436
  8.0 6.8 %collective-permute-start.1 = (bf16[4,16,1280]{2,1,0:T(8,128)(2,1)}, bf16[4,16,1280]{2,1,0:T(8,128)(2,1)S(1)}, u32[]{:S(2)}, u32[]{:S(2)}) collective-permute-start(bf16[4,16,1280]{2,1,0:T(8,128)(2,1)} %get-tuple-element.13), channel_id=1, source_target_pairs={{1,0},{2,1},{3,2},{4,3},{5,4},{6,5},{7,6},{9,8},{10,9},{11,10},{12... | collective-permute-start | bytes 491528 | tf_op jit(solution)/shard_map/ppermute | solution.py:437
  9.9 0.7 copy-start.3
  10.6 10.6 %copy-start.6 = (bf16[27,64,64]{2,1,0:T(8,128)(2,1)S(1)}, bf16[27,64,64]{2,1,0:T(8,128)(2,1)}, u32[]{:S(2)}) copy-start(bf16[27,64,64]{2,1,0:T(8,128)(2,1)} %weights_ref.1) | copy-start | bytes 663556
  16.2 6.8 %collective-permute-start.2 = (bf16[4,16,1280]{2,1,0:T(8,128)(2,1)}, bf16[4,16,1280]{2,1,0:T(8,128)(2,1)}, u32[]{:S(2)}, u32[]{:S(2)}) collective-permute-start(bf16[4,16,1280]{2,1,0:T(8,128)(2,1)} %get-tuple-element.15), channel_id=1, source_target_pairs={{0,8},{8,16},{16,24},{1,9},{9,17},{17,25},{2,10},{10,18},{18,26},{... | collective-permute-start | bytes 491528 | tf_op jit(solution)/shard_map/ppermute | solution.py:436
  20.0 7.1 %collective-permute-start.3 = (bf16[4,16,1280]{2,1,0:T(8,128)(2,1)}, bf16[4,16,1280]{2,1,0:T(8,128)(2,1)}, u32[]{:S(2)}, u32[]{:S(2)}) collective-permute-start(bf16[4,16,1280]{2,1,0:T(8,128)(2,1)} %get-tuple-element.16), channel_id=1, source_target_pairs={{8,0},{16,8},{24,16},{9,1},{17,9},{25,17},{10,2},{18,10},{26,18},{... | collective-permute-start | bytes 491528 | tf_op jit(solution)/shard_map/ppermute | solution.py:437
  21.5 1.2 %copy-start = (bf16[9,384,256]{2,1,0:T(8,128)(2,1)}, bf16[9,384,256]{2,1,0:T(8,128)(2,1)S(1)}, u32[]{:S(2)}) copy-start(bf16[9,384,256]{2,1,0:T(8,128)(2,1)S(1)} %band_weights.1.bands_ref) | copy-start | bytes 5308420
  23.0 5.2 %copy-start.1 = (bf16[9,384,256]{2,1,0:T(8,128)(2,1)S(1)}, bf16[9,384,256]{2,1,0:T(8,128)(2,1)}, u32[]{:S(2)}) copy-start(bf16[9,384,256]{2,1,0:T(8,128)(2,1)} %copy-done) | copy-start | bytes 5308420
  23.0 5.2 %copy-start.4 = (s32[1,1,32,25]{2,1,3,0:T(1,128)S(1)}, s32[1,1,32,25]{2,1,3,0:T(1,128)}, u32[]{:S(2)}) copy-start(s32[1,1,32,25]{2,1,3,0:T(1,128)} %param.10) | copy-start | bytes 9604
  23.0 5.2 %copy-start.5 = (s32[1,1,32,27]{2,1,3,0:T(1,128)S(1)}, s32[1,1,32,27]{2,1,3,0:T(1,128)}, u32[]{:S(2)}) copy-start(s32[1,1,32,27]{2,1,3,0:T(1,128)} %param.11) | copy-start | bytes 10372
  23.0 5.2 %copy-start.7 = (s32[1,1,8,4]{2,3,1,0:T(4,128)S(1)}, s32[1,1,8,4]{2,3,1,0:T(4,128)}, u32[]{:S(2)}) copy-start(s32[1,1,8,4]{2,3,1,0:T(4,128)} %param.14) | copy-start | bytes 388
  34.5 22.7 %collective-permute-start.10 = (bf16[4,64,512]{2,1,0:T(8,128)(2,1)S(1)}, bf16[4,64,512]{2,1,0:T(8,128)(2,1)S(1)}, u32[]{:S(2)}, u32[]{:S(2)}) collective-permute-start(bf16[4,64,512]{2,1,0:T(8,128)(2,1)S(1)} %convolve_4.1.earlier_ref), channel_id=1, source_target_pairs={{0,4},{1,5},{2,6},{3,7},{4,0},{5,1},{6,2},{7,3},{8,12},{9,13},{10,... | collective-permute-start | bytes 786440 | tf_op jit(solution)/shard_map/ppermute | solution.py:481
  42.0 17.3 %collective-permute-start.9 = (bf16[4,64,512]{2,1,0:T(8,128)(2,1)S(1)}, bf16[4,64,512]{2,1,0:T(8,128)(2,1)S(1)}, u32[]{:S(2)}, u32[]{:S(2)}) collective-permute-start(bf16[4,64,512]{2,1,0:T(8,128)(2,1)S(1)} %convolve_3.1.earlier_ref), channel_id=1, source_target_pairs={{0,3},{1,2},{2,1},{3,0},{4,7},{5,6},{6,5},{7,4},{8,11},{9,10},{10,... | collective-permute-start | bytes 786440 | tf_op jit(solution)/shard_map/ppermute | solution.py:481
  45.3 23.0 %collective-permute-start.8 = (bf16[4,64,512]{2,1,0:T(8,128)(2,1)S(1)}, bf16[4,64,512]{2,1,0:T(8,128)(2,1)S(1)}, u32[]{:S(2)}, u32[]{:S(2)}) collective-permute-start(bf16[4,64,512]{2,1,0:T(8,128)(2,1)S(1)} %convolve_5.1.earlier_ref), channel_id=1, source_target_pairs={{0,5},{1,4},{2,7},{3,6},{4,1},{5,0},{6,3},{7,2},{8,13},{9,12},{10,... | collective-permute-start | bytes 786440 | tf_op jit(solution)/shard_map/ppermute | solution.py:481
  46.7 31.3 %collective-permute-start.7 = (bf16[4,64,512]{2,1,0:T(8,128)(2,1)S(1)}, bf16[4,64,512]{2,1,0:T(8,128)(2,1)S(1)}, u32[]{:S(2)}, u32[]{:S(2)}) collective-permute-start(bf16[4,64,512]{2,1,0:T(8,128)(2,1)S(1)} %convolve_2.1.earlier_ref), channel_id=1, source_target_pairs={{0,2},{1,3},{2,0},{3,1},{4,6},{5,7},{6,4},{7,5},{8,10},{9,11},{10,... | collective-permute-start | bytes 786440 | tf_op jit(solution)/shard_map/ppermute | solution.py:481
  50.5 29.0 %collective-permute-start.6 = (bf16[4,64,512]{2,1,0:T(8,128)(2,1)S(1)}, bf16[4,64,512]{2,1,0:T(8,128)(2,1)S(1)}, u32[]{:S(2)}, u32[]{:S(2)}) collective-permute-start(bf16[4,64,512]{2,1,0:T(8,128)(2,1)S(1)} %convolve_1.1.earlier_ref), channel_id=1, source_target_pairs={{0,1},{1,0},{2,3},{3,2},{4,5},{5,4},{6,7},{7,6},{8,9},{9,8},{10,11... | collective-permute-start | bytes 786440 | tf_op jit(solution)/shard_map/ppermute | solution.py:481
  57.2 6.8 %copy-start.8 = (s32[1,1,16]{2,1,0:T(1,128)S(1)}, s32[1,1,16]{2,1,0:T(1,128)}, u32[]{:S(2)}) copy-start(s32[1,1,16]{2,1,0:T(1,128)} %param.15) | copy-start | bytes 196
  57.2 23.6 %collective-permute-start.5 = (bf16[4,64,512]{2,1,0:T(8,128)(2,1)S(1)}, bf16[4,64,512]{2,1,0:T(8,128)(2,1)S(1)}, u32[]{:S(2)}, u32[]{:S(2)}) collective-permute-start(bf16[4,64,512]{2,1,0:T(8,128)(2,1)S(1)} %convolve_6.1.earlier_ref), channel_id=1, source_target_pairs={{0,6},{1,7},{2,4},{3,5},{4,2},{5,3},{6,0},{7,1},{8,14},{9,15},{10,... | collective-permute-start | bytes 786440 | tf_op jit(solution)/shard_map/ppermute | solution.py:481
  59.3 22.9 %collective-permute-start.4 = (bf16[4,64,512]{2,1,0:T(8,128)(2,1)S(1)}, bf16[4,64,512]{2,1,0:T(8,128)(2,1)S(1)}, u32[]{:S(2)}, u32[]{:S(2)}) collective-permute-start(bf16[4,64,512]{2,1,0:T(8,128)(2,1)S(1)} %convolve_7.1.earlier_ref), channel_id=1, source_target_pairs={{0,7},{1,6},{2,5},{3,4},{4,3},{5,2},{6,1},{7,0},{8,15},{9,14},{10,... | collective-permute-start | bytes 786440 | tf_op jit(solution)/shard_map/ppermute | solution.py:481

commit v2 on v1

v2 whole, which is shorter than its diff:
```python
import functools

import jax
import jax.numpy as jnp
from jax import lax
from jax.experimental import pallas as pl
from jax.experimental.pallas import tpu as pltpu
from jax.sharding import PartitionSpec as P

C = 64
BS = 8
ROWS = BS * BS
LANES = BS * C
WORD_BITS = 21
GROUP = 4
K_BAND = (GROUP + 2) * C
N_BAND = GROUP * C
EXT = (BS + 2) * C
SHELL = (2 * BS, LANES + 6 * 128)
VMEM_LIMIT = 16 * 1024 * 1024
FIRST_LIMIT = 56 * 1024 * 1024

LITTLE = pl.CostEstimate(flops=1, bytes_accessed=1, transcendentals=0)

ANY = pl.BlockSpec(memory_space=pl.ANY)
HBM = pl.BlockSpec(memory_space=pltpu.HBM)
SMEM = pl.BlockSpec(memory_space=pltpu.SMEM)
VMEM = pl.BlockSpec(memory_space=pltpu.VMEM)


def params():
    return pltpu.CompilerParams(vmem_limit_bytes=VMEM_LIMIT)


def voxel_ids(x):
    rows = lax.broadcasted_iota(jnp.int32, (BS, LANES), 0)
    lanes = lax.broadcasted_iota(jnp.int32, (BS, LANES), 1)
    return x * ROWS + rows * BS + lanes // C


def shift_amounts(x):
    v = voxel_ids(x)
    first = (x * ROWS) // WORD_BITS
    last = (x * ROWS + ROWS - 1) // WORD_BITS
    amounts = v - first * WORD_BITS
    for k in range(first + 1, last + 1):
        amounts = jnp.where(v >= k * WORD_BITS, v - k * WORD_BITS, amounts)
    return amounts


def plane_bits(occ_ref, slot, x, shifts):
    v = voxel_ids(x)
    first = (x * ROWS) // WORD_BITS
    last = (x * ROWS + ROWS - 1) // WORD_BITS
    words = jnp.full((BS, LANES), occ_ref[first, 0, slot], jnp.int32)
    for k in range(first + 1, last + 1):
        words = jnp.where(v >= k * WORD_BITS, occ_ref[k, 0, slot], words)
    return lax.shift_right_logical(words, shifts) & 1


def masked_planes(occ_ref, slot, shift_ref, source):
    planes = []
    for i in range(BS // 2):
        values = source[pl.ds(2 * BS * i, 2 * BS), :].astype(jnp.float32)
        for half in range(2):
            x = 2 * i + half
            bits = plane_bits(occ_ref, slot, x, shift_ref[x])
            planes.append(jnp.where(bits > 0, values[half * BS : half * BS + BS], 0.0))
    return planes


def store_pair(ref, lanes, first, second):
    ref[:, lanes] = jnp.concatenate([first, second], axis=0).astype(jnp.bfloat16)


def store_block(ref, planes):
    for i in range(BS // 2):
        rows = pl.ds(2 * BS * i, 2 * BS)
        ref[rows, :] = jnp.concatenate(planes[2 * i : 2 * i + 2], axis=0).astype(jnp.bfloat16)


def columns_of(plane):
    return [plane[:, 128 * i : 128 * i + 128] for i in range(LANES // 128)]


def tile_ids():
    rows = lax.broadcasted_iota(jnp.int32, (BS, 128), 0)
    lanes = lax.broadcasted_iota(jnp.int32, (BS, 128), 1)
    return rows, lanes


def pack_shell(ref, planes):
    rows, lanes = tile_ids()
    store_pair(ref, pl.ds(0, LANES), planes[0], planes[BS - 1])
    edges, ends = [], []
    for x in range(1, BS - 1):
        columns = columns_of(planes[x])
        edges.append(jnp.where(lanes < C, columns[0], columns[-1]))
        end = columns[0]
        for i, column in enumerate(columns):
            if i:
                end = jnp.where(rows == i, pltpu.roll(column, i, 0), end)
            end = jnp.where(rows == 4 + i, pltpu.roll(column, (i + 5) % BS, 0), end)
        ends.append(end)
    for k in range(3):
        store_pair(ref, pl.ds(LANES + 128 * k, 128), edges[2 * k], edges[2 * k + 1])
        store_pair(ref, pl.ds(LANES + 128 * (3 + k), 128), ends[2 * k], ends[2 * k + 1])


def unpack_shell(ref, packed):
    rows, _ = tile_ids()
    outer = packed[:, pl.ds(0, LANES)].astype(jnp.float32)
    planes = [None] * BS
    planes[0], planes[BS - 1] = outer[:BS], outer[BS:]
    for k in range(3):
        edges = packed[:, pl.ds(LANES + 128 * k, 128)].astype(jnp.float32)
        ends = packed[:, pl.ds(LANES + 128 * (3 + k), 128)].astype(jnp.float32)
        for half in range(2):
            cut = slice(half * BS, half * BS + BS)
            edge, end = edges[cut], ends[cut]
            columns = []
            for i in range(4):
                first = pltpu.roll(end, (BS - i) % BS, 0) if i else end
                last = pltpu.roll(end, (3 - i) % BS, 0) if i != 3 else end
                columns.append(jnp.where(rows == 0, first, jnp.where(rows == BS - 1, last, edge)))
            planes[2 * k + 1 + half] = jnp.concatenate(columns, axis=1)
    store_block(ref, planes)


def upper_first(axis):
    return lax.axis_index(axis) % 2 == 0


def partner_offset(axis, width):
    return jnp.where(upper_first(axis), width, 0)


def outgoing_kernel(lists_ref, words_ref, feat_ref, *refs, axis):
    partner_ref, other_ref, held, shift_ref, lists, words, list_sems, sems = refs[-8:]
    slots = feat_ref.shape[0]
    width = partner_ref.shape[0]
    lists_in = pltpu.make_async_copy(lists_ref, lists, list_sems.at[0])
    words_in = pltpu.make_async_copy(words_ref, words, list_sems.at[1])
    lists_in.start()
    words_in.start()
    lists_in.wait()
    offset = partner_offset(axis, width)
    jobs = []
    for target, start in ((partner_ref, offset), (other_ref, width - offset)):
        for t in range(width):
            name = lists[0, 0, start + t]
            k = len(jobs)
            copy_in = pltpu.make_async_copy(feat_ref.at[jnp.minimum(name, slots - 1)], held.at[k], sems.at[k])
            copy_in.start()
            jobs.append((copy_in, name, target.at[t]))
    for x in range(BS):
        shift_ref[x] = shift_amounts(x)
    words_in.wait()
    for k, (copy_in, name, target) in enumerate(jobs):
        copy_in.wait()

        @pl.when(name < slots)
        def _():
            pack_shell(target, masked_planes(words, name, shift_ref, held.at[k]))


def masked_outgoing(lists, occupancy, features, axis, after=()):
    count = lists.shape[-1]
    half = jax.ShapeDtypeStruct((count // 2,) + SHELL, jnp.bfloat16)
    return pl.pallas_call(
        functools.partial(outgoing_kernel, axis=axis),
        out_shape=(half, half),
        in_specs=[HBM, HBM, HBM] + [ANY] * len(after),
        out_specs=(VMEM, VMEM),
        scratch_shapes=[
            pltpu.VMEM((count, ROWS, LANES), jnp.bfloat16),
            pltpu.VMEM((BS, BS, LANES), jnp.int32),
            pltpu.SMEM(lists.shape, jnp.int32),
            pltpu.SMEM(occupancy.shape, jnp.int32),
            pltpu.SemaphoreType.DMA((2,)),
            pltpu.SemaphoreType.DMA((count,)),
        ],
        compiler_params=pltpu.CompilerParams(vmem_limit_bytes=FIRST_LIMIT),
        cost_estimate=pl.CostEstimate(flops=2000000, bytes_accessed=2 * count * ROWS * LANES * 2, transcendentals=0),
        name="mask_outgoing_" + axis,
    )(lists, occupancy, features, *after)


def unpack_neighbors(pool_ref, start, axis, partner_ref, other_ref):
    width = partner_ref.shape[0]
    offset = partner_offset(axis, width)
    for t in range(width):
        unpack_shell(pool_ref.at[start + offset + t], partner_ref.at[t])
        unpack_shell(pool_ref.at[start + width - offset + t], other_ref.at[t])


def mask_all_kernel(occ_ref, feat_ref, partner_ref, other_ref, earlier_ref, pool_ref, shift_ref):
    slots = feat_ref.shape[0]
    for x in range(BS):
        shift_ref[x] = shift_amounts(x)
    pool_ref[pool_ref.shape[0] - 1] = jnp.zeros((ROWS, LANES), jnp.bfloat16)

    def body(t, carry):
        store_block(pool_ref.at[t], masked_planes(occ_ref, t, shift_ref, feat_ref.at[t]))
        return carry

    lax.fori_loop(0, slots, body, 0)
    unpack_neighbors(pool_ref, slots, "gy", partner_ref, other_ref)


def masked_all(occupancy, features, partner, other, pool_blocks, earlier):
    slots = features.shape[0]
    return pl.pallas_call(
        mask_all_kernel,
        out_shape=jax.ShapeDtypeStruct((pool_blocks, ROWS, LANES), jnp.bfloat16),
        in_specs=[SMEM, VMEM, VMEM, VMEM, ANY],
        out_specs=VMEM,
        scratch_shapes=[pltpu.VMEM((BS, BS, LANES), jnp.int32)],
        compiler_params=params(),
        cost_estimate=pl.CostEstimate(flops=8000000, bytes_accessed=3 * slots * ROWS * LANES * 2, transcendentals=0),
        name="mask_held",
    )(occupancy, features, partner, other, earlier)


def bands_kernel(weights_ref, earlier_ref, out_ref):
    zeros = jnp.zeros((C, C), jnp.float32)
    for pair in range(9):
        taps = [weights_ref[3 * pair + c].astype(jnp.float32) for c in range(3)]
        for z_in in range(GROUP + 2):
            row = [taps[z_in - z_out] if 0 <= z_in - z_out <= 2 else zeros for z_out in range(GROUP)]
            out_ref[pair, pl.ds(z_in * C, C), :] = jnp.concatenate(row, axis=1).astype(jnp.bfloat16)


def banded(weights, earlier):
    return pl.pallas_call(
        bands_kernel,
        out_shape=jax.ShapeDtypeStruct((9, K_BAND, N_BAND), jnp.bfloat16),
        in_specs=[VMEM, ANY],
        out_specs=VMEM,
        compiler_params=params(),
        cost_estimate=pl.CostEstimate(flops=100000, bytes_accessed=4000000, transcendentals=0),
        name="band_weights",
    )(weights, earlier)


def relay_kernel(relays_ref, partner_ref, other_ref, own_partner, own_other, out_partner, out_other, sems, *, slots):
    width = partner_ref.shape[0]
    offset = partner_offset("gx", width)

    def each(act):
        for part, (start, out) in enumerate(((offset, out_partner), (width - offset, out_other))):
            for t in range(width):
                index = relays_ref[0, 0, start + t] - slots
                from_partner = (index >= width) == upper_first("gy")
                place = index % width
                sem = sems.at[part * width + t]

                @pl.when((index >= 0) & from_partner)
                def _():
                    act(pltpu.make_async_copy(partner_ref.at[place], out.at[t], sem))

                @pl.when((index >= 0) & jnp.logical_not(from_partner))
                def _():
                    act(pltpu.make_async_copy(other_ref.at[place], out.at[t], sem))

    each(lambda copy: copy.start())
    each(lambda copy: copy.wait())


def relayed(face_relays, partner, other, own_partner, own_other, slots):
    half = jax.ShapeDtypeStruct(partner.shape, jnp.bfloat16)
    count = face_relays.shape[-1]
    return pl.pallas_call(
        functools.partial(relay_kernel, slots=slots),
        out_shape=(half, half),
        in_specs=[SMEM, ANY, ANY, ANY, ANY],
        out_specs=(ANY, ANY),
        scratch_shapes=[pltpu.SemaphoreType.DMA((count,))],
        input_output_aliases={3: 0, 4: 1},
        compiler_params=params(),
        cost_estimate=pl.CostEstimate(flops=0, bytes_accessed=2 * count * SHELL[0] * SHELL[1] * 2, transcendentals=0),
        name="gather_relays",
    )(face_relays, partner, other, own_partner, own_other)


def extended_plane(blocks, lane_low):
    below, own, above = blocks
    columns = [below] + [own[:, 128 * i : 128 * i + 128] for i in range(4)] + [above]
    turned = [pltpu.roll(column, C, 1) for column in columns]
    return [jnp.where(lane_low, turned[i], turned[i + 1]) for i in range(5)]


def conv_kernel(sent_ref, table_ref, bias_ref, bands_ref, pool_ref, *refs, jobs, start, waits):
    refs = list(refs)
    shift_ref, tiles = refs.pop(), refs.pop()
    del refs[:waits]
    if start is None:
        pool = pool_ref
    else:
        pool = refs.pop()
        unpack_neighbors(pool, start, "gx", refs.pop(0), refs.pop(0))
    (out_ref,) = refs
    items = len(jobs)
    pairs = (items + 1) // 2
    for x in range(BS):
        shift_ref[x] = shift_amounts(x)
    me = lax.axis_index("gy")
    offsets = table_ref.shape[0] - 27
    slots = [jnp.maximum(sent_ref[item, me ^ distance], 0) for distance, item in jobs]
    slots = slots + slots[-1:] * (2 * pairs - items)

    row_ids = lax.broadcasted_iota(jnp.int32, (BS, 128), 0)
    lane_low = lax.broadcasted_iota(jnp.int32, (2 * BS, 128), 1) < C
    is_last = row_ids == BS - 1
    is_first = row_ids == 0

    def row_pair(slot, depth_x, depth_y, i):
        row = offsets + 9 * depth_x + 3 * depth_y
        rows = pl.ds(2 * BS * i, 2 * BS)
        below = pool[table_ref[row, 0, slot], rows, pl.ds(LANES - 128, 128)]
        own = pool[table_ref[row + 1, 0, slot], rows, :]
        above = pool[table_ref[row + 2, 0, slot], rows, pl.ds(0, 128)]
        return extended_plane([v.astype(jnp.float32) for v in (below, own, above)], lane_low)

    def build(pair, both):
        for depth_x, i in ((0, 3), (1, 0), (1, 1), (1, 2), (1, 3), (2, 0)):
            rows = [[row_pair(slot, depth_x, depth_y, i) for depth_y in range(3)] for slot in both]
            if depth_x == 0:
                planes = ((1, 0),)
            elif depth_x == 2:
                planes = ((0, BS + 1),)
            else:
                planes = ((0, 2 * i + 1), (1, 2 * i + 2))
            for half, plane in planes:
                cut = slice(half * BS, half * BS + BS)
                for column in range(5):
                    lanes = pl.ds(128 * column, 128)
                    shifted = ([], [], [])
                    for k in range(2):
                        before, own, after = (rows[k][depth_y][column][cut] for depth_y in range(3))
                        shifted[0].append(pltpu.roll(jnp.where(is_last, before, own), 1, 0))
                        shifted[1].append(own)
                        shifted[2].append(pltpu.roll(jnp.where(is_first, after, own), BS - 1, 0))
                    for depth_y in range(3):
                        tiles[depth_y, plane, pair, :, lanes] = jnp.concatenate(shifted[depth_y], axis=0).astype(
                            jnp.bfloat16
                        )

    for pair in range(pairs):
        build(pair, slots[2 * pair : 2 * pair + 2])

    bias = bias_ref[...]
    for group in range(BS // GROUP):
        window = pl.ds(group * N_BAND, K_BAND)
        total = None
        for depth_x in range(3):
            for depth_y in range(3):
                left = tiles[depth_y, pl.ds(depth_x, BS), :, :, window].reshape(BS * pairs * 2 * BS, K_BAND)
                term = jnp.dot(left, bands_ref[3 * depth_x + depth_y], preferred_element_type=jnp.float32)
                total = term if total is None else total + term
        total = (total + bias).reshape(BS, pairs * 2, BS, N_BAND)
        for item in range(items):
            slot = slots[item]
            for i in range(BS // 2):
                parts = []
                for x in (2 * i, 2 * i + 1):
                    bits = plane_bits(table_ref, slot, x, shift_ref[x])[:, group * N_BAND : group * N_BAND + N_BAND]
                    parts.append(jnp.where(bits > 0, total[x, item], 0.0))
                out_ref[item, pl.ds(2 * BS * i, 2 * BS), pl.ds(group * N_BAND, N_BAND)] = jnp.concatenate(
                    parts, axis=0
                ).astype(jnp.bfloat16)


def convolved(jobs, tables, bias, bands, pool, after, shells=(), start=None):
    pairs = (len(jobs) + 1) // 2
    out_shape = [jax.ShapeDtypeStruct((len(jobs), ROWS, LANES), jnp.bfloat16)]
    if shells:
        out_shape.append(jax.ShapeDtypeStruct(pool.shape, pool.dtype))
    return pl.pallas_call(
        functools.partial(conv_kernel, jobs=jobs, start=start, waits=len(after)),
        out_shape=out_shape,
        in_specs=[SMEM, SMEM, VMEM, VMEM, VMEM] + [ANY] * len(after) + [VMEM] * len(shells),
        out_specs=[VMEM] * len(out_shape),
        scratch_shapes=[
            pltpu.VMEM((3, BS + 2, pairs, 2 * BS, EXT), jnp.bfloat16),
            pltpu.VMEM((BS, BS, LANES), jnp.int32),
        ],
        input_output_aliases={4: 1} if shells else {},
        compiler_params=params(),
        cost_estimate=LITTLE,
        name="convolve_%d" % jobs[0][0],
    )(*tables, bias, bands, pool, *after, *shells)


def place_kernel(order_ref, *refs, distances):
    out_ref, sems = refs[-2:]
    names = [order_ref[r] for r in range(out_ref.shape[0])]

    def each(act):
        for distance, source in zip(distances, refs):
            items = source.shape[0]
            first = (lax.axis_index("gy") ^ distance) * items
            for r, name in enumerate(names):

                @pl.when((name >= first) & (name < first + items))
                def _():
                    act(pltpu.make_async_copy(source.at[name - first], out_ref.at[r], sems.at[r]))

    each(lambda copy: copy.start())
    each(lambda copy: copy.wait())


def placed(distances, receive_order, arrived, output):
    count = receive_order.shape[0]
    filled = () if output is None else (output,)
    return pl.pallas_call(
        functools.partial(place_kernel, distances=distances),
        out_shape=jax.ShapeDtypeStruct((count, ROWS, LANES), jnp.bfloat16),
        in_specs=[SMEM] + [ANY] * (len(distances) + len(filled)),
        out_specs=ANY,
        scratch_shapes=[pltpu.SemaphoreType.DMA((count,))],
        input_output_aliases={1 + len(distances): 0} if filled else {},
        compiler_params=params(),
        cost_estimate=LITTLE,
        name="place_%d" % distances[0],
    )(receive_order, *[arrived[m] for m in distances], *filled)


def exchanged(for_partner, for_other, axis):
    count = lax.axis_size(axis)
    others = [(i, i + 1) for i in range(1, count - 1, 2)]
    from_other = lax.ppermute(for_other, axis, others + [(j, i) for i, j in others])
    from_partner = lax.ppermute(for_partner, axis, [(i, i ^ 1) for i in range(count)])
    return from_partner, from_other


def on_device(
    features,
    occupancy,
    neighbors,
    face_lists,
    face_relays,
    send_slots,
    receive_order,
    weights,
    channel_bias,
):
    slots = features.shape[2]
    blocks = features.reshape(slots, ROWS, LANES)
    words = jnp.transpose(occupancy[0], (2, 0, 1))
    peers = send_slots.shape[2]
    faces = face_lists.shape[-1]
    rules = jnp.concatenate([words, jnp.transpose(neighbors[0], (2, 0, 1))], axis=0)
    tables = (jnp.transpose(send_slots[0, 0]), rules)
    bias = jnp.tile(channel_bias, GROUP).reshape(1, N_BAND)

    for_partner, for_other = masked_outgoing(face_lists, words, blocks, "gy")
    own_partner, own_other = masked_outgoing(face_relays, words, blocks, "gx", (for_partner,))
    y_partner, y_other = exchanged(for_partner, for_other, "gy")
    relay_partner, relay_other = relayed(face_relays, y_partner, y_other, own_partner, own_other, slots)
    x_partner, x_other = exchanged(relay_partner, relay_other, "gx")
    pool = masked_all(words, blocks, y_partner, y_other, slots + 2 * faces + 1, relay_partner)
    bands = banded(weights, relay_partner)

    far, near = list(range(peers // 2, peers)), list(reversed(range(1, peers // 2)))
    order = far + near + [0]
    arrived, shells, last = {}, (x_partner, x_other), ()
    for i, m in enumerate(order):
        first = i - (len(order) - 2)
        after = last + ((arrived[order[first]],) if 0 <= first < i else ())
        jobs = [(m, item) for item in range(send_slots.shape[3])]
        made = convolved(jobs, tables, bias, bands, pool, after, shells, slots + faces if shells else None)
        last = (made[0],)
        if shells:
            pool, shells = made[1], ()
        arrived[m] = lax.ppermute(made[0], "gy", [(d, d ^ m) for d in range(peers)]) if m else made[0]
    output = placed((0,) + tuple(far[:2]), receive_order[0, 0], arrived, None)
    if far[2:-1]:
        output = placed(tuple(far[2:-1]), receive_order[0, 0], arrived, output)
    output = placed(tuple(m for m in far[2:][-1:] + near), receive_order[0, 0], arrived, output)
    return output.reshape(1, 1, output.shape[0], BS, BS, LANES)


def solution(mesh):
    in_specs = (
        P("gx", "gy", None, None, None, None),
        P("gx", "gy", None, None),
        P("gx", "gy", None, None),
        P("gx", "gy", None),
        P("gx", "gy", None),
        P("gx", "gy", None, None),
        P("gx", "gy", None),
        P(),
        P(),
    )
    out_specs = P("gx", "gy", None, None, None, None)
    return jax.shard_map(
        on_device, mesh=mesh, in_specs=in_specs, out_specs=out_specs, check_vma=False
    )
```

time: 84.7 us -> 78.5 us (0.927)
  Pallas kernels: 45.5 us -> 36.3 us
  waiting for transfers between devices: 13.5 us -> 21.1 us
  starting transfers between devices: 22.3 us -> 19.7 us
  local copies, waits for them, and re-layouts: 2.06 us -> 0.12 us
    ppermute x11, waiting for transfers between devices: 13.5 us -> 21.1 us  [the longest x7 16.3 us: on_device(): lax.ppermute(made[0], 'gy', [(d, d ^ m) for d in range(peers)])]
    pallas_call x8 -> x3, Pallas kernels: 11.2 us -> 4.4 us  [placed(): pl.pallas_call(functools.partial(place_kernel, distances=distances), out_...]
    ppermute x11, starting transfers between devices: 22.3 us -> 19.7 us  [the longest x7 10.5 us: on_device(): lax.ppermute(made[0], 'gy', [(d, d ^ m) for d in range(peers)])]
    pallas_call x13 -> x12, Pallas kernels: 34 us -> 31.7 us  [the longest x8 21.7 us: convolved(): pl.pallas_call(functools.partial(conv_kernel, jobs=jobs, start=start, wai...]
    unnamed x22 -> x16, local copies, waits for them, and re-layouts: 1.97 us -> 0.04 us
  transfers between devices with their start and end apart: 11 -> 11, of which waited for: 3 -> 4; matrix products, arithmetic and copies ran while one was open for 0% -> 0% of each run, Pallas kernels for 38% -> 36%
where the time goes in v2:
time: 78.5 us; the launch traced here: 77.8 us
  Pallas kernels  36.3 us (46%)
  waiting for transfers between devices  21.1 us (27%)
  starting transfers between devices  19.7 us (25%)
    pallas_call x8, Pallas kernels, convolved(): pl.pallas_call(functools.partial(conv_kernel, jobs=jobs, start=start, wai...  21.7 us
    ppermute x7, waiting for transfers between devices, on_device(): lax.ppermute(made[0], 'gy', [(d, d ^ m) for d in range(peers)])  16.3 us
    ppermute x7, starting transfers between devices, on_device(): lax.ppermute(made[0], 'gy', [(d, d ^ m) for d in range(peers)])  10.5 us
    pallas_call x2, Pallas kernels, masked_outgoing(): pl.pallas_call(functools.partial(outgoing_kernel, axis=axis), out_shape=(...  5.77 us
    ppermute x2, starting transfers between devices, exchanged(): lax.ppermute(for_other, axis, others + [(j, i) for i, j in others])  5.4 us
    ppermute x2, waiting for transfers between devices, exchanged(): lax.ppermute(for_partner, axis, [(i, i ^ 1) for i in range(count)])  4.53 us
    pallas_call x3, Pallas kernels, placed(): pl.pallas_call(functools.partial(place_kernel, distances=distances), out_...  4.4 us
    ppermute x2, starting transfers between devices, exchanged(): lax.ppermute(for_partner, axis, [(i, i ^ 1) for i in range(count)])  3.81 us
  transfers between devices with their start and end apart: 11, of which 4 were waited for; matrix products, arithmetic and copies ran while one was open for 0% of the time, Pallas kernels for 36%

profile of v2, /device:TPU:1, one launch (start us, length us, event | category | flops | bytes accessed | tf_op | source)
XLA Modules:
  0.0 77.8 jit_solution(4397047160487279552)
XLA Ops:
  0.0 0.0 copy-start.6
  0.0 0.0 copy-start.1
  0.0 3.0 %mask_outgoing_gy.1 = (bf16[4,16,1280]{2,1,0:T(8,128)(2,1)}, bf16[4,16,1280]{2,1,0:T(8,128)(2,1)}) custom-call(s32[1,1,8]{2,1,0:T(1,128)} %lists_ref.2, s32[25,1,32]{2,1,0:T(1,128)} %bitcast.15, bf16[32,64,512]{2,1,0:T(8,128)(2,1)} %bitcast.12), custom_call_target="tpu_custom_call" | custom-call | flops 2000000 | bytes 1048576 | tf_op jit(solution)/shard_map/mask_outgoing_gy/pallas_call | solution.py:170
  3.0 0.0 copy-start
  3.1 4.7 %collective-permute-start.1 = (bf16[4,16,1280]{2,1,0:T(8,128)(2,1)}, bf16[4,16,1280]{2,1,0:T(8,128)(2,1)S(1)}, u32[]{:S(2)}, u32[]{:S(2)}) collective-permute-start(bf16[4,16,1280]{2,1,0:T(8,128)(2,1)} %get-tuple-element.14), channel_id=1, source_target_pairs={{1,2},{3,4},{5,6},{2,1},{4,3},{6,5},{9,10},{11,12},{13,14},{10,9},... | collective-permute-start | bytes 491528 | tf_op jit(solution)/shard_map/ppermute | solution.py:432
  7.8 0.1 collective-permute-start
  7.9 2.8 %mask_outgoing_gx.1 = (bf16[4,16,1280]{2,1,0:T(8,128)(2,1)}, bf16[4,16,1280]{2,1,0:T(8,128)(2,1)}) custom-call(s32[1,1,8]{2,1,0:T(1,128)} %relays_ref.1, s32[25,1,32]{2,1,0:T(1,128)} %bitcast.16, bf16[32,64,512]{2,1,0:T(8,128)(2,1)} %bitcast.13, bf16[4,16,1280]{2,1,0:T(8,128)(2,1)} %get-tuple-element.13.refs_0_), custom_call_target="tpu_custom_call" | custom-call | flops 2000000 | bytes 1048576 | tf_op jit(solution)/shard_map/mask_outgoing_gx/pallas_call | solution.py:170
  10.6 0.4 collective-permute-done.1.other_ref
  11.0 0.0 collective-permute-done.partner_ref
  11.0 0.0 copy-done.5
  11.0 1.3 %gather_relays.1 = (bf16[4,16,1280]{2,1,0:T(8,128)(2,1)}, bf16[4,16,1280]{2,1,0:T(8,128)(2,1)}) custom-call(s32[1,1,8]{2,1,0:T(1,128)S(1)} %copy-done.5, bf16[4,16,1280]{2,1,0:T(8,128)(2,1)S(1)} %collective-permute-done.partner_ref, bf16[4,16,1280]{2,1,0:T(8,128)(2,1)S(1)} %collective-permute-done.1.other_ref, ...), custom_call_target="tpu_custom_call", output_to_operand_aliasing={{0}: (3, {}), {1}: (4, {})} | custom-call | bytes 655360 | tf_op jit(solution)/shard_map/gather_relays/pallas_call | solution.py:273
  12.3 0.7 collective-permute-start.3
  13.0 3.7 %collective-permute-start.2 = (bf16[4,16,1280]{2,1,0:T(8,128)(2,1)}, bf16[4,16,1280]{2,1,0:T(8,128)(2,1)S(1)}, u32[]{:S(2)}, u32[]{:S(2)}) collective-permute-start(bf16[4,16,1280]{2,1,0:T(8,128)(2,1)} %get-tuple-element.17.earlier_ref), channel_id=1, source_target_pairs={{0,8},{8,0},{16,24},{24,16},{1,9},{9,1},{17,25},{25,17},{2,10},{10... | collective-permute-start | bytes 491528 | tf_op jit(solution)/shard_map/ppermute | solution.py:433
  16.7 0.1 reshape_tile.3.bias_ref
  16.9 0.0 copy-done.1
  16.9 0.2 band_weights.1.bands_ref
  17.1 0.0 copy-start.3
  17.1 3.0 %mask_held.1.pool_ref = bf16[49,64,512]{2,1,0:T(8,128)(2,1)S(1)} custom-call(s32[25,1,32]{2,1,0:T(1,128)S(1)} %bitcast.18, bf16[32,64,512]{2,1,0:T(8,128)(2,1)S(1)} %bitcast.14, bf16[4,16,1280]{2,1,0:T(8,128)(2,1)S(1)} %collective-permute-done.partner_ref, bf16[4,16,1280]{2,1,0:T(8,128)(2,1)S(1)} %collective-permute-done.1.other_ref, ...), custom_call_target="tpu_custom_call" | custom-call | flops 8000000 | bytes 6291456 | tf_op jit(solution)/shard_map/mask_held/pallas_call | solution.py:213
  20.1 0.0 collective-permute-done.3.refs_1_
  20.1 4.5 %collective-permute-done.2.refs_0_ = bf16[4,16,1280]{2,1,0:T(8,128)(2,1)S(1)} collective-permute-done((bf16[4,16,1280]{2,1,0:T(8,128)(2,1)}, bf16[4,16,1280]{2,1,0:T(8,128)(2,1)S(1)}, u32[]{:S(2)}, u32[]{:S(2)}) %collective-permute-start.2) | collective-permute-done | bytes 163872 | tf_op jit(solution)/shard_map/ppermute | solution.py:433
  24.7 0.0 copy-done.3
  24.7 2.8 %convolve_4.1 = (bf16[4,64,512]{2,1,0:T(8,128)(2,1)S(1)}, bf16[49,64,512]{2,1,0:T(8,128)(2,1)S(1)}) custom-call(s32[4,8]{1,0:T(4,128)S(1)} %bitcast.19, s32[52,1,32]{2,1,0:T(1,128)S(1)} %pad_add_fusion.table_ref, f32[1,256]{1,0:T(1,128)S(1)} %reshape_tile.3.bias_ref, ...), custom_call_target="tpu_custom_call", output_to_operand_aliasing={{1}: (4, {})} | custom-call | flops 1 | bytes 1 | tf_op jit(solution)/shard_map/convolve_4/pallas_call | solution.py:379
  27.5 2.1 %collective-permute-start.7 = (bf16[4,64,512]{2,1,0:T(8,128)(2,1)S(1)}, bf16[4,64,512]{2,1,0:T(8,128)(2,1)S(1)}, u32[]{:S(2)}, u32[]{:S(2)}) collective-permute-start(bf16[4,64,512]{2,1,0:T(8,128)(2,1)S(1)} %get-tuple-element.20.refs_0_), channel_id=1, source_target_pairs={{0,4},{1,5},{2,6},{3,7},{4,0},{5,1},{6,2},{7,3},{8,12},{9,13},{10,... | collective-permute-start | bytes 786440 | tf_op jit(solution)/shard_map/ppermute | solution.py:476
  29.6 2.7 %convolve_5.1.refs_0_ = bf16[4,64,512]{2,1,0:T(8,128)(2,1)S(1)} custom-call(s32[4,8]{1,0:T(4,128)S(1)} %bitcast.20, s32[52,1,32]{2,1,0:T(1,128)S(1)} %pad_add_fusion.table_ref, f32[1,256]{1,0:T(1,128)S(1)} %reshape_tile.3.bias_ref, bf16[9,384,256]{2,1,0:T(8,128)(2,1)S(1)} %band_weights.1.bands_ref, bf16[49,64,512]{2,1,0:T(8,128)(2,1)S(1)} %get-tuple-element.19.pool_ref, ...), custom_call_target="tpu_custom_call" | custom-call | flops 1 | bytes 1 | tf_op jit(solution)/shard_map/convolve_5/pallas_call | solution.py:379
  32.3 1.4 %collective-permute-start.10 = (bf16[4,64,512]{2,1,0:T(8,128)(2,1)S(1)}, bf16[4,64,512]{2,1,0:T(8,128)(2,1)S(1)}, u32[]{:S(2)}, u32[]{:S(2)}) collective-permute-start(bf16[4,64,512]{2,1,0:T(8,128)(2,1)S(1)} %convolve_5.1.refs_0_), channel_id=1, source_target_pairs={{0,5},{1,4},{2,7},{3,6},{4,1},{5,0},{6,3},{7,2},{8,13},{9,12},{10,... | collective-permute-start | bytes 786440 | tf_op jit(solution)/shard_map/ppermute | solution.py:476
  33.7 2.7 %convolve_6.1.refs_0_ = bf16[4,64,512]{2,1,0:T(8,128)(2,1)S(1)} custom-call(s32[4,8]{1,0:T(4,128)S(1)} %bitcast.21, s32[52,1,32]{2,1,0:T(1,128)S(1)} %pad_add_fusion.table_ref, f32[1,256]{1,0:T(1,128)S(1)} %reshape_tile.3.bias_ref, bf16[9,384,256]{2,1,0:T(8,128)(2,1)S(1)} %band_weights.1.bands_ref, bf16[49,64,512]{2,1,0:T(8,128)(2,1)S(1)} %get-tuple-element.19.pool_ref, ...), custom_call_target="tpu_custom_call" | custom-call | flops 1 | bytes 1 | tf_op jit(solution)/shard_map/convolve_6/pallas_call | solution.py:379
  36.4 2.7 %convolve_7.1.refs_0_ = bf16[4,64,512]{2,1,0:T(8,128)(2,1)S(1)} custom-call(s32[4,8]{1,0:T(4,128)S(1)} %bitcast.22, s32[52,1,32]{2,1,0:T(1,128)S(1)} %pad_add_fusion.table_ref, f32[1,256]{1,0:T(1,128)S(1)} %reshape_tile.3.bias_ref, bf16[9,384,256]{2,1,0:T(8,128)(2,1)S(1)} %band_weights.1.bands_ref, bf16[49,64,512]{2,1,0:T(8,128)(2,1)S(1)} %get-tuple-element.19.pool_ref, ...), custom_call_target="tpu_custom_call" | custom-call | flops 1 | bytes 1 | tf_op jit(solution)/shard_map/convolve_7/pallas_call | solution.py:379
  39.1 2.7 %convolve_3.1.refs_0_ = bf16[4,64,512]{2,1,0:T(8,128)(2,1)S(1)} custom-call(s32[4,8]{1,0:T(4,128)S(1)} %bitcast.23, s32[52,1,32]{2,1,0:T(1,128)S(1)} %pad_add_fusion.table_ref, f32[1,256]{1,0:T(1,128)S(1)} %reshape_tile.3.bias_ref, bf16[9,384,256]{2,1,0:T(8,128)(2,1)S(1)} %band_weights.1.bands_ref, bf16[49,64,512]{2,1,0:T(8,128)(2,1)S(1)} %get-tuple-element.19.pool_ref, ...), custom_call_target="tpu_custom_call" | custom-call | flops 1 | bytes 1 | tf_op jit(solution)/shard_map/convolve_3/pallas_call | solution.py:379
  41.8 2.7 %convolve_2.1.refs_0_ = bf16[4,64,512]{2,1,0:T(8,128)(2,1)S(1)} custom-call(s32[4,8]{1,0:T(4,128)S(1)} %bitcast.24, s32[52,1,32]{2,1,0:T(1,128)S(1)} %pad_add_fusion.table_ref, f32[1,256]{1,0:T(1,128)S(1)} %reshape_tile.3.bias_ref, bf16[9,384,256]{2,1,0:T(8,128)(2,1)S(1)} %band_weights.1.bands_ref, bf16[49,64,512]{2,1,0:T(8,128)(2,1)S(1)} %get-tuple-element.19.pool_ref, ...), custom_call_target="tpu_custom_call" | custom-call | flops 1 | bytes 1 | tf_op jit(solution)/shard_map/convolve_2/pallas_call | solution.py:379
  44.5 0.4 collective-permute-start.5
  44.9 2.1 %collective-permute-start.9 = (bf16[4,64,512]{2,1,0:T(8,128)(2,1)S(1)}, bf16[4,64,512]{2,1,0:T(8,128)(2,1)S(1)}, u32[]{:S(2)}, u32[]{:S(2)}) collective-permute-start(bf16[4,64,512]{2,1,0:T(8,128)(2,1)S(1)} %convolve_6.1.refs_0_), channel_id=1, source_target_pairs={{0,6},{1,7},{2,4},{3,5},{4,2},{5,3},{6,0},{7,1},{8,14},{9,15},{10,... | collective-permute-start | bytes 786440 | tf_op jit(solution)/shard_map/ppermute | solution.py:476
  47.0 0.3 collective-permute-start.6
  47.4 0.0 collective-permute-done.7.refs_1_
  47.4 4.1 %collective-permute-start.4 = (bf16[4,64,512]{2,1,0:T(8,128)(2,1)S(1)}, bf16[4,64,512]{2,1,0:T(8,128)(2,1)S(1)}, u32[]{:S(2)}, u32[]{:S(2)}) collective-permute-start(bf16[4,64,512]{2,1,0:T(8,128)(2,1)S(1)} %convolve_7.1.refs_0_), channel_id=1, source_target_pairs={{0,7},{1,6},{2,5},{3,4},{4,3},{5,2},{6,1},{7,0},{8,15},{9,14},{10,... | collective-permute-start | bytes 786440 | tf_op jit(solution)/shard_map/ppermute | solution.py:476
  51.5 2.7 %convolve_1.1.refs_0_ = bf16[4,64,512]{2,1,0:T(8,128)(2,1)S(1)} custom-call(s32[4,8]{1,0:T(4,128)S(1)} %bitcast.25, s32[52,1,32]{2,1,0:T(1,128)S(1)} %pad_add_fusion.table_ref, f32[1,256]{1,0:T(1,128)S(1)} %reshape_tile.3.bias_ref, bf16[9,384,256]{2,1,0:T(8,128)(2,1)S(1)} %band_weights.1.bands_ref, bf16[49,64,512]{2,1,0:T(8,128)(2,1)S(1)} %get-tuple-element.19.pool_ref, ...), custom_call_target="tpu_custom_call" | custom-call | flops 1 | bytes 1 | tf_op jit(solution)/shard_map/convolve_1/pallas_call | solution.py:379
  54.2 0.0 copy-start.4
  54.2 4.9 %collective-permute-done.10.refs_1_.refs_2_ = bf16[4,64,512]{2,1,0:T(8,128)(2,1)S(1)} collective-permute-done((bf16[4,64,512]{2,1,0:T(8,128)(2,1)S(1)}, bf16[4,64,512]{2,1,0:T(8,128)(2,1)S(1)}, u32[]{:S(2)}, u32[]{:S(2)}) %collective-permute-start.10) | collective-permute-done | bytes 262176 | tf_op jit(solution)/shard_map/ppermute | solution.py:476
  59.1 0.0 collective-permute-start.8
  59.1 2.7 %convolve_0.1.refs_0_ = bf16[4,64,512]{2,1,0:T(8,128)(2,1)S(1)} custom-call(s32[4,8]{1,0:T(4,128)S(1)} %bitcast.26, s32[52,1,32]{2,1,0:T(1,128)S(1)} %pad_add_fusion.table_ref, f32[1,256]{1,0:T(1,128)S(1)} %reshape_tile.3.bias_ref, bf16[9,384,256]{2,1,0:T(8,128)(2,1)S(1)} %band_weights.1.bands_ref, bf16[49,64,512]{2,1,0:T(8,128)(2,1)S(1)} %get-tuple-element.19.pool_ref, ...), custom_call_target="tpu_custom_call" | custom-call | flops 1 | bytes 1 | tf_op jit(solution)/shard_map/convolve_0/pallas_call | solution.py:379
  61.8 0.0 copy-done.4
  61.9 1.5 %place_0.1.refs_1_ = bf16[16,64,512]{2,1,0:T(8,128)(2,1)} custom-call(s32[16]{0:T(128)S(1)} %bitcast.27, bf16[4,64,512]{2,1,0:T(8,128)(2,1)S(1)} %convolve_0.1.refs_0_, bf16[4,64,512]{2,1,0:T(8,128)(2,1)S(1)} %collective-permute-done.7.refs_1_, bf16[4,64,512]{2,1,0:T(8,128)(2,1)S(1)} %collective-permute-done.10.refs_1_.refs_2_), custom_call_target="tpu_custom_call" | custom-call | flops 1 | bytes 1 | tf_op jit(solution)/shard_map/place_0/pallas_call | solution.py:416
  63.4 0.0 collective-permute-done.9.refs_0_
  63.4 1.4 %place_6.1.refs_4_ = bf16[16,64,512]{2,1,0:T(8,128)(2,1)} custom-call(s32[16]{0:T(128)S(1)} %bitcast.28, bf16[4,64,512]{2,1,0:T(8,128)(2,1)S(1)} %collective-permute-done.9.refs_0_, bf16[16,64,512]{2,1,0:T(8,128)(2,1)} %place_0.1.refs_1_), custom_call_target="tpu_custom_call", output_to_operand_aliasing={{}: (2, {})} | custom-call | flops 1 | bytes 1 | tf_op jit(solution)/shard_map/place_6/pallas_call | solution.py:416
  64.7 11.3 %collective-permute-done.6.refs_2_ = bf16[4,64,512]{2,1,0:T(8,128)(2,1)S(1)} collective-permute-done((bf16[4,64,512]{2,1,0:T(8,128)(2,1)S(1)}, bf16[4,64,512]{2,1,0:T(8,128)(2,1)S(1)}, u32[]{:S(2)}, u32[]{:S(2)}) %collective-permute-start.6) | collective-permute-done | bytes 262176 | tf_op jit(solution)/shard_map/ppermute | solution.py:476
  76.0 0.0 collective-permute-done.5.refs_1_
  76.0 0.0 collective-permute-done.4.refs_0_
  76.0 0.0 collective-permute-done.8.refs_3_
  76.1 1.5 %place_7.1 = bf16[16,64,512]{2,1,0:T(8,128)(2,1)} custom-call(s32[16]{0:T(128)S(1)} %bitcast.29, bf16[4,64,512]{2,1,0:T(8,128)(2,1)S(1)} %collective-permute-done.4.refs_0_, bf16[4,64,512]{2,1,0:T(8,128)(2,1)S(1)} %collective-permute-done.5.refs_1_, bf16[4,64,512]{2,1,0:T(8,128)(2,1)S(1)} %collective-permute-done.6.refs_2_, ...), custom_call_target="tpu_custom_call", output_to_operand_aliasing={{}: (5, {})} | custom-call | flops 1 | bytes 1 | tf_op jit(solution)/shard_map/place_7/pallas_call | solution.py:416
  (9 shorter events, 0.0 us)
Async XLA Ops:
  0.0 16.8 %copy-start.2 = (s32[1,1,32,25]{2,1,3,0:T(1,128)S(1)}, s32[1,1,32,25]{2,1,3,0:T(1,128)}, u32[]{:S(2)}) copy-start(s32[1,1,32,25]{2,1,3,0:T(1,128)} %param.10) | copy-start | bytes 9604
  0.0 11.0 %copy-start.5 = (s32[1,1,8]{2,1,0:T(1,128)S(1)}, s32[1,1,8]{2,1,0:T(1,128)}, u32[]{:S(2)}) copy-start(s32[1,1,8]{2,1,0:T(1,128)} %relays_ref.1) | copy-start | bytes 100
  0.0 16.7 %copy-start.7 = (f32[64]{0:T(128)S(1)}, f32[64]{0:T(128)}, u32[]{:S(2)}) copy-start(f32[64]{0:T(128)} %param.17) | copy-start | bytes 772
  0.0 16.8 %copy-start.6 = (s32[1,1,32,27]{2,1,3,0:T(1,128)S(1)}, s32[1,1,32,27]{2,1,3,0:T(1,128)}, u32[]{:S(2)}) copy-start(s32[1,1,32,27]{2,1,3,0:T(1,128)} %param.11) | copy-start | bytes 10372
  0.0 16.8 %copy-start.1 = (bf16[27,64,64]{2,1,0:T(8,128)(2,1)S(1)}, bf16[27,64,64]{2,1,0:T(8,128)(2,1)}, u32[]{:S(2)}) copy-start(bf16[27,64,64]{2,1,0:T(8,128)(2,1)} %weights_ref.1) | copy-start | bytes 663556
  3.0 14.1 %copy-start = (bf16[1,1,32,8,8,512]{5,4,3,2,1,0:T(8,128)(2,1)S(1)}, bf16[1,1,32,8,8,512]{5,4,3,2,1,0:T(8,128)(2,1)}, u32[]{:S(2)}) copy-start(bf16[1,1,32,8,8,512]{5,4,3,2,1,0:T(8,128)(2,1)} %param.9) | copy-start | bytes 6291460
  3.1 7.9 %collective-permute-start.1 = (bf16[4,16,1280]{2,1,0:T(8,128)(2,1)}, bf16[4,16,1280]{2,1,0:T(8,128)(2,1)S(1)}, u32[]{:S(2)}, u32[]{:S(2)}) collective-permute-start(bf16[4,16,1280]{2,1,0:T(8,128)(2,1)} %get-tuple-element.14), channel_id=1, source_target_pairs={{1,2},{3,4},{5,6},{2,1},{4,3},{6,5},{9,10},{11,12},{13,14},{10,9},... | collective-permute-start | bytes 491528 | tf_op jit(solution)/shard_map/ppermute | solution.py:432
  7.8 3.2 %collective-permute-start = (bf16[4,16,1280]{2,1,0:T(8,128)(2,1)}, bf16[4,16,1280]{2,1,0:T(8,128)(2,1)S(1)}, u32[]{:S(2)}, u32[]{:S(2)}) collective-permute-start(bf16[4,16,1280]{2,1,0:T(8,128)(2,1)} %get-tuple-element.13.refs_0_), channel_id=1, source_target_pairs={{0,1},{1,0},{2,3},{3,2},{4,5},{5,4},{6,7},{7,6},{8,9},{9,8},{10,11... | collective-permute-start | bytes 491528 | tf_op jit(solution)/shard_map/ppermute | solution.py:433
  12.3 7.8 %collective-permute-start.3 = (bf16[4,16,1280]{2,1,0:T(8,128)(2,1)}, bf16[4,16,1280]{2,1,0:T(8,128)(2,1)S(1)}, u32[]{:S(2)}, u32[]{:S(2)}) collective-permute-start(bf16[4,16,1280]{2,1,0:T(8,128)(2,1)} %get-tuple-element.18), channel_id=1, source_target_pairs={{8,16},{16,8},{9,17},{17,9},{10,18},{18,10},{11,19},{19,11},{12,20... | collective-permute-start | bytes 491528 | tf_op jit(solution)/shard_map/ppermute | solution.py:432
  13.0 11.7 %collective-permute-start.2 = (bf16[4,16,1280]{2,1,0:T(8,128)(2,1)}, bf16[4,16,1280]{2,1,0:T(8,128)(2,1)S(1)}, u32[]{:S(2)}, u32[]{:S(2)}) collective-permute-start(bf16[4,16,1280]{2,1,0:T(8,128)(2,1)} %get-tuple-element.17.earlier_ref), channel_id=1, source_target_pairs={{0,8},{8,0},{16,24},{24,16},{1,9},{9,1},{17,25},{25,17},{2,10},{10... | collective-permute-start | bytes 491528 | tf_op jit(solution)/shard_map/ppermute | solution.py:433
  17.1 7.5 %copy-start.3 = (s32[1,1,8,4]{2,3,1,0:T(4,128)S(1)}, s32[1,1,8,4]{2,3,1,0:T(4,128)}, u32[]{:S(2)}) copy-start(s32[1,1,8,4]{2,3,1,0:T(4,128)} %param.14) | copy-start | bytes 388
  27.5 19.9 %collective-permute-start.7 = (bf16[4,64,512]{2,1,0:T(8,128)(2,1)S(1)}, bf16[4,64,512]{2,1,0:T(8,128)(2,1)S(1)}, u32[]{:S(2)}, u32[]{:S(2)}) collective-permute-start(bf16[4,64,512]{2,1,0:T(8,128)(2,1)S(1)} %get-tuple-element.20.refs_0_), channel_id=1, source_target_pairs={{0,4},{1,5},{2,6},{3,7},{4,0},{5,1},{6,2},{7,3},{8,12},{9,13},{10,... | collective-permute-start | bytes 786440 | tf_op jit(solution)/shard_map/ppermute | solution.py:476
  32.3 26.9 %collective-permute-start.10 = (bf16[4,64,512]{2,1,0:T(8,128)(2,1)S(1)}, bf16[4,64,512]{2,1,0:T(8,128)(2,1)S(1)}, u32[]{:S(2)}, u32[]{:S(2)}) collective-permute-start(bf16[4,64,512]{2,1,0:T(8,128)(2,1)S(1)} %convolve_5.1.refs_0_), channel_id=1, source_target_pairs={{0,5},{1,4},{2,7},{3,6},{4,1},{5,0},{6,3},{7,2},{8,13},{9,12},{10,... | collective-permute-start | bytes 786440 | tf_op jit(solution)/shard_map/ppermute | solution.py:476
  44.5 31.5 %collective-permute-start.5 = (bf16[4,64,512]{2,1,0:T(8,128)(2,1)S(1)}, bf16[4,64,512]{2,1,0:T(8,128)(2,1)S(1)}, u32[]{:S(2)}, u32[]{:S(2)}) collective-permute-start(bf16[4,64,512]{2,1,0:T(8,128)(2,1)S(1)} %convolve_3.1.refs_0_), channel_id=1, source_target_pairs={{0,3},{1,2},{2,1},{3,0},{4,7},{5,6},{6,5},{7,4},{8,11},{9,10},{10,... | collective-permute-start | bytes 786440 | tf_op jit(solution)/shard_map/ppermute | solution.py:476
  44.9 18.4 %collective-permute-start.9 = (bf16[4,64,512]{2,1,0:T(8,128)(2,1)S(1)}, bf16[4,64,512]{2,1,0:T(8,128)(2,1)S(1)}, u32[]{:S(2)}, u32[]{:S(2)}) collective-permute-start(bf16[4,64,512]{2,1,0:T(8,128)(2,1)S(1)} %convolve_6.1.refs_0_), channel_id=1, source_target_pairs={{0,6},{1,7},{2,4},{3,5},{4,2},{5,3},{6,0},{7,1},{8,14},{9,15},{10,... | collective-permute-start | bytes 786440 | tf_op jit(solution)/shard_map/ppermute | solution.py:476
  47.0 29.0 %collective-permute-start.6 = (bf16[4,64,512]{2,1,0:T(8,128)(2,1)S(1)}, bf16[4,64,512]{2,1,0:T(8,128)(2,1)S(1)}, u32[]{:S(2)}, u32[]{:S(2)}) collective-permute-start(bf16[4,64,512]{2,1,0:T(8,128)(2,1)S(1)} %convolve_2.1.refs_0_), channel_id=1, source_target_pairs={{0,2},{1,3},{2,0},{3,1},{4,6},{5,7},{6,4},{7,5},{8,10},{9,11},{10,... | collective-permute-start | bytes 786440 | tf_op jit(solution)/shard_map/ppermute | solution.py:476
  47.4 28.7 %collective-permute-start.4 = (bf16[4,64,512]{2,1,0:T(8,128)(2,1)S(1)}, bf16[4,64,512]{2,1,0:T(8,128)(2,1)S(1)}, u32[]{:S(2)}, u32[]{:S(2)}) collective-permute-start(bf16[4,64,512]{2,1,0:T(8,128)(2,1)S(1)} %convolve_7.1.refs_0_), channel_id=1, source_target_pairs={{0,7},{1,6},{2,5},{3,4},{4,3},{5,2},{6,1},{7,0},{8,15},{9,14},{10,... | collective-permute-start | bytes 786440 | tf_op jit(solution)/shard_map/ppermute | solution.py:476
  54.2 7.7 %copy-start.4 = (s32[1,1,16]{2,1,0:T(1,128)S(1)}, s32[1,1,16]{2,1,0:T(1,128)}, u32[]{:S(2)}) copy-start(s32[1,1,16]{2,1,0:T(1,128)} %param.15) | copy-start | bytes 196
  59.1 16.9 %collective-permute-start.8 = (bf16[4,64,512]{2,1,0:T(8,128)(2,1)S(1)}, bf16[4,64,512]{2,1,0:T(8,128)(2,1)S(1)}, u32[]{:S(2)}, u32[]{:S(2)}) collective-permute-start(bf16[4,64,512]{2,1,0:T(8,128)(2,1)S(1)} %convolve_1.1.refs_0_), channel_id=1, source_target_pairs={{0,1},{1,0},{2,3},{3,2},{4,5},{5,4},{6,7},{7,6},{8,9},{9,8},{10,11... | collective-permute-start | bytes 786440 | tf_op jit(solution)/shard_map/ppermute | solution.py:476

commit v3 on v2

--- a/solution.py
+++ b/solution.py
@@ -290,9 +290,15 @@
     return [jnp.where(lane_low, turned[i], turned[i + 1]) for i in range(5)]
 
 
-def conv_kernel(sent_ref, table_ref, bias_ref, bands_ref, pool_ref, *refs, jobs, start, waits):
+def conv_kernel(sent_in, table_in, bias_ref, bands_ref, pool_ref, *refs, jobs, start, waits):
     refs = list(refs)
-    shift_ref, tiles = refs.pop(), refs.pop()
+    sems, table_ref, sent_ref, shift_ref, tiles = (refs.pop() for _ in range(5))
+    copies = [
+        pltpu.make_async_copy(source, target, sems.at[i])
+        for i, (source, target) in enumerate(((sent_in, sent_ref), (table_in, table_ref)))
+    ]
+    for copy in copies:
+        copy.start()
     del refs[:waits]
     if start is None:
         pool = pool_ref
@@ -304,6 +310,8 @@
     pairs = (items + 1) // 2
     for x in range(BS):
         shift_ref[x] = shift_amounts(x)
+    for copy in copies:
+        copy.wait()
     me = lax.axis_index("gy")
     offsets = table_ref.shape[0] - 27
     slots = [jnp.maximum(sent_ref[item, me ^ distance], 0) for distance, item in jobs]
@@ -352,12 +360,16 @@
     bias = bias_ref[...]
     for group in range(BS // GROUP):
         window = pl.ds(group * N_BAND, K_BAND)
-        total = None
-        for depth_x in range(3):
-            for depth_y in range(3):
-                left = tiles[depth_y, pl.ds(depth_x, BS), :, :, window].reshape(BS * pairs * 2 * BS, K_BAND)
-                term = jnp.dot(left, bands_ref[3 * depth_x + depth_y], preferred_element_type=jnp.float32)
-                total = term if total is None else total + term
+        windows = [
+            tiles[depth_y, pl.ds(depth_x, BS), :, :, window].reshape(BS * pairs * 2 * BS, K_BAND)
+            for depth_x in range(3)
+            for depth_y in range(3)
+        ]
+        total = jnp.dot(
+            jnp.concatenate(windows, axis=1),
+            bands_ref[...].reshape(9 * K_BAND, N_BAND),
+            preferred_element_type=jnp.float32,
+        )
         total = (total + bias).reshape(BS, pairs * 2, BS, N_BAND)
         for item in range(items):
             slot = slots[item]
@@ -379,11 +391,14 @@
     return pl.pallas_call(
         functools.partial(conv_kernel, jobs=jobs, start=start, waits=len(after)),
         out_shape=out_shape,
-        in_specs=[SMEM, SMEM, VMEM, VMEM, VMEM] + [ANY] * len(after) + [VMEM] * len(shells),
+        in_specs=[ANY, ANY, VMEM, VMEM, VMEM] + [ANY] * len(after) + [VMEM] * len(shells),
         out_specs=[VMEM] * len(out_shape),
         scratch_shapes=[
             pltpu.VMEM((3, BS + 2, pairs, 2 * BS, EXT), jnp.bfloat16),
             pltpu.VMEM((BS, BS, LANES), jnp.int32),
+            pltpu.SMEM(tables[0].shape, jnp.int32),
+            pltpu.SMEM(tables[1].shape, jnp.int32),
+            pltpu.SemaphoreType.DMA((2,)),
         ],
         input_output_aliases={4: 1} if shells else {},
         compiler_params=params(),

time: 78.5 us -> 78.1 us (level)
  Pallas kernels: 36.3 us -> 34.5 us
  waiting for transfers between devices: 21.1 us -> 22.4 us
    pallas_call x8, Pallas kernels: 21.7 us -> 19.9 us  [convolved(): pl.pallas_call(functools.partial(conv_kernel, jobs=jobs, start=start, wai...]
    ppermute x7, waiting for transfers between devices: 16.3 us -> 17.4 us  [on_device(): lax.ppermute(made[0], 'gy', [(d, d ^ m) for d in range(peers)])]
  transfers between devices with their start and end apart: 11 -> 11, of which waited for: 4 -> 5; matrix products, arithmetic and copies ran while one was open for 0% -> 0% of each run, Pallas kernels for 36% -> 34%
where the time goes in v3:
time: 78.1 us; the launch traced here: 77.4 us
  Pallas kernels  34.5 us (44%)
  waiting for transfers between devices  22.4 us (29%)
  starting transfers between devices  20 us (26%)
    pallas_call x8, Pallas kernels, convolved(): pl.pallas_call(functools.partial(conv_kernel, jobs=jobs, start=start, wai...  19.9 us
    ppermute x7, waiting for transfers between devices, on_device(): lax.ppermute(made[0], 'gy', [(d, d ^ m) for d in range(peers)])  17.4 us
    ppermute x7, starting transfers between devices, on_device(): lax.ppermute(made[0], 'gy', [(d, d ^ m) for d in range(peers)])  10.8 us
    pallas_call x2, Pallas kernels, masked_outgoing(): pl.pallas_call(functools.partial(outgoing_kernel, axis=axis), out_shape=(...  5.67 us
    ppermute x2, starting transfers between devices, exchanged(): lax.ppermute(for_other, axis, others + [(j, i) for i, j in others])  5.4 us
    ppermute x2, waiting for transfers between devices, exchanged(): lax.ppermute(for_partner, axis, [(i, i ^ 1) for i in range(count)])  4.55 us
    pallas_call x3, Pallas kernels, placed(): pl.pallas_call(functools.partial(place_kernel, distances=distances), out_...  4.39 us
    ppermute x2, starting transfers between devices, exchanged(): lax.ppermute(for_partner, axis, [(i, i ^ 1) for i in range(count)])  3.81 us
  transfers between devices with their start and end apart: 11, of which 5 were waited for; matrix products, arithmetic and copies ran while one was open for 0% of the time, Pallas kernels for 34%

profile of v3, /device:TPU:1, one launch (start us, length us, event | category | flops | bytes accessed | tf_op | source)
XLA Modules:
  0.0 77.4 jit_solution(2294030437865345432)
XLA Ops:
  0.0 0.0 copy-start.6
  0.0 0.0 copy-start.1
  0.0 3.0 %mask_outgoing_gy.1 = (bf16[4,16,1280]{2,1,0:T(8,128)(2,1)}, bf16[4,16,1280]{2,1,0:T(8,128)(2,1)}) custom-call(s32[1,1,8]{2,1,0:T(1,128)} %lists_ref.2, s32[25,1,32]{2,1,0:T(1,128)} %bitcast.15, bf16[32,64,512]{2,1,0:T(8,128)(2,1)} %bitcast.12), custom_call_target="tpu_custom_call" | custom-call | flops 2000000 | bytes 1048576 | tf_op jit(solution)/shard_map/mask_outgoing_gy/pallas_call | solution.py:170
  3.0 0.0 copy-start
  3.1 4.7 %collective-permute-start.1 = (bf16[4,16,1280]{2,1,0:T(8,128)(2,1)}, bf16[4,16,1280]{2,1,0:T(8,128)(2,1)S(1)}, u32[]{:S(2)}, u32[]{:S(2)}) collective-permute-start(bf16[4,16,1280]{2,1,0:T(8,128)(2,1)} %get-tuple-element.14), channel_id=1, source_target_pairs={{1,2},{3,4},{5,6},{2,1},{4,3},{6,5},{9,10},{11,12},{13,14},{10,9},... | collective-permute-start | bytes 491528 | tf_op jit(solution)/shard_map/ppermute | solution.py:447
  7.8 0.1 collective-permute-start
  7.9 2.7 %mask_outgoing_gx.1 = (bf16[4,16,1280]{2,1,0:T(8,128)(2,1)}, bf16[4,16,1280]{2,1,0:T(8,128)(2,1)}) custom-call(s32[1,1,8]{2,1,0:T(1,128)} %relays_ref.1, s32[25,1,32]{2,1,0:T(1,128)} %bitcast.16, bf16[32,64,512]{2,1,0:T(8,128)(2,1)} %bitcast.13, bf16[4,16,1280]{2,1,0:T(8,128)(2,1)} %get-tuple-element.13.refs_0_), custom_call_target="tpu_custom_call" | custom-call | flops 2000000 | bytes 1048576 | tf_op jit(solution)/shard_map/mask_outgoing_gx/pallas_call | solution.py:170
  10.5 0.5 collective-permute-done.1.other_ref
  11.0 0.0 collective-permute-done.partner_ref
  11.0 0.0 copy-done.5
  11.0 1.3 %gather_relays.1 = (bf16[4,16,1280]{2,1,0:T(8,128)(2,1)}, bf16[4,16,1280]{2,1,0:T(8,128)(2,1)}) custom-call(s32[1,1,8]{2,1,0:T(1,128)S(1)} %copy-done.5, bf16[4,16,1280]{2,1,0:T(8,128)(2,1)S(1)} %collective-permute-done.partner_ref, bf16[4,16,1280]{2,1,0:T(8,128)(2,1)S(1)} %collective-permute-done.1.other_ref, ...), custom_call_target="tpu_custom_call", output_to_operand_aliasing={{0}: (3, {}), {1}: (4, {})} | custom-call | bytes 655360 | tf_op jit(solution)/shard_map/gather_relays/pallas_call | solution.py:273
  12.3 0.7 collective-permute-start.3
  13.0 3.7 %collective-permute-start.2 = (bf16[4,16,1280]{2,1,0:T(8,128)(2,1)}, bf16[4,16,1280]{2,1,0:T(8,128)(2,1)S(1)}, u32[]{:S(2)}, u32[]{:S(2)}) collective-permute-start(bf16[4,16,1280]{2,1,0:T(8,128)(2,1)} %get-tuple-element.17.earlier_ref), channel_id=1, source_target_pairs={{0,8},{8,0},{16,24},{24,16},{1,9},{9,1},{17,25},{25,17},{2,10},{10... | collective-permute-start | bytes 491528 | tf_op jit(solution)/shard_map/ppermute | solution.py:448
  16.7 0.1 reshape_tile.3.bias_ref
  16.8 0.0 copy-done.6
  16.9 0.2 band_weights.1.bands_ref
  17.1 0.0 copy-start.3
  17.1 3.0 %mask_held.1.pool_ref = bf16[49,64,512]{2,1,0:T(8,128)(2,1)S(1)} custom-call(s32[25,1,32]{2,1,0:T(1,128)S(1)} %bitcast.18, bf16[32,64,512]{2,1,0:T(8,128)(2,1)S(1)} %bitcast.14, bf16[4,16,1280]{2,1,0:T(8,128)(2,1)S(1)} %collective-permute-done.partner_ref, bf16[4,16,1280]{2,1,0:T(8,128)(2,1)S(1)} %collective-permute-done.1.other_ref, ...), custom_call_target="tpu_custom_call" | custom-call | flops 8000000 | bytes 6291456 | tf_op jit(solution)/shard_map/mask_held/pallas_call | solution.py:213
  20.1 0.0 collective-permute-done.3.refs_1_
  20.1 4.5 %collective-permute-done.2.refs_0_ = bf16[4,16,1280]{2,1,0:T(8,128)(2,1)S(1)} collective-permute-done((bf16[4,16,1280]{2,1,0:T(8,128)(2,1)}, bf16[4,16,1280]{2,1,0:T(8,128)(2,1)S(1)}, u32[]{:S(2)}, u32[]{:S(2)}) %collective-permute-start.2) | collective-permute-done | bytes 163872 | tf_op jit(solution)/shard_map/ppermute | solution.py:448
  24.7 0.0 copy-done.3
  24.7 2.5 %convolve_4.1 = (bf16[4,64,512]{2,1,0:T(8,128)(2,1)S(1)}, bf16[49,64,512]{2,1,0:T(8,128)(2,1)S(1)}) custom-call(s32[4,8]{1,0:T(4,128)S(1)} %bitcast.19, s32[52,1,32]{2,1,0:T(1,128)S(1)} %pad_add_fusion.table_in, f32[1,256]{1,0:T(1,128)S(1)} %reshape_tile.3.bias_ref, bf16[9,384,256]{2,1,0:T(8,128)(2,1)S(1)} %band_weights.1.bands_ref, ...), custom_call_target="tpu_custom_call", output_to_operand_aliasing={{1}: (4, {})} | custom-call | flops 1 | bytes 1 | tf_op jit(solution)/shard_map/convolve_4/pallas_call | solution.py:391
  27.1 2.1 %collective-permute-start.7 = (bf16[4,64,512]{2,1,0:T(8,128)(2,1)S(1)}, bf16[4,64,512]{2,1,0:T(8,128)(2,1)S(1)}, u32[]{:S(2)}, u32[]{:S(2)}) collective-permute-start(bf16[4,64,512]{2,1,0:T(8,128)(2,1)S(1)} %get-tuple-element.20.refs_0_), channel_id=1, source_target_pairs={{0,4},{1,5},{2,6},{3,7},{4,0},{5,1},{6,2},{7,3},{8,12},{9,13},{10,... | collective-permute-start | bytes 786440 | tf_op jit(solution)/shard_map/ppermute | solution.py:491
  29.3 2.5 %convolve_5.1.refs_0_ = bf16[4,64,512]{2,1,0:T(8,128)(2,1)S(1)} custom-call(s32[4,8]{1,0:T(4,128)S(1)} %bitcast.20, s32[52,1,32]{2,1,0:T(1,128)S(1)} %pad_add_fusion.table_in, f32[1,256]{1,0:T(1,128)S(1)} %reshape_tile.3.bias_ref, bf16[9,384,256]{2,1,0:T(8,128)(2,1)S(1)} %band_weights.1.bands_ref, bf16[49,64,512]{2,1,0:T(8,128)(2,1)S(1)} %get-tuple-element.19.pool_ref, ...), custom_call_target="tpu_custom_call" | custom-call | flops 1 | bytes 1 | tf_op jit(solution)/shard_map/convolve_5/pallas_call | solution.py:391
  31.8 1.4 %collective-permute-start.10 = (bf16[4,64,512]{2,1,0:T(8,128)(2,1)S(1)}, bf16[4,64,512]{2,1,0:T(8,128)(2,1)S(1)}, u32[]{:S(2)}, u32[]{:S(2)}) collective-permute-start(bf16[4,64,512]{2,1,0:T(8,128)(2,1)S(1)} %convolve_5.1.refs_0_), channel_id=1, source_target_pairs={{0,5},{1,4},{2,7},{3,6},{4,1},{5,0},{6,3},{7,2},{8,13},{9,12},{10,... | collective-permute-start | bytes 786440 | tf_op jit(solution)/shard_map/ppermute | solution.py:491
  33.1 2.5 %convolve_6.1.refs_0_ = bf16[4,64,512]{2,1,0:T(8,128)(2,1)S(1)} custom-call(s32[4,8]{1,0:T(4,128)S(1)} %bitcast.21, s32[52,1,32]{2,1,0:T(1,128)S(1)} %pad_add_fusion.table_in, f32[1,256]{1,0:T(1,128)S(1)} %reshape_tile.3.bias_ref, bf16[9,384,256]{2,1,0:T(8,128)(2,1)S(1)} %band_weights.1.bands_ref, bf16[49,64,512]{2,1,0:T(8,128)(2,1)S(1)} %get-tuple-element.19.pool_ref, ...), custom_call_target="tpu_custom_call" | custom-call | flops 1 | bytes 1 | tf_op jit(solution)/shard_map/convolve_6/pallas_call | solution.py:391
  35.6 2.5 %convolve_7.1.refs_0_ = bf16[4,64,512]{2,1,0:T(8,128)(2,1)S(1)} custom-call(s32[4,8]{1,0:T(4,128)S(1)} %bitcast.22, s32[52,1,32]{2,1,0:T(1,128)S(1)} %pad_add_fusion.table_in, f32[1,256]{1,0:T(1,128)S(1)} %reshape_tile.3.bias_ref, bf16[9,384,256]{2,1,0:T(8,128)(2,1)S(1)} %band_weights.1.bands_ref, bf16[49,64,512]{2,1,0:T(8,128)(2,1)S(1)} %get-tuple-element.19.pool_ref, ...), custom_call_target="tpu_custom_call" | custom-call | flops 1 | bytes 1 | tf_op jit(solution)/shard_map/convolve_7/pallas_call | solution.py:391
  38.1 2.5 %convolve_3.1.refs_0_ = bf16[4,64,512]{2,1,0:T(8,128)(2,1)S(1)} custom-call(s32[4,8]{1,0:T(4,128)S(1)} %bitcast.23, s32[52,1,32]{2,1,0:T(1,128)S(1)} %pad_add_fusion.table_in, f32[1,256]{1,0:T(1,128)S(1)} %reshape_tile.3.bias_ref, bf16[9,384,256]{2,1,0:T(8,128)(2,1)S(1)} %band_weights.1.bands_ref, bf16[49,64,512]{2,1,0:T(8,128)(2,1)S(1)} %get-tuple-element.19.pool_ref, ...), custom_call_target="tpu_custom_call" | custom-call | flops 1 | bytes 1 | tf_op jit(solution)/shard_map/convolve_3/pallas_call | solution.py:391
  40.6 2.5 %convolve_2.1.refs_0_ = bf16[4,64,512]{2,1,0:T(8,128)(2,1)S(1)} custom-call(s32[4,8]{1,0:T(4,128)S(1)} %bitcast.24, s32[52,1,32]{2,1,0:T(1,128)S(1)} %pad_add_fusion.table_in, f32[1,256]{1,0:T(1,128)S(1)} %reshape_tile.3.bias_ref, bf16[9,384,256]{2,1,0:T(8,128)(2,1)S(1)} %band_weights.1.bands_ref, bf16[49,64,512]{2,1,0:T(8,128)(2,1)S(1)} %get-tuple-element.19.pool_ref, ...), custom_call_target="tpu_custom_call" | custom-call | flops 1 | bytes 1 | tf_op jit(solution)/shard_map/convolve_2/pallas_call | solution.py:391
  43.1 0.4 collective-permute-start.5
  43.5 2.2 %collective-permute-start.9 = (bf16[4,64,512]{2,1,0:T(8,128)(2,1)S(1)}, bf16[4,64,512]{2,1,0:T(8,128)(2,1)S(1)}, u32[]{:S(2)}, u32[]{:S(2)}) collective-permute-start(bf16[4,64,512]{2,1,0:T(8,128)(2,1)S(1)} %convolve_6.1.refs_0_), channel_id=1, source_target_pairs={{0,6},{1,7},{2,4},{3,5},{4,2},{5,3},{6,0},{7,1},{8,14},{9,15},{10,... | collective-permute-start | bytes 786440 | tf_op jit(solution)/shard_map/ppermute | solution.py:491
  45.7 0.3 collective-permute-start.6
  46.0 0.7 collective-permute-done.7.refs_1_
  46.8 4.4 %collective-permute-start.4 = (bf16[4,64,512]{2,1,0:T(8,128)(2,1)S(1)}, bf16[4,64,512]{2,1,0:T(8,128)(2,1)S(1)}, u32[]{:S(2)}, u32[]{:S(2)}) collective-permute-start(bf16[4,64,512]{2,1,0:T(8,128)(2,1)S(1)} %convolve_7.1.refs_0_), channel_id=1, source_target_pairs={{0,7},{1,6},{2,5},{3,4},{4,3},{5,2},{6,1},{7,0},{8,15},{9,14},{10,... | collective-permute-start | bytes 786440 | tf_op jit(solution)/shard_map/ppermute | solution.py:491
  51.1 2.5 %convolve_1.1.refs_0_ = bf16[4,64,512]{2,1,0:T(8,128)(2,1)S(1)} custom-call(s32[4,8]{1,0:T(4,128)S(1)} %bitcast.25, s32[52,1,32]{2,1,0:T(1,128)S(1)} %pad_add_fusion.table_in, f32[1,256]{1,0:T(1,128)S(1)} %reshape_tile.3.bias_ref, bf16[9,384,256]{2,1,0:T(8,128)(2,1)S(1)} %band_weights.1.bands_ref, bf16[49,64,512]{2,1,0:T(8,128)(2,1)S(1)} %get-tuple-element.19.pool_ref, ...), custom_call_target="tpu_custom_call" | custom-call | flops 1 | bytes 1 | tf_op jit(solution)/shard_map/convolve_1/pallas_call | solution.py:391
  53.6 0.0 copy-start.4
  53.6 6.0 %collective-permute-done.10.refs_1_.refs_2_ = bf16[4,64,512]{2,1,0:T(8,128)(2,1)S(1)} collective-permute-done((bf16[4,64,512]{2,1,0:T(8,128)(2,1)S(1)}, bf16[4,64,512]{2,1,0:T(8,128)(2,1)S(1)}, u32[]{:S(2)}, u32[]{:S(2)}) %collective-permute-start.10) | collective-permute-done | bytes 262176 | tf_op jit(solution)/shard_map/ppermute | solution.py:491
  59.7 0.0 collective-permute-start.8
  59.7 2.5 %convolve_0.1.refs_0_ = bf16[4,64,512]{2,1,0:T(8,128)(2,1)S(1)} custom-call(s32[4,8]{1,0:T(4,128)S(1)} %bitcast.26, s32[52,1,32]{2,1,0:T(1,128)S(1)} %pad_add_fusion.table_in, f32[1,256]{1,0:T(1,128)S(1)} %reshape_tile.3.bias_ref, bf16[9,384,256]{2,1,0:T(8,128)(2,1)S(1)} %band_weights.1.bands_ref, bf16[49,64,512]{2,1,0:T(8,128)(2,1)S(1)} %get-tuple-element.19.pool_ref, ...), custom_call_target="tpu_custom_call" | custom-call | flops 1 | bytes 1 | tf_op jit(solution)/shard_map/convolve_0/pallas_call | solution.py:391
  62.2 0.0 copy-done.4
  62.2 1.5 %place_0.1.refs_1_ = bf16[16,64,512]{2,1,0:T(8,128)(2,1)} custom-call(s32[16]{0:T(128)S(1)} %bitcast.27, bf16[4,64,512]{2,1,0:T(8,128)(2,1)S(1)} %convolve_0.1.refs_0_, bf16[4,64,512]{2,1,0:T(8,128)(2,1)S(1)} %collective-permute-done.7.refs_1_, bf16[4,64,512]{2,1,0:T(8,128)(2,1)S(1)} %collective-permute-done.10.refs_1_.refs_2_), custom_call_target="tpu_custom_call" | custom-call | flops 1 | bytes 1 | tf_op jit(solution)/shard_map/place_0/pallas_call | solution.py:431
  63.7 0.0 collective-permute-done.9.refs_0_
  63.7 1.4 %place_6.1.refs_4_ = bf16[16,64,512]{2,1,0:T(8,128)(2,1)} custom-call(s32[16]{0:T(128)S(1)} %bitcast.28, bf16[4,64,512]{2,1,0:T(8,128)(2,1)S(1)} %collective-permute-done.9.refs_0_, bf16[16,64,512]{2,1,0:T(8,128)(2,1)} %place_0.1.refs_1_), custom_call_target="tpu_custom_call", output_to_operand_aliasing={{}: (2, {})} | custom-call | flops 1 | bytes 1 | tf_op jit(solution)/shard_map/place_6/pallas_call | solution.py:431
  65.1 10.6 %collective-permute-done.6.refs_2_ = bf16[4,64,512]{2,1,0:T(8,128)(2,1)S(1)} collective-permute-done((bf16[4,64,512]{2,1,0:T(8,128)(2,1)S(1)}, bf16[4,64,512]{2,1,0:T(8,128)(2,1)S(1)}, u32[]{:S(2)}, u32[]{:S(2)}) %collective-permute-start.6) | collective-permute-done | bytes 262176 | tf_op jit(solution)/shard_map/ppermute | solution.py:491
  75.7 0.0 collective-permute-done.5.refs_1_
  75.7 0.0 collective-permute-done.4.refs_0_
  75.7 0.0 collective-permute-done.8.refs_3_
  75.7 1.5 %place_7.1 = bf16[16,64,512]{2,1,0:T(8,128)(2,1)} custom-call(s32[16]{0:T(128)S(1)} %bitcast.29, bf16[4,64,512]{2,1,0:T(8,128)(2,1)S(1)} %collective-permute-done.4.refs_0_, bf16[4,64,512]{2,1,0:T(8,128)(2,1)S(1)} %collective-permute-done.5.refs_1_, bf16[4,64,512]{2,1,0:T(8,128)(2,1)S(1)} %collective-permute-done.6.refs_2_, ...), custom_call_target="tpu_custom_call", output_to_operand_aliasing={{}: (5, {})} | custom-call | flops 1 | bytes 1 | tf_op jit(solution)/shard_map/place_7/pallas_call | solution.py:431
  (9 shorter events, 0.0 us)
Async XLA Ops:
  0.0 16.8 %copy-start.2 = (s32[1,1,32,25]{2,1,3,0:T(1,128)S(1)}, s32[1,1,32,25]{2,1,3,0:T(1,128)}, u32[]{:S(2)}) copy-start(s32[1,1,32,25]{2,1,3,0:T(1,128)} %param.10) | copy-start | bytes 9604
  0.0 11.0 %copy-start.5 = (s32[1,1,8]{2,1,0:T(1,128)S(1)}, s32[1,1,8]{2,1,0:T(1,128)}, u32[]{:S(2)}) copy-start(s32[1,1,8]{2,1,0:T(1,128)} %relays_ref.1) | copy-start | bytes 100
  0.0 16.7 %copy-start.7 = (f32[64]{0:T(128)S(1)}, f32[64]{0:T(128)}, u32[]{:S(2)}) copy-start(f32[64]{0:T(128)} %param.17) | copy-start | bytes 772
  0.0 16.8 %copy-start.6 = (s32[1,1,32,27]{2,1,3,0:T(1,128)S(1)}, s32[1,1,32,27]{2,1,3,0:T(1,128)}, u32[]{:S(2)}) copy-start(s32[1,1,32,27]{2,1,3,0:T(1,128)} %param.11) | copy-start | bytes 10372
  0.0 16.8 %copy-start.1 = (bf16[27,64,64]{2,1,0:T(8,128)(2,1)S(1)}, bf16[27,64,64]{2,1,0:T(8,128)(2,1)}, u32[]{:S(2)}) copy-start(bf16[27,64,64]{2,1,0:T(8,128)(2,1)} %weights_ref.1) | copy-start | bytes 663556
  3.0 14.0 %copy-start = (bf16[1,1,32,8,8,512]{5,4,3,2,1,0:T(8,128)(2,1)S(1)}, bf16[1,1,32,8,8,512]{5,4,3,2,1,0:T(8,128)(2,1)}, u32[]{:S(2)}) copy-start(bf16[1,1,32,8,8,512]{5,4,3,2,1,0:T(8,128)(2,1)} %param.9) | copy-start | bytes 6291460
  3.1 7.9 %collective-permute-start.1 = (bf16[4,16,1280]{2,1,0:T(8,128)(2,1)}, bf16[4,16,1280]{2,1,0:T(8,128)(2,1)S(1)}, u32[]{:S(2)}, u32[]{:S(2)}) collective-permute-start(bf16[4,16,1280]{2,1,0:T(8,128)(2,1)} %get-tuple-element.14), channel_id=1, source_target_pairs={{1,2},{3,4},{5,6},{2,1},{4,3},{6,5},{9,10},{11,12},{13,14},{10,9},... | collective-permute-start | bytes 491528 | tf_op jit(solution)/shard_map/ppermute | solution.py:447
  7.8 3.2 %collective-permute-start = (bf16[4,16,1280]{2,1,0:T(8,128)(2,1)}, bf16[4,16,1280]{2,1,0:T(8,128)(2,1)S(1)}, u32[]{:S(2)}, u32[]{:S(2)}) collective-permute-start(bf16[4,16,1280]{2,1,0:T(8,128)(2,1)} %get-tuple-element.13.refs_0_), channel_id=1, source_target_pairs={{0,1},{1,0},{2,3},{3,2},{4,5},{5,4},{6,7},{7,6},{8,9},{9,8},{10,11... | collective-permute-start | bytes 491528 | tf_op jit(solution)/shard_map/ppermute | solution.py:448
  12.3 7.8 %collective-permute-start.3 = (bf16[4,16,1280]{2,1,0:T(8,128)(2,1)}, bf16[4,16,1280]{2,1,0:T(8,128)(2,1)S(1)}, u32[]{:S(2)}, u32[]{:S(2)}) collective-permute-start(bf16[4,16,1280]{2,1,0:T(8,128)(2,1)} %get-tuple-element.18), channel_id=1, source_target_pairs={{8,16},{16,8},{9,17},{17,9},{10,18},{18,10},{11,19},{19,11},{12,20... | collective-permute-start | bytes 491528 | tf_op jit(solution)/shard_map/ppermute | solution.py:447
  13.0 11.7 %collective-permute-start.2 = (bf16[4,16,1280]{2,1,0:T(8,128)(2,1)}, bf16[4,16,1280]{2,1,0:T(8,128)(2,1)S(1)}, u32[]{:S(2)}, u32[]{:S(2)}) collective-permute-start(bf16[4,16,1280]{2,1,0:T(8,128)(2,1)} %get-tuple-element.17.earlier_ref), channel_id=1, source_target_pairs={{0,8},{8,0},{16,24},{24,16},{1,9},{9,1},{17,25},{25,17},{2,10},{10... | collective-permute-start | bytes 491528 | tf_op jit(solution)/shard_map/ppermute | solution.py:448
  17.1 7.6 %copy-start.3 = (s32[1,1,8,4]{2,3,1,0:T(4,128)S(1)}, s32[1,1,8,4]{2,3,1,0:T(4,128)}, u32[]{:S(2)}) copy-start(s32[1,1,8,4]{2,3,1,0:T(4,128)} %param.14) | copy-start | bytes 388
  27.1 19.6 %collective-permute-start.7 = (bf16[4,64,512]{2,1,0:T(8,128)(2,1)S(1)}, bf16[4,64,512]{2,1,0:T(8,128)(2,1)S(1)}, u32[]{:S(2)}, u32[]{:S(2)}) collective-permute-start(bf16[4,64,512]{2,1,0:T(8,128)(2,1)S(1)} %get-tuple-element.20.refs_0_), channel_id=1, source_target_pairs={{0,4},{1,5},{2,6},{3,7},{4,0},{5,1},{6,2},{7,3},{8,12},{9,13},{10,... | collective-permute-start | bytes 786440 | tf_op jit(solution)/shard_map/ppermute | solution.py:491
  31.8 27.9 %collective-permute-start.10 = (bf16[4,64,512]{2,1,0:T(8,128)(2,1)S(1)}, bf16[4,64,512]{2,1,0:T(8,128)(2,1)S(1)}, u32[]{:S(2)}, u32[]{:S(2)}) collective-permute-start(bf16[4,64,512]{2,1,0:T(8,128)(2,1)S(1)} %convolve_5.1.refs_0_), channel_id=1, source_target_pairs={{0,5},{1,4},{2,7},{3,6},{4,1},{5,0},{6,3},{7,2},{8,13},{9,12},{10,... | collective-permute-start | bytes 786440 | tf_op jit(solution)/shard_map/ppermute | solution.py:491
  43.1 32.6 %collective-permute-start.5 = (bf16[4,64,512]{2,1,0:T(8,128)(2,1)S(1)}, bf16[4,64,512]{2,1,0:T(8,128)(2,1)S(1)}, u32[]{:S(2)}, u32[]{:S(2)}) collective-permute-start(bf16[4,64,512]{2,1,0:T(8,128)(2,1)S(1)} %convolve_3.1.refs_0_), channel_id=1, source_target_pairs={{0,3},{1,2},{2,1},{3,0},{4,7},{5,6},{6,5},{7,4},{8,11},{9,10},{10,... | collective-permute-start | bytes 786440 | tf_op jit(solution)/shard_map/ppermute | solution.py:491
  43.5 20.2 %collective-permute-start.9 = (bf16[4,64,512]{2,1,0:T(8,128)(2,1)S(1)}, bf16[4,64,512]{2,1,0:T(8,128)(2,1)S(1)}, u32[]{:S(2)}, u32[]{:S(2)}) collective-permute-start(bf16[4,64,512]{2,1,0:T(8,128)(2,1)S(1)} %convolve_6.1.refs_0_), channel_id=1, source_target_pairs={{0,6},{1,7},{2,4},{3,5},{4,2},{5,3},{6,0},{7,1},{8,14},{9,15},{10,... | collective-permute-start | bytes 786440 | tf_op jit(solution)/shard_map/ppermute | solution.py:491
  45.7 30.0 %collective-permute-start.6 = (bf16[4,64,512]{2,1,0:T(8,128)(2,1)S(1)}, bf16[4,64,512]{2,1,0:T(8,128)(2,1)S(1)}, u32[]{:S(2)}, u32[]{:S(2)}) collective-permute-start(bf16[4,64,512]{2,1,0:T(8,128)(2,1)S(1)} %convolve_2.1.refs_0_), channel_id=1, source_target_pairs={{0,2},{1,3},{2,0},{3,1},{4,6},{5,7},{6,4},{7,5},{8,10},{9,11},{10,... | collective-permute-start | bytes 786440 | tf_op jit(solution)/shard_map/ppermute | solution.py:491
  46.8 29.0 %collective-permute-start.4 = (bf16[4,64,512]{2,1,0:T(8,128)(2,1)S(1)}, bf16[4,64,512]{2,1,0:T(8,128)(2,1)S(1)}, u32[]{:S(2)}, u32[]{:S(2)}) collective-permute-start(bf16[4,64,512]{2,1,0:T(8,128)(2,1)S(1)} %convolve_7.1.refs_0_), channel_id=1, source_target_pairs={{0,7},{1,6},{2,5},{3,4},{4,3},{5,2},{6,1},{7,0},{8,15},{9,14},{10,... | collective-permute-start | bytes 786440 | tf_op jit(solution)/shard_map/ppermute | solution.py:491
  53.6 8.5 %copy-start.4 = (s32[1,1,16]{2,1,0:T(1,128)S(1)}, s32[1,1,16]{2,1,0:T(1,128)}, u32[]{:S(2)}) copy-start(s32[1,1,16]{2,1,0:T(1,128)} %param.15) | copy-start | bytes 196
  59.7 16.0 %collective-permute-start.8 = (bf16[4,64,512]{2,1,0:T(8,128)(2,1)S(1)}, bf16[4,64,512]{2,1,0:T(8,128)(2,1)S(1)}, u32[]{:S(2)}, u32[]{:S(2)}) collective-permute-start(bf16[4,64,512]{2,1,0:T(8,128)(2,1)S(1)} %convolve_1.1.refs_0_), channel_id=1, source_target_pairs={{0,1},{1,0},{2,3},{3,2},{4,5},{5,4},{6,7},{7,6},{8,9},{9,8},{10,11... | collective-permute-start | bytes 786440 | tf_op jit(solution)/shard_map/ppermute | solution.py:491

commit v4 on v3

--- a/solution.py
+++ b/solution.py
@@ -477,7 +477,8 @@
     pool = masked_all(words, blocks, y_partner, y_other, slots + 2 * faces + 1, relay_partner)
     bands = banded(weights, relay_partner)
 
-    far, near = list(range(peers // 2, peers)), list(reversed(range(1, peers // 2)))
+    far = list(range(3 * peers // 4, peers)) + list(range(peers // 2, 3 * peers // 4))
+    near = list(reversed(range(1, peers // 2)))
     order = far + near + [0]
     arrived, shells, last = {}, (x_partner, x_other), ()
     for i, m in enumerate(order):
@@ -490,9 +491,8 @@
             pool, shells = made[1], ()
         arrived[m] = lax.ppermute(made[0], "gy", [(d, d ^ m) for d in range(peers)]) if m else made[0]
     output = placed((0,) + tuple(far[:2]), receive_order[0, 0], arrived, None)
-    if far[2:-1]:
-        output = placed(tuple(far[2:-1]), receive_order[0, 0], arrived, output)
-    output = placed(tuple(m for m in far[2:][-1:] + near), receive_order[0, 0], arrived, output)
+    output = placed(tuple(far[2:-1] + near), receive_order[0, 0], arrived, output)
+    output = placed(tuple(far[2:][-1:]), receive_order[0, 0], arrived, output)
     return output.reshape(1, 1, output.shape[0], BS, BS, LANES)
 
 

time: 78.1 us -> 77.2 us (0.988)
  waiting for transfers between devices: 22.4 us -> 15.3 us
  starting transfers between devices: 20 us -> 26.6 us
    ppermute x7, waiting for transfers between devices: 17.4 us -> 10.5 us  [on_device(): lax.ppermute(made[0], 'gy', [(d, d ^ m) for d in range(peers)])]
    ppermute x7, starting transfers between devices: 10.8 us -> 17.4 us  [on_device(): lax.ppermute(made[0], 'gy', [(d, d ^ m) for d in range(peers)])]
  transfers between devices with their start and end apart: 11 -> 11, of which waited for: 5 -> 4; matrix products, arithmetic and copies ran while one was open for 0% -> 0% of each run, Pallas kernels for 34% -> 34%
where the time goes in v4:
time: 77.2 us; the launch traced here: 76.9 us
  Pallas kernels  34.5 us (45%)
  starting transfers between devices  26.6 us (34%)
  waiting for transfers between devices  15.3 us (20%)
    pallas_call x8, Pallas kernels, convolved(): pl.pallas_call(functools.partial(conv_kernel, jobs=jobs, start=start, wai...  19.9 us
    ppermute x7, starting transfers between devices, on_device(): lax.ppermute(made[0], 'gy', [(d, d ^ m) for d in range(peers)])  17.4 us
    ppermute x7, waiting for transfers between devices, on_device(): lax.ppermute(made[0], 'gy', [(d, d ^ m) for d in range(peers)])  10.5 us
    pallas_call x2, Pallas kernels, masked_outgoing(): pl.pallas_call(functools.partial(outgoing_kernel, axis=axis), out_shape=(...  5.74 us
    ppermute x2, starting transfers between devices, exchanged(): lax.ppermute(for_other, axis, others + [(j, i) for i, j in others])  5.4 us
    ppermute x2, waiting for transfers between devices, exchanged(): lax.ppermute(for_partner, axis, [(i, i ^ 1) for i in range(count)])  4.43 us
    pallas_call x3, Pallas kernels, placed(): pl.pallas_call(functools.partial(place_kernel, distances=distances), out_...  4.39 us
    ppermute x2, starting transfers between devices, exchanged(): lax.ppermute(for_partner, axis, [(i, i ^ 1) for i in range(count)])  3.81 us
  transfers between devices with their start and end apart: 11, of which 4 were waited for; matrix products, arithmetic and copies ran while one was open for 0% of the time, Pallas kernels for 34%

profile of v4, /device:TPU:1, one launch (start us, length us, event | category | flops | bytes accessed | tf_op | source)
XLA Modules:
  0.0 76.9 jit_solution(11407006327592604418)
XLA Ops:
  0.0 0.0 copy-start.6
  0.0 0.0 copy-start.1
  0.0 3.0 %mask_outgoing_gy.1 = (bf16[4,16,1280]{2,1,0:T(8,128)(2,1)}, bf16[4,16,1280]{2,1,0:T(8,128)(2,1)}) custom-call(s32[1,1,8]{2,1,0:T(1,128)} %lists_ref.2, s32[25,1,32]{2,1,0:T(1,128)} %bitcast.15, bf16[32,64,512]{2,1,0:T(8,128)(2,1)} %bitcast.12), custom_call_target="tpu_custom_call" | custom-call | flops 2000000 | bytes 1048576 | tf_op jit(solution)/shard_map/mask_outgoing_gy/pallas_call | solution.py:170
  3.0 0.0 copy-start
  3.1 4.7 %collective-permute-start.1 = (bf16[4,16,1280]{2,1,0:T(8,128)(2,1)}, bf16[4,16,1280]{2,1,0:T(8,128)(2,1)S(1)}, u32[]{:S(2)}, u32[]{:S(2)}) collective-permute-start(bf16[4,16,1280]{2,1,0:T(8,128)(2,1)} %get-tuple-element.14), channel_id=1, source_target_pairs={{1,2},{3,4},{5,6},{2,1},{4,3},{6,5},{9,10},{11,12},{13,14},{10,9},... | collective-permute-start | bytes 491528 | tf_op jit(solution)/shard_map/ppermute | solution.py:447
  7.8 0.1 collective-permute-start
  7.9 2.7 %mask_outgoing_gx.1 = (bf16[4,16,1280]{2,1,0:T(8,128)(2,1)}, bf16[4,16,1280]{2,1,0:T(8,128)(2,1)}) custom-call(s32[1,1,8]{2,1,0:T(1,128)} %relays_ref.1, s32[25,1,32]{2,1,0:T(1,128)} %bitcast.16, bf16[32,64,512]{2,1,0:T(8,128)(2,1)} %bitcast.13, bf16[4,16,1280]{2,1,0:T(8,128)(2,1)} %get-tuple-element.13.refs_0_), custom_call_target="tpu_custom_call" | custom-call | flops 2000000 | bytes 1048576 | tf_op jit(solution)/shard_map/mask_outgoing_gx/pallas_call | solution.py:170
  10.6 0.4 collective-permute-done.1.other_ref
  11.0 0.0 collective-permute-done.partner_ref
  11.0 0.0 copy-done.5
  11.0 1.3 %gather_relays.1 = (bf16[4,16,1280]{2,1,0:T(8,128)(2,1)}, bf16[4,16,1280]{2,1,0:T(8,128)(2,1)}) custom-call(s32[1,1,8]{2,1,0:T(1,128)S(1)} %copy-done.5, bf16[4,16,1280]{2,1,0:T(8,128)(2,1)S(1)} %collective-permute-done.partner_ref, bf16[4,16,1280]{2,1,0:T(8,128)(2,1)S(1)} %collective-permute-done.1.other_ref, ...), custom_call_target="tpu_custom_call", output_to_operand_aliasing={{0}: (3, {}), {1}: (4, {})} | custom-call | bytes 655360 | tf_op jit(solution)/shard_map/gather_relays/pallas_call | solution.py:273
  12.3 0.7 collective-permute-start.3
  13.0 3.7 %collective-permute-start.2 = (bf16[4,16,1280]{2,1,0:T(8,128)(2,1)}, bf16[4,16,1280]{2,1,0:T(8,128)(2,1)S(1)}, u32[]{:S(2)}, u32[]{:S(2)}) collective-permute-start(bf16[4,16,1280]{2,1,0:T(8,128)(2,1)} %get-tuple-element.17.earlier_ref), channel_id=1, source_target_pairs={{0,8},{8,0},{16,24},{24,16},{1,9},{9,1},{17,25},{25,17},{2,10},{10... | collective-permute-start | bytes 491528 | tf_op jit(solution)/shard_map/ppermute | solution.py:448
  16.7 0.0 copy-done.7
  16.7 0.1 reshape_tile.3.bias_ref
  16.8 0.0 copy-done.2
  16.9 0.2 band_weights.1.bands_ref
  17.1 0.0 copy-start.3
  17.1 3.0 %mask_held.1.pool_ref = bf16[49,64,512]{2,1,0:T(8,128)(2,1)S(1)} custom-call(s32[25,1,32]{2,1,0:T(1,128)S(1)} %bitcast.18, bf16[32,64,512]{2,1,0:T(8,128)(2,1)S(1)} %bitcast.14, bf16[4,16,1280]{2,1,0:T(8,128)(2,1)S(1)} %collective-permute-done.partner_ref, bf16[4,16,1280]{2,1,0:T(8,128)(2,1)S(1)} %collective-permute-done.1.other_ref, ...), custom_call_target="tpu_custom_call" | custom-call | flops 8000000 | bytes 6291456 | tf_op jit(solution)/shard_map/mask_held/pallas_call | solution.py:213
  20.1 0.0 collective-permute-done.3.refs_1_
  20.1 4.4 %collective-permute-done.2.refs_0_ = bf16[4,16,1280]{2,1,0:T(8,128)(2,1)S(1)} collective-permute-done((bf16[4,16,1280]{2,1,0:T(8,128)(2,1)}, bf16[4,16,1280]{2,1,0:T(8,128)(2,1)S(1)}, u32[]{:S(2)}, u32[]{:S(2)}) %collective-permute-start.2) | collective-permute-done | bytes 163872 | tf_op jit(solution)/shard_map/ppermute | solution.py:448
  24.5 0.0 copy-done.3
  24.5 2.5 %convolve_6.1 = (bf16[4,64,512]{2,1,0:T(8,128)(2,1)S(1)}, bf16[49,64,512]{2,1,0:T(8,128)(2,1)S(1)}) custom-call(s32[4,8]{1,0:T(4,128)S(1)} %bitcast.19, s32[52,1,32]{2,1,0:T(1,128)S(1)} %pad_add_fusion.table_in, f32[1,256]{1,0:T(1,128)S(1)} %reshape_tile.3.bias_ref, bf16[9,384,256]{2,1,0:T(8,128)(2,1)S(1)} %band_weights.1.bands_ref, ...), custom_call_target="tpu_custom_call", output_to_operand_aliasing={{1}: (4, {})} | custom-call | flops 1 | bytes 1 | tf_op jit(solution)/shard_map/convolve_6/pallas_call | solution.py:391
  27.0 0.1 collective-permute-start.8
  27.1 2.5 %convolve_7.1.refs_0_ = bf16[4,64,512]{2,1,0:T(8,128)(2,1)S(1)} custom-call(s32[4,8]{1,0:T(4,128)S(1)} %bitcast.20, s32[52,1,32]{2,1,0:T(1,128)S(1)} %pad_add_fusion.table_in, f32[1,256]{1,0:T(1,128)S(1)} %reshape_tile.3.bias_ref, bf16[9,384,256]{2,1,0:T(8,128)(2,1)S(1)} %band_weights.1.bands_ref, bf16[49,64,512]{2,1,0:T(8,128)(2,1)S(1)} %get-tuple-element.19.pool_ref, ...), custom_call_target="tpu_custom_call" | custom-call | flops 1 | bytes 1 | tf_op jit(solution)/shard_map/convolve_7/pallas_call | solution.py:391
  29.6 4.4 %collective-permute-start.10 = (bf16[4,64,512]{2,1,0:T(8,128)(2,1)S(1)}, bf16[4,64,512]{2,1,0:T(8,128)(2,1)S(1)}, u32[]{:S(2)}, u32[]{:S(2)}) collective-permute-start(bf16[4,64,512]{2,1,0:T(8,128)(2,1)S(1)} %convolve_7.1.refs_0_), channel_id=1, source_target_pairs={{0,7},{1,6},{2,5},{3,4},{4,3},{5,2},{6,1},{7,0},{8,15},{9,14},{10,... | collective-permute-start | bytes 786440 | tf_op jit(solution)/shard_map/ppermute | solution.py:492
  34.0 2.5 %convolve_4.1.refs_0_ = bf16[4,64,512]{2,1,0:T(8,128)(2,1)S(1)} custom-call(s32[4,8]{1,0:T(4,128)S(1)} %bitcast.21, s32[52,1,32]{2,1,0:T(1,128)S(1)} %pad_add_fusion.table_in, f32[1,256]{1,0:T(1,128)S(1)} %reshape_tile.3.bias_ref, bf16[9,384,256]{2,1,0:T(8,128)(2,1)S(1)} %band_weights.1.bands_ref, bf16[49,64,512]{2,1,0:T(8,128)(2,1)S(1)} %get-tuple-element.19.pool_ref, ...), custom_call_target="tpu_custom_call" | custom-call | flops 1 | bytes 1 | tf_op jit(solution)/shard_map/convolve_4/pallas_call | solution.py:391
  36.5 2.5 %convolve_5.1.refs_0_ = bf16[4,64,512]{2,1,0:T(8,128)(2,1)S(1)} custom-call(s32[4,8]{1,0:T(4,128)S(1)} %bitcast.22, s32[52,1,32]{2,1,0:T(1,128)S(1)} %pad_add_fusion.table_in, f32[1,256]{1,0:T(1,128)S(1)} %reshape_tile.3.bias_ref, bf16[9,384,256]{2,1,0:T(8,128)(2,1)S(1)} %band_weights.1.bands_ref, bf16[49,64,512]{2,1,0:T(8,128)(2,1)S(1)} %get-tuple-element.19.pool_ref, ...), custom_call_target="tpu_custom_call" | custom-call | flops 1 | bytes 1 | tf_op jit(solution)/shard_map/convolve_5/pallas_call | solution.py:391
  39.0 2.5 %convolve_3.1.refs_0_ = bf16[4,64,512]{2,1,0:T(8,128)(2,1)S(1)} custom-call(s32[4,8]{1,0:T(4,128)S(1)} %bitcast.23, s32[52,1,32]{2,1,0:T(1,128)S(1)} %pad_add_fusion.table_in, f32[1,256]{1,0:T(1,128)S(1)} %reshape_tile.3.bias_ref, bf16[9,384,256]{2,1,0:T(8,128)(2,1)S(1)} %band_weights.1.bands_ref, bf16[49,64,512]{2,1,0:T(8,128)(2,1)S(1)} %get-tuple-element.19.pool_ref, ...), custom_call_target="tpu_custom_call" | custom-call | flops 1 | bytes 1 | tf_op jit(solution)/shard_map/convolve_3/pallas_call | solution.py:391
  41.5 2.5 %convolve_2.1.refs_0_ = bf16[4,64,512]{2,1,0:T(8,128)(2,1)S(1)} custom-call(s32[4,8]{1,0:T(4,128)S(1)} %bitcast.24, s32[52,1,32]{2,1,0:T(1,128)S(1)} %pad_add_fusion.table_in, f32[1,256]{1,0:T(1,128)S(1)} %reshape_tile.3.bias_ref, bf16[9,384,256]{2,1,0:T(8,128)(2,1)S(1)} %band_weights.1.bands_ref, bf16[49,64,512]{2,1,0:T(8,128)(2,1)S(1)} %get-tuple-element.19.pool_ref, ...), custom_call_target="tpu_custom_call" | custom-call | flops 1 | bytes 1 | tf_op jit(solution)/shard_map/convolve_2/pallas_call | solution.py:391
  44.0 0.1 collective-permute-start.6
  44.1 0.7 collective-permute-start.5
  44.8 1.4 %collective-permute-start.7 = (bf16[4,64,512]{2,1,0:T(8,128)(2,1)S(1)}, bf16[4,64,512]{2,1,0:T(8,128)(2,1)S(1)}, u32[]{:S(2)}, u32[]{:S(2)}) collective-permute-start(bf16[4,64,512]{2,1,0:T(8,128)(2,1)S(1)} %convolve_2.1.refs_0_), channel_id=1, source_target_pairs={{0,2},{1,3},{2,0},{3,1},{4,6},{5,7},{6,4},{7,5},{8,10},{9,11},{10,... | collective-permute-start | bytes 786440 | tf_op jit(solution)/shard_map/ppermute | solution.py:492
  46.3 0.0 collective-permute-done.8.refs_1_
  46.3 2.5 %convolve_1.1.refs_0_ = bf16[4,64,512]{2,1,0:T(8,128)(2,1)S(1)} custom-call(s32[4,8]{1,0:T(4,128)S(1)} %bitcast.25, s32[52,1,32]{2,1,0:T(1,128)S(1)} %pad_add_fusion.table_in, f32[1,256]{1,0:T(1,128)S(1)} %reshape_tile.3.bias_ref, bf16[9,384,256]{2,1,0:T(8,128)(2,1)S(1)} %band_weights.1.bands_ref, bf16[49,64,512]{2,1,0:T(8,128)(2,1)S(1)} %get-tuple-element.19.pool_ref, ...), custom_call_target="tpu_custom_call" | custom-call | flops 1 | bytes 1 | tf_op jit(solution)/shard_map/convolve_1/pallas_call | solution.py:391
  48.8 0.0 copy-start.4
  48.8 1.0 %collective-permute-start.9 = (bf16[4,64,512]{2,1,0:T(8,128)(2,1)S(1)}, bf16[4,64,512]{2,1,0:T(8,128)(2,1)S(1)}, u32[]{:S(2)}, u32[]{:S(2)}) collective-permute-start(bf16[4,64,512]{2,1,0:T(8,128)(2,1)S(1)} %convolve_1.1.refs_0_), channel_id=1, source_target_pairs={{0,1},{1,0},{2,3},{3,2},{4,5},{5,4},{6,7},{7,6},{8,9},{9,8},{10,11... | collective-permute-start | bytes 786440 | tf_op jit(solution)/shard_map/ppermute | solution.py:492
  49.8 0.0 collective-permute-done.10.refs_1_.refs_2_
  49.8 9.6 %collective-permute-start.4 = (bf16[4,64,512]{2,1,0:T(8,128)(2,1)S(1)}, bf16[4,64,512]{2,1,0:T(8,128)(2,1)S(1)}, u32[]{:S(2)}, u32[]{:S(2)}) collective-permute-start(bf16[4,64,512]{2,1,0:T(8,128)(2,1)S(1)} %convolve_5.1.refs_0_), channel_id=1, source_target_pairs={{0,5},{1,4},{2,7},{3,6},{4,1},{5,0},{6,3},{7,2},{8,13},{9,12},{10,... | collective-permute-start | bytes 786440 | tf_op jit(solution)/shard_map/ppermute | solution.py:492
  59.4 2.5 %convolve_0.1.refs_0_ = bf16[4,64,512]{2,1,0:T(8,128)(2,1)S(1)} custom-call(s32[4,8]{1,0:T(4,128)S(1)} %bitcast.26, s32[52,1,32]{2,1,0:T(1,128)S(1)} %pad_add_fusion.table_in, f32[1,256]{1,0:T(1,128)S(1)} %reshape_tile.3.bias_ref, bf16[9,384,256]{2,1,0:T(8,128)(2,1)S(1)} %band_weights.1.bands_ref, bf16[49,64,512]{2,1,0:T(8,128)(2,1)S(1)} %get-tuple-element.19.pool_ref, ...), custom_call_target="tpu_custom_call" | custom-call | flops 1 | bytes 1 | tf_op jit(solution)/shard_map/convolve_0/pallas_call | solution.py:391
  61.9 1.5 %place_0.1.refs_4_ = bf16[16,64,512]{2,1,0:T(8,128)(2,1)} custom-call(s32[16]{0:T(128)S(1)} %bitcast.27, bf16[4,64,512]{2,1,0:T(8,128)(2,1)S(1)} %convolve_0.1.refs_0_, bf16[4,64,512]{2,1,0:T(8,128)(2,1)S(1)} %collective-permute-done.8.refs_1_, bf16[4,64,512]{2,1,0:T(8,128)(2,1)S(1)} %collective-permute-done.10.refs_1_.refs_2_), custom_call_target="tpu_custom_call" | custom-call | flops 1 | bytes 1 | tf_op jit(solution)/shard_map/place_0/pallas_call | solution.py:431
  63.4 0.0 collective-permute-done.7.refs_2_
  63.4 0.0 collective-permute-done.6.refs_1_
  63.4 0.1 collective-permute-done.5.refs_0_
  63.5 0.0 collective-permute-done.9.refs_3_
  63.5 1.5 %place_4.1.refs_1_ = bf16[16,64,512]{2,1,0:T(8,128)(2,1)} custom-call(s32[16]{0:T(128)S(1)} %bitcast.28, bf16[4,64,512]{2,1,0:T(8,128)(2,1)S(1)} %collective-permute-done.5.refs_0_, bf16[4,64,512]{2,1,0:T(8,128)(2,1)S(1)} %collective-permute-done.6.refs_1_, bf16[4,64,512]{2,1,0:T(8,128)(2,1)S(1)} %collective-permute-done.7.refs_2_, ...), custom_call_target="tpu_custom_call", output_to_operand_aliasing={{}: (5, {})} | custom-call | flops 1 | bytes 1 | tf_op jit(solution)/shard_map/place_4/pallas_call | solution.py:431
  65.1 10.4 %collective-permute-done.4.refs_0_ = bf16[4,64,512]{2,1,0:T(8,128)(2,1)S(1)} collective-permute-done((bf16[4,64,512]{2,1,0:T(8,128)(2,1)S(1)}, bf16[4,64,512]{2,1,0:T(8,128)(2,1)S(1)}, u32[]{:S(2)}, u32[]{:S(2)}) %collective-permute-start.4) | collective-permute-done | bytes 262176 | tf_op jit(solution)/shard_map/ppermute | solution.py:492
  75.4 1.4 %place_5.1 = bf16[16,64,512]{2,1,0:T(8,128)(2,1)} custom-call(s32[16]{0:T(128)S(1)} %bitcast.29, bf16[4,64,512]{2,1,0:T(8,128)(2,1)S(1)} %collective-permute-done.4.refs_0_, bf16[16,64,512]{2,1,0:T(8,128)(2,1)} %place_4.1.refs_1_), custom_call_target="tpu_custom_call", output_to_operand_aliasing={{}: (2, {})} | custom-call | flops 1 | bytes 1 | tf_op jit(solution)/shard_map/place_5/pallas_call | solution.py:431
  (9 shorter events, 0.0 us)
Async XLA Ops:
  0.0 16.8 %copy-start.2 = (s32[1,1,32,25]{2,1,3,0:T(1,128)S(1)}, s32[1,1,32,25]{2,1,3,0:T(1,128)}, u32[]{:S(2)}) copy-start(s32[1,1,32,25]{2,1,3,0:T(1,128)} %param.10) | copy-start | bytes 9604
  0.0 11.0 %copy-start.5 = (s32[1,1,8]{2,1,0:T(1,128)S(1)}, s32[1,1,8]{2,1,0:T(1,128)}, u32[]{:S(2)}) copy-start(s32[1,1,8]{2,1,0:T(1,128)} %relays_ref.1) | copy-start | bytes 100
  0.0 16.7 %copy-start.7 = (f32[64]{0:T(128)S(1)}, f32[64]{0:T(128)}, u32[]{:S(2)}) copy-start(f32[64]{0:T(128)} %param.17) | copy-start | bytes 772
  0.0 16.8 %copy-start.6 = (s32[1,1,32,27]{2,1,3,0:T(1,128)S(1)}, s32[1,1,32,27]{2,1,3,0:T(1,128)}, u32[]{:S(2)}) copy-start(s32[1,1,32,27]{2,1,3,0:T(1,128)} %param.11) | copy-start | bytes 10372
  0.0 16.8 %copy-start.1 = (bf16[27,64,64]{2,1,0:T(8,128)(2,1)S(1)}, bf16[27,64,64]{2,1,0:T(8,128)(2,1)}, u32[]{:S(2)}) copy-start(bf16[27,64,64]{2,1,0:T(8,128)(2,1)} %weights_ref.1) | copy-start | bytes 663556
  3.0 14.0 %copy-start = (bf16[1,1,32,8,8,512]{5,4,3,2,1,0:T(8,128)(2,1)S(1)}, bf16[1,1,32,8,8,512]{5,4,3,2,1,0:T(8,128)(2,1)}, u32[]{:S(2)}) copy-start(bf16[1,1,32,8,8,512]{5,4,3,2,1,0:T(8,128)(2,1)} %param.9) | copy-start | bytes 6291460
  3.1 7.9 %collective-permute-start.1 = (bf16[4,16,1280]{2,1,0:T(8,128)(2,1)}, bf16[4,16,1280]{2,1,0:T(8,128)(2,1)S(1)}, u32[]{:S(2)}, u32[]{:S(2)}) collective-permute-start(bf16[4,16,1280]{2,1,0:T(8,128)(2,1)} %get-tuple-element.14), channel_id=1, source_target_pairs={{1,2},{3,4},{5,6},{2,1},{4,3},{6,5},{9,10},{11,12},{13,14},{10,9},... | collective-permute-start | bytes 491528 | tf_op jit(solution)/shard_map/ppermute | solution.py:447
  7.8 3.2 %collective-permute-start = (bf16[4,16,1280]{2,1,0:T(8,128)(2,1)}, bf16[4,16,1280]{2,1,0:T(8,128)(2,1)S(1)}, u32[]{:S(2)}, u32[]{:S(2)}) collective-permute-start(bf16[4,16,1280]{2,1,0:T(8,128)(2,1)} %get-tuple-element.13.refs_0_), channel_id=1, source_target_pairs={{0,1},{1,0},{2,3},{3,2},{4,5},{5,4},{6,7},{7,6},{8,9},{9,8},{10,11... | collective-permute-start | bytes 491528 | tf_op jit(solution)/shard_map/ppermute | solution.py:448
  12.3 7.8 %collective-permute-start.3 = (bf16[4,16,1280]{2,1,0:T(8,128)(2,1)}, bf16[4,16,1280]{2,1,0:T(8,128)(2,1)S(1)}, u32[]{:S(2)}, u32[]{:S(2)}) collective-permute-start(bf16[4,16,1280]{2,1,0:T(8,128)(2,1)} %get-tuple-element.18), channel_id=1, source_target_pairs={{8,16},{16,8},{9,17},{17,9},{10,18},{18,10},{11,19},{19,11},{12,20... | collective-permute-start | bytes 491528 | tf_op jit(solution)/shard_map/ppermute | solution.py:447
  13.0 11.6 %collective-permute-start.2 = (bf16[4,16,1280]{2,1,0:T(8,128)(2,1)}, bf16[4,16,1280]{2,1,0:T(8,128)(2,1)S(1)}, u32[]{:S(2)}, u32[]{:S(2)}) collective-permute-start(bf16[4,16,1280]{2,1,0:T(8,128)(2,1)} %get-tuple-element.17.earlier_ref), channel_id=1, source_target_pairs={{0,8},{8,0},{16,24},{24,16},{1,9},{9,1},{17,25},{25,17},{2,10},{10... | collective-permute-start | bytes 491528 | tf_op jit(solution)/shard_map/ppermute | solution.py:448
  17.1 7.4 %copy-start.3 = (s32[1,1,8,4]{2,3,1,0:T(4,128)S(1)}, s32[1,1,8,4]{2,3,1,0:T(4,128)}, u32[]{:S(2)}) copy-start(s32[1,1,8,4]{2,3,1,0:T(4,128)} %param.14) | copy-start | bytes 388
  27.0 19.3 %collective-permute-start.8 = (bf16[4,64,512]{2,1,0:T(8,128)(2,1)S(1)}, bf16[4,64,512]{2,1,0:T(8,128)(2,1)S(1)}, u32[]{:S(2)}, u32[]{:S(2)}) collective-permute-start(bf16[4,64,512]{2,1,0:T(8,128)(2,1)S(1)} %get-tuple-element.20.refs_0_), channel_id=1, source_target_pairs={{0,6},{1,7},{2,4},{3,5},{4,2},{5,3},{6,0},{7,1},{8,14},{9,15},{10,... | collective-permute-start | bytes 786440 | tf_op jit(solution)/shard_map/ppermute | solution.py:492
  29.6 20.2 %collective-permute-start.10 = (bf16[4,64,512]{2,1,0:T(8,128)(2,1)S(1)}, bf16[4,64,512]{2,1,0:T(8,128)(2,1)S(1)}, u32[]{:S(2)}, u32[]{:S(2)}) collective-permute-start(bf16[4,64,512]{2,1,0:T(8,128)(2,1)S(1)} %convolve_7.1.refs_0_), channel_id=1, source_target_pairs={{0,7},{1,6},{2,5},{3,4},{4,3},{5,2},{6,1},{7,0},{8,15},{9,14},{10,... | collective-permute-start | bytes 786440 | tf_op jit(solution)/shard_map/ppermute | solution.py:492
  44.0 19.4 %collective-permute-start.6 = (bf16[4,64,512]{2,1,0:T(8,128)(2,1)S(1)}, bf16[4,64,512]{2,1,0:T(8,128)(2,1)S(1)}, u32[]{:S(2)}, u32[]{:S(2)}) collective-permute-start(bf16[4,64,512]{2,1,0:T(8,128)(2,1)S(1)} %convolve_3.1.refs_0_), channel_id=1, source_target_pairs={{0,3},{1,2},{2,1},{3,0},{4,7},{5,6},{6,5},{7,4},{8,11},{9,10},{10,... | collective-permute-start | bytes 786440 | tf_op jit(solution)/shard_map/ppermute | solution.py:492
  44.1 19.4 %collective-permute-start.5 = (bf16[4,64,512]{2,1,0:T(8,128)(2,1)S(1)}, bf16[4,64,512]{2,1,0:T(8,128)(2,1)S(1)}, u32[]{:S(2)}, u32[]{:S(2)}) collective-permute-start(bf16[4,64,512]{2,1,0:T(8,128)(2,1)S(1)} %convolve_4.1.refs_0_), channel_id=1, source_target_pairs={{0,4},{1,5},{2,6},{3,7},{4,0},{5,1},{6,2},{7,3},{8,12},{9,13},{10,... | collective-permute-start | bytes 786440 | tf_op jit(solution)/shard_map/ppermute | solution.py:492
  44.8 18.5 %collective-permute-start.7 = (bf16[4,64,512]{2,1,0:T(8,128)(2,1)S(1)}, bf16[4,64,512]{2,1,0:T(8,128)(2,1)S(1)}, u32[]{:S(2)}, u32[]{:S(2)}) collective-permute-start(bf16[4,64,512]{2,1,0:T(8,128)(2,1)S(1)} %convolve_2.1.refs_0_), channel_id=1, source_target_pairs={{0,2},{1,3},{2,0},{3,1},{4,6},{5,7},{6,4},{7,5},{8,10},{9,11},{10,... | collective-permute-start | bytes 786440 | tf_op jit(solution)/shard_map/ppermute | solution.py:492
  48.8 13.1 %copy-start.4 = (s32[1,1,16]{2,1,0:T(1,128)S(1)}, s32[1,1,16]{2,1,0:T(1,128)}, u32[]{:S(2)}) copy-start(s32[1,1,16]{2,1,0:T(1,128)} %param.15) | copy-start | bytes 196
  48.8 14.7 %collective-permute-start.9 = (bf16[4,64,512]{2,1,0:T(8,128)(2,1)S(1)}, bf16[4,64,512]{2,1,0:T(8,128)(2,1)S(1)}, u32[]{:S(2)}, u32[]{:S(2)}) collective-permute-start(bf16[4,64,512]{2,1,0:T(8,128)(2,1)S(1)} %convolve_1.1.refs_0_), channel_id=1, source_target_pairs={{0,1},{1,0},{2,3},{3,2},{4,5},{5,4},{6,7},{7,6},{8,9},{9,8},{10,11... | collective-permute-start | bytes 786440 | tf_op jit(solution)/shard_map/ppermute | solution.py:492
  49.8 25.6 %collective-permute-start.4 = (bf16[4,64,512]{2,1,0:T(8,128)(2,1)S(1)}, bf16[4,64,512]{2,1,0:T(8,128)(2,1)S(1)}, u32[]{:S(2)}, u32[]{:S(2)}) collective-permute-start(bf16[4,64,512]{2,1,0:T(8,128)(2,1)S(1)} %convolve_5.1.refs_0_), channel_id=1, source_target_pairs={{0,5},{1,4},{2,7},{3,6},{4,1},{5,0},{6,3},{7,2},{8,13},{9,12},{10,... | collective-permute-start | bytes 786440 | tf_op jit(solution)/shard_map/ppermute | solution.py:492

commit v5 on v4

--- a/solution.py
+++ b/solution.py
@@ -478,7 +478,7 @@
     bands = banded(weights, relay_partner)
 
     far = list(range(3 * peers // 4, peers)) + list(range(peers // 2, 3 * peers // 4))
-    near = list(reversed(range(1, peers // 2)))
+    near = list(range(2, peers // 2)) + [1]
     order = far + near + [0]
     arrived, shells, last = {}, (x_partner, x_other), ()
     for i, m in enumerate(order):

time: 77.2 us -> 77.1 us (level)
  transfers between devices with their start and end apart: 11 -> 11, of which waited for: 4 -> 3; matrix products, arithmetic and copies ran while one was open for 0% -> 0% of each run, Pallas kernels for 34% -> 34%
where the time goes in v5:
time: 77.1 us; the launch traced here: 76.8 us
  Pallas kernels  34.5 us (45%)
  starting transfers between devices  26.6 us (35%)
  waiting for transfers between devices  15.2 us (20%)
    pallas_call x8, Pallas kernels, convolved(): pl.pallas_call(functools.partial(conv_kernel, jobs=jobs, start=start, wai...  19.9 us
    ppermute x7, starting transfers between devices, on_device(): lax.ppermute(made[0], 'gy', [(d, d ^ m) for d in range(peers)])  17.4 us
    ppermute x7, waiting for transfers between devices, on_device(): lax.ppermute(made[0], 'gy', [(d, d ^ m) for d in range(peers)])  10.5 us
    pallas_call x2, Pallas kernels, masked_outgoing(): pl.pallas_call(functools.partial(outgoing_kernel, axis=axis), out_shape=(...  5.77 us
    ppermute x2, starting transfers between devices, exchanged(): lax.ppermute(for_other, axis, others + [(j, i) for i, j in others])  5.4 us
    ppermute x2, waiting for transfers between devices, exchanged(): lax.ppermute(for_partner, axis, [(i, i ^ 1) for i in range(count)])  4.38 us
    pallas_call x3, Pallas kernels, placed(): pl.pallas_call(functools.partial(place_kernel, distances=distances), out_...  4.36 us
    ppermute x2, starting transfers between devices, exchanged(): lax.ppermute(for_partner, axis, [(i, i ^ 1) for i in range(count)])  3.83 us
  transfers between devices with their start and end apart: 11, of which 3 were waited for; matrix products, arithmetic and copies ran while one was open for 0% of the time, Pallas kernels for 34%

profile of v5, /device:TPU:1, one launch (start us, length us, event | category | flops | bytes accessed | tf_op | source)
XLA Modules:
  0.0 76.8 jit_solution(16823687833784070112)
XLA Ops:
  0.0 0.0 copy-start.6
  0.0 0.0 copy-start.1
  0.0 3.0 %mask_outgoing_gy.1 = (bf16[4,16,1280]{2,1,0:T(8,128)(2,1)}, bf16[4,16,1280]{2,1,0:T(8,128)(2,1)}) custom-call(s32[1,1,8]{2,1,0:T(1,128)} %lists_ref.2, s32[25,1,32]{2,1,0:T(1,128)} %bitcast.15, bf16[32,64,512]{2,1,0:T(8,128)(2,1)} %bitcast.12), custom_call_target="tpu_custom_call" | custom-call | flops 2000000 | bytes 1048576 | tf_op jit(solution)/shard_map/mask_outgoing_gy/pallas_call | solution.py:170
  3.0 0.0 copy-start
  3.1 4.7 %collective-permute-start.1 = (bf16[4,16,1280]{2,1,0:T(8,128)(2,1)}, bf16[4,16,1280]{2,1,0:T(8,128)(2,1)S(1)}, u32[]{:S(2)}, u32[]{:S(2)}) collective-permute-start(bf16[4,16,1280]{2,1,0:T(8,128)(2,1)} %get-tuple-element.14), channel_id=1, source_target_pairs={{1,2},{3,4},{5,6},{2,1},{4,3},{6,5},{9,10},{11,12},{13,14},{10,9},... | collective-permute-start | bytes 491528 | tf_op jit(solution)/shard_map/ppermute | solution.py:447
  7.8 0.1 collective-permute-start
  7.9 2.8 %mask_outgoing_gx.1 = (bf16[4,16,1280]{2,1,0:T(8,128)(2,1)}, bf16[4,16,1280]{2,1,0:T(8,128)(2,1)}) custom-call(s32[1,1,8]{2,1,0:T(1,128)} %relays_ref.1, s32[25,1,32]{2,1,0:T(1,128)} %bitcast.16, bf16[32,64,512]{2,1,0:T(8,128)(2,1)} %bitcast.13, bf16[4,16,1280]{2,1,0:T(8,128)(2,1)} %get-tuple-element.13.refs_0_), custom_call_target="tpu_custom_call" | custom-call | flops 2000000 | bytes 1048576 | tf_op jit(solution)/shard_map/mask_outgoing_gx/pallas_call | solution.py:170
  10.6 0.4 collective-permute-done.1.other_ref
  11.0 0.0 collective-permute-done.partner_ref
  11.0 0.0 copy-done.5
  11.0 1.3 %gather_relays.1 = (bf16[4,16,1280]{2,1,0:T(8,128)(2,1)}, bf16[4,16,1280]{2,1,0:T(8,128)(2,1)}) custom-call(s32[1,1,8]{2,1,0:T(1,128)S(1)} %copy-done.5, bf16[4,16,1280]{2,1,0:T(8,128)(2,1)S(1)} %collective-permute-done.partner_ref, bf16[4,16,1280]{2,1,0:T(8,128)(2,1)S(1)} %collective-permute-done.1.other_ref, ...), custom_call_target="tpu_custom_call", output_to_operand_aliasing={{0}: (3, {}), {1}: (4, {})} | custom-call | bytes 655360 | tf_op jit(solution)/shard_map/gather_relays/pallas_call | solution.py:273
  12.3 0.7 collective-permute-start.3
  13.0 3.8 %collective-permute-start.2 = (bf16[4,16,1280]{2,1,0:T(8,128)(2,1)}, bf16[4,16,1280]{2,1,0:T(8,128)(2,1)S(1)}, u32[]{:S(2)}, u32[]{:S(2)}) collective-permute-start(bf16[4,16,1280]{2,1,0:T(8,128)(2,1)} %get-tuple-element.17.earlier_ref), channel_id=1, source_target_pairs={{0,8},{8,0},{16,24},{24,16},{1,9},{9,1},{17,25},{25,17},{2,10},{10... | collective-permute-start | bytes 491528 | tf_op jit(solution)/shard_map/ppermute | solution.py:448
  16.7 0.0 copy-done.7
  16.7 0.1 reshape_tile.3.bias_ref
  16.8 0.0 copy-done.2
  16.8 0.0 copy-done.6
  16.8 0.2 band_weights.1.bands_ref
  17.1 0.0 copy-start.3
  17.1 3.0 %mask_held.1.pool_ref = bf16[49,64,512]{2,1,0:T(8,128)(2,1)S(1)} custom-call(s32[25,1,32]{2,1,0:T(1,128)S(1)} %bitcast.18, bf16[32,64,512]{2,1,0:T(8,128)(2,1)S(1)} %bitcast.14, bf16[4,16,1280]{2,1,0:T(8,128)(2,1)S(1)} %collective-permute-done.partner_ref, bf16[4,16,1280]{2,1,0:T(8,128)(2,1)S(1)} %collective-permute-done.1.other_ref, ...), custom_call_target="tpu_custom_call" | custom-call | flops 8000000 | bytes 6291456 | tf_op jit(solution)/shard_map/mask_held/pallas_call | solution.py:213
  20.1 0.0 collective-permute-done.3.refs_1_
  20.1 4.4 %collective-permute-done.2.refs_0_ = bf16[4,16,1280]{2,1,0:T(8,128)(2,1)S(1)} collective-permute-done((bf16[4,16,1280]{2,1,0:T(8,128)(2,1)}, bf16[4,16,1280]{2,1,0:T(8,128)(2,1)S(1)}, u32[]{:S(2)}, u32[]{:S(2)}) %collective-permute-start.2) | collective-permute-done | bytes 163872 | tf_op jit(solution)/shard_map/ppermute | solution.py:448
  24.5 2.5 %convolve_6.1 = (bf16[4,64,512]{2,1,0:T(8,128)(2,1)S(1)}, bf16[49,64,512]{2,1,0:T(8,128)(2,1)S(1)}) custom-call(s32[4,8]{1,0:T(4,128)S(1)} %bitcast.19, s32[52,1,32]{2,1,0:T(1,128)S(1)} %pad_add_fusion.table_in, f32[1,256]{1,0:T(1,128)S(1)} %reshape_tile.3.bias_ref, bf16[9,384,256]{2,1,0:T(8,128)(2,1)S(1)} %band_weights.1.bands_ref, ...), custom_call_target="tpu_custom_call", output_to_operand_aliasing={{1}: (4, {})} | custom-call | flops 1 | bytes 1 | tf_op jit(solution)/shard_map/convolve_6/pallas_call | solution.py:391
  27.0 0.1 collective-permute-start.8
  27.0 2.5 %convolve_7.1.refs_0_ = bf16[4,64,512]{2,1,0:T(8,128)(2,1)S(1)} custom-call(s32[4,8]{1,0:T(4,128)S(1)} %bitcast.20, s32[52,1,32]{2,1,0:T(1,128)S(1)} %pad_add_fusion.table_in, f32[1,256]{1,0:T(1,128)S(1)} %reshape_tile.3.bias_ref, bf16[9,384,256]{2,1,0:T(8,128)(2,1)S(1)} %band_weights.1.bands_ref, bf16[49,64,512]{2,1,0:T(8,128)(2,1)S(1)} %get-tuple-element.19.pool_ref, ...), custom_call_target="tpu_custom_call" | custom-call | flops 1 | bytes 1 | tf_op jit(solution)/shard_map/convolve_7/pallas_call | solution.py:391
  29.5 4.5 %collective-permute-start.10 = (bf16[4,64,512]{2,1,0:T(8,128)(2,1)S(1)}, bf16[4,64,512]{2,1,0:T(8,128)(2,1)S(1)}, u32[]{:S(2)}, u32[]{:S(2)}) collective-permute-start(bf16[4,64,512]{2,1,0:T(8,128)(2,1)S(1)} %convolve_7.1.refs_0_), channel_id=1, source_target_pairs={{0,7},{1,6},{2,5},{3,4},{4,3},{5,2},{6,1},{7,0},{8,15},{9,14},{10,... | collective-permute-start | bytes 786440 | tf_op jit(solution)/shard_map/ppermute | solution.py:492
  34.0 2.5 %convolve_4.1.refs_0_ = bf16[4,64,512]{2,1,0:T(8,128)(2,1)S(1)} custom-call(s32[4,8]{1,0:T(4,128)S(1)} %bitcast.21, s32[52,1,32]{2,1,0:T(1,128)S(1)} %pad_add_fusion.table_in, f32[1,256]{1,0:T(1,128)S(1)} %reshape_tile.3.bias_ref, bf16[9,384,256]{2,1,0:T(8,128)(2,1)S(1)} %band_weights.1.bands_ref, bf16[49,64,512]{2,1,0:T(8,128)(2,1)S(1)} %get-tuple-element.19.pool_ref, ...), custom_call_target="tpu_custom_call" | custom-call | flops 1 | bytes 1 | tf_op jit(solution)/shard_map/convolve_4/pallas_call | solution.py:391
  36.5 2.5 %convolve_5.1.refs_0_ = bf16[4,64,512]{2,1,0:T(8,128)(2,1)S(1)} custom-call(s32[4,8]{1,0:T(4,128)S(1)} %bitcast.22, s32[52,1,32]{2,1,0:T(1,128)S(1)} %pad_add_fusion.table_in, f32[1,256]{1,0:T(1,128)S(1)} %reshape_tile.3.bias_ref, bf16[9,384,256]{2,1,0:T(8,128)(2,1)S(1)} %band_weights.1.bands_ref, bf16[49,64,512]{2,1,0:T(8,128)(2,1)S(1)} %get-tuple-element.19.pool_ref, ...), custom_call_target="tpu_custom_call" | custom-call | flops 1 | bytes 1 | tf_op jit(solution)/shard_map/convolve_5/pallas_call | solution.py:391
  39.0 2.5 %convolve_2.1.refs_0_ = bf16[4,64,512]{2,1,0:T(8,128)(2,1)S(1)} custom-call(s32[4,8]{1,0:T(4,128)S(1)} %bitcast.23, s32[52,1,32]{2,1,0:T(1,128)S(1)} %pad_add_fusion.table_in, f32[1,256]{1,0:T(1,128)S(1)} %reshape_tile.3.bias_ref, bf16[9,384,256]{2,1,0:T(8,128)(2,1)S(1)} %band_weights.1.bands_ref, bf16[49,64,512]{2,1,0:T(8,128)(2,1)S(1)} %get-tuple-element.19.pool_ref, ...), custom_call_target="tpu_custom_call" | custom-call | flops 1 | bytes 1 | tf_op jit(solution)/shard_map/convolve_2/pallas_call | solution.py:391
  41.5 2.5 %convolve_3.1.refs_0_ = bf16[4,64,512]{2,1,0:T(8,128)(2,1)S(1)} custom-call(s32[4,8]{1,0:T(4,128)S(1)} %bitcast.24, s32[52,1,32]{2,1,0:T(1,128)S(1)} %pad_add_fusion.table_in, f32[1,256]{1,0:T(1,128)S(1)} %reshape_tile.3.bias_ref, bf16[9,384,256]{2,1,0:T(8,128)(2,1)S(1)} %band_weights.1.bands_ref, bf16[49,64,512]{2,1,0:T(8,128)(2,1)S(1)} %get-tuple-element.19.pool_ref, ...), custom_call_target="tpu_custom_call" | custom-call | flops 1 | bytes 1 | tf_op jit(solution)/shard_map/convolve_3/pallas_call | solution.py:391
  44.0 0.1 collective-permute-start.6
  44.1 2.1 %collective-permute-start.5 = (bf16[4,64,512]{2,1,0:T(8,128)(2,1)S(1)}, bf16[4,64,512]{2,1,0:T(8,128)(2,1)S(1)}, u32[]{:S(2)}, u32[]{:S(2)}) collective-permute-start(bf16[4,64,512]{2,1,0:T(8,128)(2,1)S(1)} %convolve_4.1.refs_0_), channel_id=1, source_target_pairs={{0,4},{1,5},{2,6},{3,7},{4,0},{5,1},{6,2},{7,3},{8,12},{9,13},{10,... | collective-permute-start | bytes 786440 | tf_op jit(solution)/shard_map/ppermute | solution.py:492
  46.2 0.0 collective-permute-start.7
  46.2 0.0 collective-permute-done.8.refs_1_
  46.2 2.5 %convolve_1.1.refs_0_ = bf16[4,64,512]{2,1,0:T(8,128)(2,1)S(1)} custom-call(s32[4,8]{1,0:T(4,128)S(1)} %bitcast.25, s32[52,1,32]{2,1,0:T(1,128)S(1)} %pad_add_fusion.table_in, f32[1,256]{1,0:T(1,128)S(1)} %reshape_tile.3.bias_ref, bf16[9,384,256]{2,1,0:T(8,128)(2,1)S(1)} %band_weights.1.bands_ref, bf16[49,64,512]{2,1,0:T(8,128)(2,1)S(1)} %get-tuple-element.19.pool_ref, ...), custom_call_target="tpu_custom_call" | custom-call | flops 1 | bytes 1 | tf_op jit(solution)/shard_map/convolve_1/pallas_call | solution.py:391
  48.7 0.0 copy-start.4
  48.7 0.5 collective-permute-start.9
  49.2 0.0 collective-permute-done.10.refs_1_.refs_2_
  49.2 10.1 %collective-permute-start.4 = (bf16[4,64,512]{2,1,0:T(8,128)(2,1)S(1)}, bf16[4,64,512]{2,1,0:T(8,128)(2,1)S(1)}, u32[]{:S(2)}, u32[]{:S(2)}) collective-permute-start(bf16[4,64,512]{2,1,0:T(8,128)(2,1)S(1)} %convolve_5.1.refs_0_), channel_id=1, source_target_pairs={{0,5},{1,4},{2,7},{3,6},{4,1},{5,0},{6,3},{7,2},{8,13},{9,12},{10,... | collective-permute-start | bytes 786440 | tf_op jit(solution)/shard_map/ppermute | solution.py:492
  59.3 2.5 %convolve_0.1.refs_0_ = bf16[4,64,512]{2,1,0:T(8,128)(2,1)S(1)} custom-call(s32[4,8]{1,0:T(4,128)S(1)} %bitcast.26, s32[52,1,32]{2,1,0:T(1,128)S(1)} %pad_add_fusion.table_in, f32[1,256]{1,0:T(1,128)S(1)} %reshape_tile.3.bias_ref, bf16[9,384,256]{2,1,0:T(8,128)(2,1)S(1)} %band_weights.1.bands_ref, bf16[49,64,512]{2,1,0:T(8,128)(2,1)S(1)} %get-tuple-element.19.pool_ref, ...), custom_call_target="tpu_custom_call" | custom-call | flops 1 | bytes 1 | tf_op jit(solution)/shard_map/convolve_0/pallas_call | solution.py:391
  61.8 1.5 %place_0.1.refs_4_ = bf16[16,64,512]{2,1,0:T(8,128)(2,1)} custom-call(s32[16]{0:T(128)S(1)} %bitcast.27, bf16[4,64,512]{2,1,0:T(8,128)(2,1)S(1)} %convolve_0.1.refs_0_, bf16[4,64,512]{2,1,0:T(8,128)(2,1)S(1)} %collective-permute-done.8.refs_1_, bf16[4,64,512]{2,1,0:T(8,128)(2,1)S(1)} %collective-permute-done.10.refs_1_.refs_2_), custom_call_target="tpu_custom_call" | custom-call | flops 1 | bytes 1 | tf_op jit(solution)/shard_map/place_0/pallas_call | solution.py:431
  63.3 0.0 collective-permute-done.7.refs_2_
  63.3 0.0 collective-permute-done.6.refs_1_
  63.3 0.0 collective-permute-done.5.refs_0_
  63.4 0.0 collective-permute-done.9.refs_3_
  63.4 1.5 %place_4.1.refs_1_ = bf16[16,64,512]{2,1,0:T(8,128)(2,1)} custom-call(s32[16]{0:T(128)S(1)} %bitcast.28, bf16[4,64,512]{2,1,0:T(8,128)(2,1)S(1)} %collective-permute-done.5.refs_0_, bf16[4,64,512]{2,1,0:T(8,128)(2,1)S(1)} %collective-permute-done.6.refs_1_, bf16[4,64,512]{2,1,0:T(8,128)(2,1)S(1)} %collective-permute-done.7.refs_2_, ...), custom_call_target="tpu_custom_call", output_to_operand_aliasing={{}: (5, {})} | custom-call | flops 1 | bytes 1 | tf_op jit(solution)/shard_map/place_4/pallas_call | solution.py:431
  64.9 10.4 %collective-permute-done.4.refs_0_ = bf16[4,64,512]{2,1,0:T(8,128)(2,1)S(1)} collective-permute-done((bf16[4,64,512]{2,1,0:T(8,128)(2,1)S(1)}, bf16[4,64,512]{2,1,0:T(8,128)(2,1)S(1)}, u32[]{:S(2)}, u32[]{:S(2)}) %collective-permute-start.4) | collective-permute-done | bytes 262176 | tf_op jit(solution)/shard_map/ppermute | solution.py:492
  75.3 1.4 %place_5.1 = bf16[16,64,512]{2,1,0:T(8,128)(2,1)} custom-call(s32[16]{0:T(128)S(1)} %bitcast.29, bf16[4,64,512]{2,1,0:T(8,128)(2,1)S(1)} %collective-permute-done.4.refs_0_, bf16[16,64,512]{2,1,0:T(8,128)(2,1)} %place_4.1.refs_1_), custom_call_target="tpu_custom_call", output_to_operand_aliasing={{}: (2, {})} | custom-call | flops 1 | bytes 1 | tf_op jit(solution)/shard_map/place_5/pallas_call | solution.py:431
  (9 shorter events, 0.0 us)
Async XLA Ops:
  0.0 16.8 %copy-start.2 = (s32[1,1,32,25]{2,1,3,0:T(1,128)S(1)}, s32[1,1,32,25]{2,1,3,0:T(1,128)}, u32[]{:S(2)}) copy-start(s32[1,1,32,25]{2,1,3,0:T(1,128)} %param.10) | copy-start | bytes 9604
  0.0 11.0 %copy-start.5 = (s32[1,1,8]{2,1,0:T(1,128)S(1)}, s32[1,1,8]{2,1,0:T(1,128)}, u32[]{:S(2)}) copy-start(s32[1,1,8]{2,1,0:T(1,128)} %relays_ref.1) | copy-start | bytes 100
  0.0 16.7 %copy-start.7 = (f32[64]{0:T(128)S(1)}, f32[64]{0:T(128)}, u32[]{:S(2)}) copy-start(f32[64]{0:T(128)} %param.17) | copy-start | bytes 772
  0.0 16.8 %copy-start.6 = (s32[1,1,32,27]{2,1,3,0:T(1,128)S(1)}, s32[1,1,32,27]{2,1,3,0:T(1,128)}, u32[]{:S(2)}) copy-start(s32[1,1,32,27]{2,1,3,0:T(1,128)} %param.11) | copy-start | bytes 10372
  0.0 16.8 %copy-start.1 = (bf16[27,64,64]{2,1,0:T(8,128)(2,1)S(1)}, bf16[27,64,64]{2,1,0:T(8,128)(2,1)}, u32[]{:S(2)}) copy-start(bf16[27,64,64]{2,1,0:T(8,128)(2,1)} %weights_ref.1) | copy-start | bytes 663556
  3.0 14.0 %copy-start = (bf16[1,1,32,8,8,512]{5,4,3,2,1,0:T(8,128)(2,1)S(1)}, bf16[1,1,32,8,8,512]{5,4,3,2,1,0:T(8,128)(2,1)}, u32[]{:S(2)}) copy-start(bf16[1,1,32,8,8,512]{5,4,3,2,1,0:T(8,128)(2,1)} %param.9) | copy-start | bytes 6291460
  3.1 7.9 %collective-permute-start.1 = (bf16[4,16,1280]{2,1,0:T(8,128)(2,1)}, bf16[4,16,1280]{2,1,0:T(8,128)(2,1)S(1)}, u32[]{:S(2)}, u32[]{:S(2)}) collective-permute-start(bf16[4,16,1280]{2,1,0:T(8,128)(2,1)} %get-tuple-element.14), channel_id=1, source_target_pairs={{1,2},{3,4},{5,6},{2,1},{4,3},{6,5},{9,10},{11,12},{13,14},{10,9},... | collective-permute-start | bytes 491528 | tf_op jit(solution)/shard_map/ppermute | solution.py:447
  7.8 3.2 %collective-permute-start = (bf16[4,16,1280]{2,1,0:T(8,128)(2,1)}, bf16[4,16,1280]{2,1,0:T(8,128)(2,1)S(1)}, u32[]{:S(2)}, u32[]{:S(2)}) collective-permute-start(bf16[4,16,1280]{2,1,0:T(8,128)(2,1)} %get-tuple-element.13.refs_0_), channel_id=1, source_target_pairs={{0,1},{1,0},{2,3},{3,2},{4,5},{5,4},{6,7},{7,6},{8,9},{9,8},{10,11... | collective-permute-start | bytes 491528 | tf_op jit(solution)/shard_map/ppermute | solution.py:448
  12.3 7.8 %collective-permute-start.3 = (bf16[4,16,1280]{2,1,0:T(8,128)(2,1)}, bf16[4,16,1280]{2,1,0:T(8,128)(2,1)S(1)}, u32[]{:S(2)}, u32[]{:S(2)}) collective-permute-start(bf16[4,16,1280]{2,1,0:T(8,128)(2,1)} %get-tuple-element.18), channel_id=1, source_target_pairs={{8,16},{16,8},{9,17},{17,9},{10,18},{18,10},{11,19},{19,11},{12,20... | collective-permute-start | bytes 491528 | tf_op jit(solution)/shard_map/ppermute | solution.py:447
  13.0 11.5 %collective-permute-start.2 = (bf16[4,16,1280]{2,1,0:T(8,128)(2,1)}, bf16[4,16,1280]{2,1,0:T(8,128)(2,1)S(1)}, u32[]{:S(2)}, u32[]{:S(2)}) collective-permute-start(bf16[4,16,1280]{2,1,0:T(8,128)(2,1)} %get-tuple-element.17.earlier_ref), channel_id=1, source_target_pairs={{0,8},{8,0},{16,24},{24,16},{1,9},{9,1},{17,25},{25,17},{2,10},{10... | collective-permute-start | bytes 491528 | tf_op jit(solution)/shard_map/ppermute | solution.py:448
  17.1 7.4 %copy-start.3 = (s32[1,1,8,4]{2,3,1,0:T(4,128)S(1)}, s32[1,1,8,4]{2,3,1,0:T(4,128)}, u32[]{:S(2)}) copy-start(s32[1,1,8,4]{2,3,1,0:T(4,128)} %param.14) | copy-start | bytes 388
  27.0 19.2 %collective-permute-start.8 = (bf16[4,64,512]{2,1,0:T(8,128)(2,1)S(1)}, bf16[4,64,512]{2,1,0:T(8,128)(2,1)S(1)}, u32[]{:S(2)}, u32[]{:S(2)}) collective-permute-start(bf16[4,64,512]{2,1,0:T(8,128)(2,1)S(1)} %get-tuple-element.20.refs_0_), channel_id=1, source_target_pairs={{0,6},{1,7},{2,4},{3,5},{4,2},{5,3},{6,0},{7,1},{8,14},{9,15},{10,... | collective-permute-start | bytes 786440 | tf_op jit(solution)/shard_map/ppermute | solution.py:492
  29.5 19.7 %collective-permute-start.10 = (bf16[4,64,512]{2,1,0:T(8,128)(2,1)S(1)}, bf16[4,64,512]{2,1,0:T(8,128)(2,1)S(1)}, u32[]{:S(2)}, u32[]{:S(2)}) collective-permute-start(bf16[4,64,512]{2,1,0:T(8,128)(2,1)S(1)} %convolve_7.1.refs_0_), channel_id=1, source_target_pairs={{0,7},{1,6},{2,5},{3,4},{4,3},{5,2},{6,1},{7,0},{8,15},{9,14},{10,... | collective-permute-start | bytes 786440 | tf_op jit(solution)/shard_map/ppermute | solution.py:492
  44.0 19.3 %collective-permute-start.6 = (bf16[4,64,512]{2,1,0:T(8,128)(2,1)S(1)}, bf16[4,64,512]{2,1,0:T(8,128)(2,1)S(1)}, u32[]{:S(2)}, u32[]{:S(2)}) collective-permute-start(bf16[4,64,512]{2,1,0:T(8,128)(2,1)S(1)} %convolve_2.1.refs_0_), channel_id=1, source_target_pairs={{0,2},{1,3},{2,0},{3,1},{4,6},{5,7},{6,4},{7,5},{8,10},{9,11},{10,... | collective-permute-start | bytes 786440 | tf_op jit(solution)/shard_map/ppermute | solution.py:492
  44.1 19.3 %collective-permute-start.5 = (bf16[4,64,512]{2,1,0:T(8,128)(2,1)S(1)}, bf16[4,64,512]{2,1,0:T(8,128)(2,1)S(1)}, u32[]{:S(2)}, u32[]{:S(2)}) collective-permute-start(bf16[4,64,512]{2,1,0:T(8,128)(2,1)S(1)} %convolve_4.1.refs_0_), channel_id=1, source_target_pairs={{0,4},{1,5},{2,6},{3,7},{4,0},{5,1},{6,2},{7,3},{8,12},{9,13},{10,... | collective-permute-start | bytes 786440 | tf_op jit(solution)/shard_map/ppermute | solution.py:492
  46.2 17.2 %collective-permute-start.7 = (bf16[4,64,512]{2,1,0:T(8,128)(2,1)S(1)}, bf16[4,64,512]{2,1,0:T(8,128)(2,1)S(1)}, u32[]{:S(2)}, u32[]{:S(2)}) collective-permute-start(bf16[4,64,512]{2,1,0:T(8,128)(2,1)S(1)} %convolve_3.1.refs_0_), channel_id=1, source_target_pairs={{0,3},{1,2},{2,1},{3,0},{4,7},{5,6},{6,5},{7,4},{8,11},{9,10},{10,... | collective-permute-start | bytes 786440 | tf_op jit(solution)/shard_map/ppermute | solution.py:492
  48.7 13.2 %copy-start.4 = (s32[1,1,16]{2,1,0:T(1,128)S(1)}, s32[1,1,16]{2,1,0:T(1,128)}, u32[]{:S(2)}) copy-start(s32[1,1,16]{2,1,0:T(1,128)} %param.15) | copy-start | bytes 196
  48.7 14.7 %collective-permute-start.9 = (bf16[4,64,512]{2,1,0:T(8,128)(2,1)S(1)}, bf16[4,64,512]{2,1,0:T(8,128)(2,1)S(1)}, u32[]{:S(2)}, u32[]{:S(2)}) collective-permute-start(bf16[4,64,512]{2,1,0:T(8,128)(2,1)S(1)} %convolve_1.1.refs_0_), channel_id=1, source_target_pairs={{0,1},{1,0},{2,3},{3,2},{4,5},{5,4},{6,7},{7,6},{8,9},{9,8},{10,11... | collective-permute-start | bytes 786440 | tf_op jit(solution)/shard_map/ppermute | solution.py:492
  49.2 26.1 %collective-permute-start.4 = (bf16[4,64,512]{2,1,0:T(8,128)(2,1)S(1)}, bf16[4,64,512]{2,1,0:T(8,128)(2,1)S(1)}, u32[]{:S(2)}, u32[]{:S(2)}) collective-permute-start(bf16[4,64,512]{2,1,0:T(8,128)(2,1)S(1)} %convolve_5.1.refs_0_), channel_id=1, source_target_pairs={{0,5},{1,4},{2,7},{3,6},{4,1},{5,0},{6,3},{7,2},{8,13},{9,12},{10,... | collective-permute-start | bytes 786440 | tf_op jit(solution)/shard_map/ppermute | solution.py:492

commit v6 on v5

--- a/solution.py
+++ b/solution.py
@@ -483,7 +483,7 @@
     arrived, shells, last = {}, (x_partner, x_other), ()
     for i, m in enumerate(order):
         first = i - (len(order) - 2)
-        after = last + ((arrived[order[first]],) if 0 <= first < i else ())
+        after = last + ((arrived[order[first]],) if first == 0 < i else ())
         jobs = [(m, item) for item in range(send_slots.shape[3])]
         made = convolved(jobs, tables, bias, bands, pool, after, shells, slots + faces if shells else None)
         last = (made[0],)

time: 77.1 us -> 77.1 us (level)
  no operation moved by 1% of the time
where the time goes in v6:
time: 77.1 us; the launch traced here: 76.9 us
  Pallas kernels  34.5 us (45%)
  starting transfers between devices  26.5 us (34%)
  waiting for transfers between devices  15.3 us (20%)
    pallas_call x8, Pallas kernels, convolved(): pl.pallas_call(functools.partial(conv_kernel, jobs=jobs, start=start, wai...  19.9 us
    ppermute x7, starting transfers between devices, on_device(): lax.ppermute(made[0], 'gy', [(d, d ^ m) for d in range(peers)])  17.4 us
    ppermute x7, waiting for transfers between devices, on_device(): lax.ppermute(made[0], 'gy', [(d, d ^ m) for d in range(peers)])  10.3 us
    pallas_call x2, Pallas kernels, masked_outgoing(): pl.pallas_call(functools.partial(outgoing_kernel, axis=axis), out_shape=(...  5.65 us
    ppermute x2, starting transfers between devices, exchanged(): lax.ppermute(for_other, axis, others + [(j, i) for i, j in others])  5.4 us
    ppermute x2, waiting for transfers between devices, exchanged(): lax.ppermute(for_partner, axis, [(i, i ^ 1) for i in range(count)])  4.53 us
    pallas_call x3, Pallas kernels, placed(): pl.pallas_call(functools.partial(place_kernel, distances=distances), out_...  4.36 us
    ppermute x2, starting transfers between devices, exchanged(): lax.ppermute(for_partner, axis, [(i, i ^ 1) for i in range(count)])  3.79 us
  transfers between devices with their start and end apart: 11, of which 3 were waited for; matrix products, arithmetic and copies ran while one was open for 0% of the time, Pallas kernels for 34%

profile of v6, /device:TPU:1, one launch (start us, length us, event | category | flops | bytes accessed | tf_op | source)
XLA Modules:
  0.0 76.9 jit_solution(668792458051499624)
XLA Ops:
  0.0 0.0 copy-start.6
  0.0 3.0 %mask_outgoing_gy.1 = (bf16[4,16,1280]{2,1,0:T(8,128)(2,1)}, bf16[4,16,1280]{2,1,0:T(8,128)(2,1)}) custom-call(s32[1,1,8]{2,1,0:T(1,128)} %lists_ref.2, s32[25,1,32]{2,1,0:T(1,128)} %bitcast.15, bf16[32,64,512]{2,1,0:T(8,128)(2,1)} %bitcast.12), custom_call_target="tpu_custom_call" | custom-call | flops 2000000 | bytes 1048576 | tf_op jit(solution)/shard_map/mask_outgoing_gy/pallas_call | solution.py:170
  3.0 0.0 copy-start
  3.1 4.7 %collective-permute-start.1 = (bf16[4,16,1280]{2,1,0:T(8,128)(2,1)}, bf16[4,16,1280]{2,1,0:T(8,128)(2,1)S(1)}, u32[]{:S(2)}, u32[]{:S(2)}) collective-permute-start(bf16[4,16,1280]{2,1,0:T(8,128)(2,1)} %get-tuple-element.14), channel_id=1, source_target_pairs={{1,2},{3,4},{5,6},{2,1},{4,3},{6,5},{9,10},{11,12},{13,14},{10,9},... | collective-permute-start | bytes 491528 | tf_op jit(solution)/shard_map/ppermute | solution.py:447
  7.8 0.1 collective-permute-start
  7.9 2.6 %mask_outgoing_gx.1 = (bf16[4,16,1280]{2,1,0:T(8,128)(2,1)}, bf16[4,16,1280]{2,1,0:T(8,128)(2,1)}) custom-call(s32[1,1,8]{2,1,0:T(1,128)} %relays_ref.1, s32[25,1,32]{2,1,0:T(1,128)} %bitcast.16, bf16[32,64,512]{2,1,0:T(8,128)(2,1)} %bitcast.13, bf16[4,16,1280]{2,1,0:T(8,128)(2,1)} %get-tuple-element.13.refs_0_), custom_call_target="tpu_custom_call" | custom-call | flops 2000000 | bytes 1048576 | tf_op jit(solution)/shard_map/mask_outgoing_gx/pallas_call | solution.py:170
  10.5 0.5 collective-permute-done.1.other_ref
  11.0 0.0 collective-permute-done.partner_ref
  11.0 1.4 %gather_relays.1 = (bf16[4,16,1280]{2,1,0:T(8,128)(2,1)}, bf16[4,16,1280]{2,1,0:T(8,128)(2,1)}) custom-call(s32[1,1,8]{2,1,0:T(1,128)S(1)} %copy-done.5, bf16[4,16,1280]{2,1,0:T(8,128)(2,1)S(1)} %collective-permute-done.partner_ref, bf16[4,16,1280]{2,1,0:T(8,128)(2,1)S(1)} %collective-permute-done.1.other_ref, ...), custom_call_target="tpu_custom_call", output_to_operand_aliasing={{0}: (3, {}), {1}: (4, {})} | custom-call | bytes 655360 | tf_op jit(solution)/shard_map/gather_relays/pallas_call | solution.py:273
  12.4 0.7 collective-permute-start.3
  13.0 3.7 %collective-permute-start.2 = (bf16[4,16,1280]{2,1,0:T(8,128)(2,1)}, bf16[4,16,1280]{2,1,0:T(8,128)(2,1)S(1)}, u32[]{:S(2)}, u32[]{:S(2)}) collective-permute-start(bf16[4,16,1280]{2,1,0:T(8,128)(2,1)} %get-tuple-element.17.earlier_ref), channel_id=1, source_target_pairs={{0,8},{8,0},{16,24},{24,16},{1,9},{9,1},{17,25},{25,17},{2,10},{10... | collective-permute-start | bytes 491528 | tf_op jit(solution)/shard_map/ppermute | solution.py:448
  16.8 0.1 reshape_tile.3.bias_ref
  16.9 0.0 copy-done.2
  16.9 0.0 copy-done.1
  16.9 0.2 band_weights.1.bands_ref
  17.1 0.0 copy-done
  17.1 0.0 copy-start.3
  17.2 3.0 %mask_held.1.pool_ref = bf16[49,64,512]{2,1,0:T(8,128)(2,1)S(1)} custom-call(s32[25,1,32]{2,1,0:T(1,128)S(1)} %bitcast.18, bf16[32,64,512]{2,1,0:T(8,128)(2,1)S(1)} %bitcast.14, bf16[4,16,1280]{2,1,0:T(8,128)(2,1)S(1)} %collective-permute-done.partner_ref, bf16[4,16,1280]{2,1,0:T(8,128)(2,1)S(1)} %collective-permute-done.1.other_ref, ...), custom_call_target="tpu_custom_call" | custom-call | flops 8000000 | bytes 6291456 | tf_op jit(solution)/shard_map/mask_held/pallas_call | solution.py:213
  20.1 0.0 collective-permute-done.3.refs_1_
  20.1 4.5 %collective-permute-done.2.refs_0_ = bf16[4,16,1280]{2,1,0:T(8,128)(2,1)S(1)} collective-permute-done((bf16[4,16,1280]{2,1,0:T(8,128)(2,1)}, bf16[4,16,1280]{2,1,0:T(8,128)(2,1)S(1)}, u32[]{:S(2)}, u32[]{:S(2)}) %collective-permute-start.2) | collective-permute-done | bytes 163872 | tf_op jit(solution)/shard_map/ppermute | solution.py:448
  24.7 0.0 copy-done.3
  24.7 2.5 %convolve_6.1 = (bf16[4,64,512]{2,1,0:T(8,128)(2,1)S(1)}, bf16[49,64,512]{2,1,0:T(8,128)(2,1)S(1)}) custom-call(s32[4,8]{1,0:T(4,128)S(1)} %bitcast.19, s32[52,1,32]{2,1,0:T(1,128)S(1)} %pad_add_fusion.table_in, f32[1,256]{1,0:T(1,128)S(1)} %reshape_tile.3.bias_ref, bf16[9,384,256]{2,1,0:T(8,128)(2,1)S(1)} %band_weights.1.bands_ref, ...), custom_call_target="tpu_custom_call", output_to_operand_aliasing={{1}: (4, {})} | custom-call | flops 1 | bytes 1 | tf_op jit(solution)/shard_map/convolve_6/pallas_call | solution.py:391
  27.2 0.1 collective-permute-start.8
  27.2 2.5 %convolve_7.1.refs_0_ = bf16[4,64,512]{2,1,0:T(8,128)(2,1)S(1)} custom-call(s32[4,8]{1,0:T(4,128)S(1)} %bitcast.20, s32[52,1,32]{2,1,0:T(1,128)S(1)} %pad_add_fusion.table_in, f32[1,256]{1,0:T(1,128)S(1)} %reshape_tile.3.bias_ref, bf16[9,384,256]{2,1,0:T(8,128)(2,1)S(1)} %band_weights.1.bands_ref, bf16[49,64,512]{2,1,0:T(8,128)(2,1)S(1)} %get-tuple-element.19.pool_ref, ...), custom_call_target="tpu_custom_call" | custom-call | flops 1 | bytes 1 | tf_op jit(solution)/shard_map/convolve_7/pallas_call | solution.py:391
  29.7 4.3 %collective-permute-start.10 = (bf16[4,64,512]{2,1,0:T(8,128)(2,1)S(1)}, bf16[4,64,512]{2,1,0:T(8,128)(2,1)S(1)}, u32[]{:S(2)}, u32[]{:S(2)}) collective-permute-start(bf16[4,64,512]{2,1,0:T(8,128)(2,1)S(1)} %convolve_7.1.refs_0_), channel_id=1, source_target_pairs={{0,7},{1,6},{2,5},{3,4},{4,3},{5,2},{6,1},{7,0},{8,15},{9,14},{10,... | collective-permute-start | bytes 786440 | tf_op jit(solution)/shard_map/ppermute | solution.py:492
  34.1 2.5 %convolve_4.1.refs_0_ = bf16[4,64,512]{2,1,0:T(8,128)(2,1)S(1)} custom-call(s32[4,8]{1,0:T(4,128)S(1)} %bitcast.21, s32[52,1,32]{2,1,0:T(1,128)S(1)} %pad_add_fusion.table_in, f32[1,256]{1,0:T(1,128)S(1)} %reshape_tile.3.bias_ref, bf16[9,384,256]{2,1,0:T(8,128)(2,1)S(1)} %band_weights.1.bands_ref, bf16[49,64,512]{2,1,0:T(8,128)(2,1)S(1)} %get-tuple-element.19.pool_ref, ...), custom_call_target="tpu_custom_call" | custom-call | flops 1 | bytes 1 | tf_op jit(solution)/shard_map/convolve_4/pallas_call | solution.py:391
  36.6 2.5 %convolve_5.1.refs_0_ = bf16[4,64,512]{2,1,0:T(8,128)(2,1)S(1)} custom-call(s32[4,8]{1,0:T(4,128)S(1)} %bitcast.22, s32[52,1,32]{2,1,0:T(1,128)S(1)} %pad_add_fusion.table_in, f32[1,256]{1,0:T(1,128)S(1)} %reshape_tile.3.bias_ref, bf16[9,384,256]{2,1,0:T(8,128)(2,1)S(1)} %band_weights.1.bands_ref, bf16[49,64,512]{2,1,0:T(8,128)(2,1)S(1)} %get-tuple-element.19.pool_ref, ...), custom_call_target="tpu_custom_call" | custom-call | flops 1 | bytes 1 | tf_op jit(solution)/shard_map/convolve_5/pallas_call | solution.py:391
  39.1 2.5 %convolve_2.1.refs_0_ = bf16[4,64,512]{2,1,0:T(8,128)(2,1)S(1)} custom-call(s32[4,8]{1,0:T(4,128)S(1)} %bitcast.23, s32[52,1,32]{2,1,0:T(1,128)S(1)} %pad_add_fusion.table_in, f32[1,256]{1,0:T(1,128)S(1)} %reshape_tile.3.bias_ref, bf16[9,384,256]{2,1,0:T(8,128)(2,1)S(1)} %band_weights.1.bands_ref, bf16[49,64,512]{2,1,0:T(8,128)(2,1)S(1)} %get-tuple-element.19.pool_ref, ...), custom_call_target="tpu_custom_call" | custom-call | flops 1 | bytes 1 | tf_op jit(solution)/shard_map/convolve_2/pallas_call | solution.py:391
  41.6 2.5 %convolve_3.1.refs_0_ = bf16[4,64,512]{2,1,0:T(8,128)(2,1)S(1)} custom-call(s32[4,8]{1,0:T(4,128)S(1)} %bitcast.24, s32[52,1,32]{2,1,0:T(1,128)S(1)} %pad_add_fusion.table_in, f32[1,256]{1,0:T(1,128)S(1)} %reshape_tile.3.bias_ref, bf16[9,384,256]{2,1,0:T(8,128)(2,1)S(1)} %band_weights.1.bands_ref, bf16[49,64,512]{2,1,0:T(8,128)(2,1)S(1)} %get-tuple-element.19.pool_ref, ...), custom_call_target="tpu_custom_call" | custom-call | flops 1 | bytes 1 | tf_op jit(solution)/shard_map/convolve_3/pallas_call | solution.py:391
  44.1 0.1 collective-permute-start.6
  44.1 2.0 %collective-permute-start.5 = (bf16[4,64,512]{2,1,0:T(8,128)(2,1)S(1)}, bf16[4,64,512]{2,1,0:T(8,128)(2,1)S(1)}, u32[]{:S(2)}, u32[]{:S(2)}) collective-permute-start(bf16[4,64,512]{2,1,0:T(8,128)(2,1)S(1)} %convolve_4.1.refs_0_), channel_id=1, source_target_pairs={{0,4},{1,5},{2,6},{3,7},{4,0},{5,1},{6,2},{7,3},{8,12},{9,13},{10,... | collective-permute-start | bytes 786440 | tf_op jit(solution)/shard_map/ppermute | solution.py:492
  46.1 0.0 collective-permute-start.7
  46.1 0.0 collective-permute-done.8.refs_1_
  46.1 2.5 %convolve_1.1.refs_0_ = bf16[4,64,512]{2,1,0:T(8,128)(2,1)S(1)} custom-call(s32[4,8]{1,0:T(4,128)S(1)} %bitcast.25, s32[52,1,32]{2,1,0:T(1,128)S(1)} %pad_add_fusion.table_in, f32[1,256]{1,0:T(1,128)S(1)} %reshape_tile.3.bias_ref, bf16[9,384,256]{2,1,0:T(8,128)(2,1)S(1)} %band_weights.1.bands_ref, bf16[49,64,512]{2,1,0:T(8,128)(2,1)S(1)} %get-tuple-element.19.pool_ref, ...), custom_call_target="tpu_custom_call" | custom-call | flops 1 | bytes 1 | tf_op jit(solution)/shard_map/convolve_1/pallas_call | solution.py:391
  48.6 0.0 copy-start.4
  48.6 0.6 collective-permute-start.9
  49.2 0.0 collective-permute-done.10.refs_2_
  49.2 10.3 %collective-permute-start.4 = (bf16[4,64,512]{2,1,0:T(8,128)(2,1)S(1)}, bf16[4,64,512]{2,1,0:T(8,128)(2,1)S(1)}, u32[]{:S(2)}, u32[]{:S(2)}) collective-permute-start(bf16[4,64,512]{2,1,0:T(8,128)(2,1)S(1)} %convolve_5.1.refs_0_), channel_id=1, source_target_pairs={{0,5},{1,4},{2,7},{3,6},{4,1},{5,0},{6,3},{7,2},{8,13},{9,12},{10,... | collective-permute-start | bytes 786440 | tf_op jit(solution)/shard_map/ppermute | solution.py:492
  59.5 2.5 %convolve_0.1.refs_0_ = bf16[4,64,512]{2,1,0:T(8,128)(2,1)S(1)} custom-call(s32[4,8]{1,0:T(4,128)S(1)} %bitcast.26, s32[52,1,32]{2,1,0:T(1,128)S(1)} %pad_add_fusion.table_in, f32[1,256]{1,0:T(1,128)S(1)} %reshape_tile.3.bias_ref, bf16[9,384,256]{2,1,0:T(8,128)(2,1)S(1)} %band_weights.1.bands_ref, bf16[49,64,512]{2,1,0:T(8,128)(2,1)S(1)} %get-tuple-element.19.pool_ref, ...), custom_call_target="tpu_custom_call" | custom-call | flops 1 | bytes 1 | tf_op jit(solution)/shard_map/convolve_0/pallas_call | solution.py:391
  62.0 0.0 copy-done.4
  62.0 1.5 %place_0.1.refs_4_ = bf16[16,64,512]{2,1,0:T(8,128)(2,1)} custom-call(s32[16]{0:T(128)S(1)} %bitcast.27, bf16[4,64,512]{2,1,0:T(8,128)(2,1)S(1)} %convolve_0.1.refs_0_, bf16[4,64,512]{2,1,0:T(8,128)(2,1)S(1)} %collective-permute-done.8.refs_1_, bf16[4,64,512]{2,1,0:T(8,128)(2,1)S(1)} %collective-permute-done.10.refs_2_), custom_call_target="tpu_custom_call" | custom-call | flops 1 | bytes 1 | tf_op jit(solution)/shard_map/place_0/pallas_call | solution.py:431
  63.5 0.0 collective-permute-done.7.refs_2_
  63.5 0.0 collective-permute-done.6.refs_1_
  63.5 0.0 collective-permute-done.5.refs_0_
  63.6 0.0 collective-permute-done.9.refs_3_
  63.6 1.5 %place_4.1.refs_1_ = bf16[16,64,512]{2,1,0:T(8,128)(2,1)} custom-call(s32[16]{0:T(128)S(1)} %bitcast.28, bf16[4,64,512]{2,1,0:T(8,128)(2,1)S(1)} %collective-permute-done.5.refs_0_, bf16[4,64,512]{2,1,0:T(8,128)(2,1)S(1)} %collective-permute-done.6.refs_1_, bf16[4,64,512]{2,1,0:T(8,128)(2,1)S(1)} %collective-permute-done.7.refs_2_, ...), custom_call_target="tpu_custom_call", output_to_operand_aliasing={{}: (5, {})} | custom-call | flops 1 | bytes 1 | tf_op jit(solution)/shard_map/place_4/pallas_call | solution.py:431
  65.1 10.3 %collective-permute-done.4.refs_0_ = bf16[4,64,512]{2,1,0:T(8,128)(2,1)S(1)} collective-permute-done((bf16[4,64,512]{2,1,0:T(8,128)(2,1)S(1)}, bf16[4,64,512]{2,1,0:T(8,128)(2,1)S(1)}, u32[]{:S(2)}, u32[]{:S(2)}) %collective-permute-start.4) | collective-permute-done | bytes 262176 | tf_op jit(solution)/shard_map/ppermute | solution.py:492
  75.4 1.3 %place_5.1 = bf16[16,64,512]{2,1,0:T(8,128)(2,1)} custom-call(s32[16]{0:T(128)S(1)} %bitcast.29, bf16[4,64,512]{2,1,0:T(8,128)(2,1)S(1)} %collective-permute-done.4.refs_0_, bf16[16,64,512]{2,1,0:T(8,128)(2,1)} %place_4.1.refs_1_), custom_call_target="tpu_custom_call", output_to_operand_aliasing={{}: (2, {})} | custom-call | flops 1 | bytes 1 | tf_op jit(solution)/shard_map/place_5/pallas_call | solution.py:431
  (9 shorter events, 0.0 us)
Async XLA Ops:
  0.0 16.9 %copy-start.2 = (s32[1,1,32,25]{2,1,3,0:T(1,128)S(1)}, s32[1,1,32,25]{2,1,3,0:T(1,128)}, u32[]{:S(2)}) copy-start(s32[1,1,32,25]{2,1,3,0:T(1,128)} %param.10) | copy-start | bytes 9604
  0.0 11.0 %copy-start.5 = (s32[1,1,8]{2,1,0:T(1,128)S(1)}, s32[1,1,8]{2,1,0:T(1,128)}, u32[]{:S(2)}) copy-start(s32[1,1,8]{2,1,0:T(1,128)} %relays_ref.1) | copy-start | bytes 100
  0.0 16.8 %copy-start.7 = (f32[64]{0:T(128)S(1)}, f32[64]{0:T(128)}, u32[]{:S(2)}) copy-start(f32[64]{0:T(128)} %param.17) | copy-start | bytes 772
  0.0 16.8 %copy-start.6 = (s32[1,1,32,27]{2,1,3,0:T(1,128)S(1)}, s32[1,1,32,27]{2,1,3,0:T(1,128)}, u32[]{:S(2)}) copy-start(s32[1,1,32,27]{2,1,3,0:T(1,128)} %param.11) | copy-start | bytes 10372
  0.0 16.9 %copy-start.1 = (bf16[27,64,64]{2,1,0:T(8,128)(2,1)S(1)}, bf16[27,64,64]{2,1,0:T(8,128)(2,1)}, u32[]{:S(2)}) copy-start(bf16[27,64,64]{2,1,0:T(8,128)(2,1)} %weights_ref.1) | copy-start | bytes 663556
  3.0 14.1 %copy-start = (bf16[1,1,32,8,8,512]{5,4,3,2,1,0:T(8,128)(2,1)S(1)}, bf16[1,1,32,8,8,512]{5,4,3,2,1,0:T(8,128)(2,1)}, u32[]{:S(2)}) copy-start(bf16[1,1,32,8,8,512]{5,4,3,2,1,0:T(8,128)(2,1)} %param.9) | copy-start | bytes 6291460
  3.1 7.9 %collective-permute-start.1 = (bf16[4,16,1280]{2,1,0:T(8,128)(2,1)}, bf16[4,16,1280]{2,1,0:T(8,128)(2,1)S(1)}, u32[]{:S(2)}, u32[]{:S(2)}) collective-permute-start(bf16[4,16,1280]{2,1,0:T(8,128)(2,1)} %get-tuple-element.14), channel_id=1, source_target_pairs={{1,2},{3,4},{5,6},{2,1},{4,3},{6,5},{9,10},{11,12},{13,14},{10,9},... | collective-permute-start | bytes 491528 | tf_op jit(solution)/shard_map/ppermute | solution.py:447
  7.8 3.2 %collective-permute-start = (bf16[4,16,1280]{2,1,0:T(8,128)(2,1)}, bf16[4,16,1280]{2,1,0:T(8,128)(2,1)S(1)}, u32[]{:S(2)}, u32[]{:S(2)}) collective-permute-start(bf16[4,16,1280]{2,1,0:T(8,128)(2,1)} %get-tuple-element.13.refs_0_), channel_id=1, source_target_pairs={{0,1},{1,0},{2,3},{3,2},{4,5},{5,4},{6,7},{7,6},{8,9},{9,8},{10,11... | collective-permute-start | bytes 491528 | tf_op jit(solution)/shard_map/ppermute | solution.py:448
  12.4 7.8 %collective-permute-start.3 = (bf16[4,16,1280]{2,1,0:T(8,128)(2,1)}, bf16[4,16,1280]{2,1,0:T(8,128)(2,1)S(1)}, u32[]{:S(2)}, u32[]{:S(2)}) collective-permute-start(bf16[4,16,1280]{2,1,0:T(8,128)(2,1)} %get-tuple-element.18), channel_id=1, source_target_pairs={{8,16},{16,8},{9,17},{17,9},{10,18},{18,10},{11,19},{19,11},{12,20... | collective-permute-start | bytes 491528 | tf_op jit(solution)/shard_map/ppermute | solution.py:447
  13.0 11.6 %collective-permute-start.2 = (bf16[4,16,1280]{2,1,0:T(8,128)(2,1)}, bf16[4,16,1280]{2,1,0:T(8,128)(2,1)S(1)}, u32[]{:S(2)}, u32[]{:S(2)}) collective-permute-start(bf16[4,16,1280]{2,1,0:T(8,128)(2,1)} %get-tuple-element.17.earlier_ref), channel_id=1, source_target_pairs={{0,8},{8,0},{16,24},{24,16},{1,9},{9,1},{17,25},{25,17},{2,10},{10... | collective-permute-start | bytes 491528 | tf_op jit(solution)/shard_map/ppermute | solution.py:448
  17.1 7.5 %copy-start.3 = (s32[1,1,8,4]{2,3,1,0:T(4,128)S(1)}, s32[1,1,8,4]{2,3,1,0:T(4,128)}, u32[]{:S(2)}) copy-start(s32[1,1,8,4]{2,3,1,0:T(4,128)} %param.14) | copy-start | bytes 388
  27.2 18.9 %collective-permute-start.8 = (bf16[4,64,512]{2,1,0:T(8,128)(2,1)S(1)}, bf16[4,64,512]{2,1,0:T(8,128)(2,1)S(1)}, u32[]{:S(2)}, u32[]{:S(2)}) collective-permute-start(bf16[4,64,512]{2,1,0:T(8,128)(2,1)S(1)} %get-tuple-element.20.refs_0_), channel_id=1, source_target_pairs={{0,6},{1,7},{2,4},{3,5},{4,2},{5,3},{6,0},{7,1},{8,14},{9,15},{10,... | collective-permute-start | bytes 786440 | tf_op jit(solution)/shard_map/ppermute | solution.py:492
  29.7 19.5 %collective-permute-start.10 = (bf16[4,64,512]{2,1,0:T(8,128)(2,1)S(1)}, bf16[4,64,512]{2,1,0:T(8,128)(2,1)S(1)}, u32[]{:S(2)}, u32[]{:S(2)}) collective-permute-start(bf16[4,64,512]{2,1,0:T(8,128)(2,1)S(1)} %convolve_7.1.refs_0_), channel_id=1, source_target_pairs={{0,7},{1,6},{2,5},{3,4},{4,3},{5,2},{6,1},{7,0},{8,15},{9,14},{10,... | collective-permute-start | bytes 786440 | tf_op jit(solution)/shard_map/ppermute | solution.py:492
  44.1 19.5 %collective-permute-start.6 = (bf16[4,64,512]{2,1,0:T(8,128)(2,1)S(1)}, bf16[4,64,512]{2,1,0:T(8,128)(2,1)S(1)}, u32[]{:S(2)}, u32[]{:S(2)}) collective-permute-start(bf16[4,64,512]{2,1,0:T(8,128)(2,1)S(1)} %convolve_2.1.refs_0_), channel_id=1, source_target_pairs={{0,2},{1,3},{2,0},{3,1},{4,6},{5,7},{6,4},{7,5},{8,10},{9,11},{10,... | collective-permute-start | bytes 786440 | tf_op jit(solution)/shard_map/ppermute | solution.py:492
  44.1 19.4 %collective-permute-start.5 = (bf16[4,64,512]{2,1,0:T(8,128)(2,1)S(1)}, bf16[4,64,512]{2,1,0:T(8,128)(2,1)S(1)}, u32[]{:S(2)}, u32[]{:S(2)}) collective-permute-start(bf16[4,64,512]{2,1,0:T(8,128)(2,1)S(1)} %convolve_4.1.refs_0_), channel_id=1, source_target_pairs={{0,4},{1,5},{2,6},{3,7},{4,0},{5,1},{6,2},{7,3},{8,12},{9,13},{10,... | collective-permute-start | bytes 786440 | tf_op jit(solution)/shard_map/ppermute | solution.py:492
  46.1 17.4 %collective-permute-start.7 = (bf16[4,64,512]{2,1,0:T(8,128)(2,1)S(1)}, bf16[4,64,512]{2,1,0:T(8,128)(2,1)S(1)}, u32[]{:S(2)}, u32[]{:S(2)}) collective-permute-start(bf16[4,64,512]{2,1,0:T(8,128)(2,1)S(1)} %convolve_3.1.refs_0_), channel_id=1, source_target_pairs={{0,3},{1,2},{2,1},{3,0},{4,7},{5,6},{6,5},{7,4},{8,11},{9,10},{10,... | collective-permute-start | bytes 786440 | tf_op jit(solution)/shard_map/ppermute | solution.py:492
  48.6 13.4 %copy-start.4 = (s32[1,1,16]{2,1,0:T(1,128)S(1)}, s32[1,1,16]{2,1,0:T(1,128)}, u32[]{:S(2)}) copy-start(s32[1,1,16]{2,1,0:T(1,128)} %param.15) | copy-start | bytes 196
  48.6 14.9 %collective-permute-start.9 = (bf16[4,64,512]{2,1,0:T(8,128)(2,1)S(1)}, bf16[4,64,512]{2,1,0:T(8,128)(2,1)S(1)}, u32[]{:S(2)}, u32[]{:S(2)}) collective-permute-start(bf16[4,64,512]{2,1,0:T(8,128)(2,1)S(1)} %convolve_1.1.refs_0_), channel_id=1, source_target_pairs={{0,1},{1,0},{2,3},{3,2},{4,5},{5,4},{6,7},{7,6},{8,9},{9,8},{10,11... | collective-permute-start | bytes 786440 | tf_op jit(solution)/shard_map/ppermute | solution.py:492
  49.2 26.2 %collective-permute-start.4 = (bf16[4,64,512]{2,1,0:T(8,128)(2,1)S(1)}, bf16[4,64,512]{2,1,0:T(8,128)(2,1)S(1)}, u32[]{:S(2)}, u32[]{:S(2)}) collective-permute-start(bf16[4,64,512]{2,1,0:T(8,128)(2,1)S(1)} %convolve_5.1.refs_0_), channel_id=1, source_target_pairs={{0,5},{1,4},{2,7},{3,6},{4,1},{5,0},{6,3},{7,2},{8,13},{9,12},{10,... | collective-permute-start | bytes 786440 | tf_op jit(solution)/shard_map/ppermute | solution.py:492
